TPU v7x, 32 devices: a whole 2x2x4 slice. The times are simulated.
32 devices in a mesh: rep: 8 (over y, x, core), shard: 4 (over z).
Axes of the slice: x: 2, y: 2, z: 4, core: 2. Of those that a mesh axis runs over, the one named last changes fastest.
Arguments:
- hidden_in: bfloat16 [16384, 1024], P(('rep', 'shard')), may hold values from -6 to 6
- segment_ids: int32 [16384], P(('rep', 'shard')), may hold values from 0 to 63, never falling along the last dimension, each value on 1 to 1024 neighbouring positions
- norm_gains: float32 [2, 1024], P(None, 'shard'), may hold values from 0.1 to 1.9
- w_mix_in: bfloat16 [1024, 6144], P('shard'), may hold values from -0.1875 to 0.1875
- w_decay: bfloat16 [1024, 16], P('shard'), may hold values from -0.1875 to 0.1875
- decay_params: float32 [2, 8], P(None, 'shard'), may hold values from -4 to 1
- conv_weight: float32 [4, 4096], P(None, 'shard'), may hold values from -3 to 3
- out_gain: float32 [256], P('shard'), may hold values from 0.1 to 1.9
- w_mix_out: bfloat16 [2048, 1024], P('shard'), may hold values from -0.25 to 0.25
- w_gate_up: bfloat16 [1024, 5632], P('shard'), may hold values from -0.1875 to 0.1875
- w_down: bfloat16 [2816, 1024], P('shard'), may hold values from -0.21875 to 0.21875
- cotangent: bfloat16 [16384, 1024], P(('rep', 'shard')), may hold values from -6 to 6
Outputs:
- hidden_out: bfloat16 [16384, 1024], P(('rep', 'shard'))
- grad_in: float32 [16384, 1024], P(('rep', 'shard'))
- grad_norm_gains: float32 [2, 1024], P(None, 'shard')
- grad_mix_in: float32 [1024, 6144], P('shard')
- grad_decay: float32 [1024, 16], P('shard')
- grad_decay_params: float32 [2, 8], P(None, 'shard')
- grad_conv: float32 [4, 4096], P(None, 'shard')
- grad_out_gain: float32 [256], P('shard')
- grad_mix_out: float32 [2048, 1024], P('shard')
- grad_gate_up: float32 [1024, 5632], P('shard')
- grad_down: float32 [2816, 1024], P('shard')
Inputs may be any that keep to these rules, and one draw needn't show every extreme that they name: `segment_ids`: document numbers never fall along the tokens; every document holds 1 to 1024 tokens and one holds exactly 1024; a document may run across the end of a sequence, where the state starts afresh.
All inputs are finite; a program needn't handle non-finite values.
Results may differ from a plain program's by a relative error of at most 0.023.
Values may be sent and summed in bfloat16 or wider, within the bound.
No kernel may reach another device: no remote copies, remote signals or barrier semaphores. Data moves between devices by JAX's collectives and lax.ppermute only.
A program may use at most 384 MiB of HBM per device.

v0:
```python
import jax
import jax.numpy as jnp
from jax import lax
from jax.sharding import PartitionSpec as P

HEADS = 8
DK = 128
DV = 256
FF = 2816
CONV = 4
SPAN = 64
KEYS = 1024
VALS = 2048


HIGHEST = lax.Precision.HIGHEST
epsilon = 1e-06
out_floor = 0.01


def rms_scale(values, gain):
    return values * lax.rsqrt(jnp.mean(values * values, axis=-1, keepdims=True) + epsilon) * gain


def delayed(values, shift):
    widths = [(0, 0)] * values.ndim
    widths[-2] = (shift, 0)
    return jnp.pad(values, widths)[..., : values.shape[-2], :]


def delayed_ids(segments, shift):
    widths = [(0, 0)] * segments.ndim
    widths[-1] = (shift, 0)
    return jnp.pad(segments, widths, constant_values=-1)[..., : segments.shape[-1]]


def prepare(projected, decay_logits, segments, decay_params, conv_weight):
    channels = 2 * KEYS + VALS
    mixed = projected[..., :channels]
    gate_raw = projected[..., channels:]
    total = conv_weight[0] * mixed
    for shift in range(1, CONV):
        match = (delayed_ids(segments, shift) == segments).astype(jnp.float32)[..., None]
        total = total + conv_weight[shift] * delayed(mixed, shift) * match
    active = jax.nn.silu(total)
    leading = active.shape[:-1]
    queries = active[..., :KEYS].reshape(leading + (HEADS, DK))
    keys_raw = active[..., KEYS : 2 * KEYS].reshape(leading + (HEADS, DK))
    keys_unit = keys_raw * lax.rsqrt(jnp.sum(keys_raw * keys_raw, axis=-1, keepdims=True) + epsilon)
    values = active[..., 2 * KEYS :].reshape(leading + (HEADS, DV))
    beta = jax.nn.sigmoid(decay_logits[..., HEADS:])
    gamma = -jnp.exp(decay_params[0]) * jax.nn.softplus(decay_logits[..., :HEADS] + decay_params[1])
    return (queries, keys_unit, values, beta, gamma, gate_raw)


def finish(outputs, gate_raw, out_gain):
    normed = (
        outputs
        * lax.rsqrt(jnp.mean(outputs * outputs, axis=-1, keepdims=True) + out_floor)
        * out_gain
    )
    return normed.reshape(gate_raw.shape) * jax.nn.silu(gate_raw)


def swiglu(gate_up):
    return jax.nn.silu(gate_up[..., :FF]) * gate_up[..., FF:]


def span_step(state, block):
    queries, keys_unit, values, beta, gamma, segments, before = block
    cumulative = jnp.cumsum(gamma, axis=0).T
    same = segments[:, None] == segments[None, :]
    order = jnp.arange(SPAN)
    lower = order[:, None] >= order[None, :]
    strict = order[:, None] > order[None, :]
    within = (same & lower)[None]
    reach = (segments == before).astype(jnp.float32)[None, :] * jnp.exp(cumulative)
    gaps = cumulative[:, :, None] - cumulative[:, None, :]
    decays = jnp.where(within, jnp.exp(jnp.where(within, gaps, 0.0)), 0.0)
    key_key = jnp.einsum("ihd,jhd->hij", keys_unit, keys_unit, precision=HIGHEST)
    query_key = jnp.einsum("ihd,jhd->hij", queries, keys_unit, precision=HIGHEST)
    beta_heads = beta.T
    system = (
        jnp.eye(SPAN, dtype=jnp.float32)
        + beta_heads[:, :, None] * jnp.where(strict[None], decays, 0.0) * key_key
    )
    carried_keys = jnp.einsum("hvd,ihd->hiv", state, keys_unit, precision=HIGHEST)
    right = beta_heads[:, :, None] * (values.transpose(1, 0, 2) - reach[:, :, None] * carried_keys)
    fresh = jax.scipy.linalg.solve_triangular(system, right, lower=True, unit_diagonal=True)
    carried_queries = jnp.einsum("hvd,ihd->hiv", state, queries, precision=HIGHEST)
    outputs = reach[:, :, None] * carried_queries + jnp.einsum(
        "hij,hjv->hiv", decays * query_key, fresh, precision=HIGHEST
    )
    final_row = decays[:, -1, :]
    state = reach[:, -1][:, None, None] * state + jnp.einsum(
        "hj,hjv,jhd->hvd", final_row, fresh, keys_unit, precision=HIGHEST
    )
    return (state, outputs.transpose(1, 0, 2))


def block_rule(queries, keys_unit, values, beta, gamma, segments):
    length = queries.shape[0]
    blocks = length // SPAN
    previous = jnp.concatenate([jnp.full((1,), -1, jnp.int32), segments[:-1]])

    def split(array):
        return array.reshape((blocks, SPAN) + array.shape[1:])

    inputs = (
        split(queries),
        split(keys_unit),
        split(values),
        split(beta),
        split(gamma),
        split(segments),
        previous.reshape(blocks, SPAN)[:, 0],
    )
    state = jnp.zeros((HEADS, DV, DK), jnp.float32)
    state, outputs = lax.scan(span_step, state, inputs)
    return outputs.reshape(length, HEADS, DV)


def rounded(values):
    return lax.optimization_barrier(values.astype(jnp.bfloat16)).astype(jnp.float32)


def contract_rows(left, right):
    return lax.dot_general(
        left, right, (((0,), (0,)), ((), ())), preferred_element_type=jnp.float32
    )


def contract_cols(left, right):
    return lax.dot_general(
        left, right, (((1,), (1,)), ((), ())), preferred_element_type=jnp.float32
    )


def row_fold(left, piece):
    return jnp.dot(left, piece, preferred_element_type=jnp.float32)


def pair_fold(left, pieces):
    return (
        jnp.dot(left, pieces[0], preferred_element_type=jnp.float32),
        jnp.dot(left, pieces[1], preferred_element_type=jnp.float32),
    )


def back_rows(right, piece):
    return contract_cols(right, piece)


def back_pair(first, second, pieces):
    return contract_cols(first, pieces[0]) + contract_cols(second, pieces[1])


def body(
    hidden_in,
    segment_ids,
    norm_gains,
    w_mix_in,
    w_decay,
    decay_params,
    conv_weight,
    out_gain,
    w_mix_out,
    w_gate_up,
    w_down,
    cotangent,
):
    gains, rate_params, conv_full, gain_row = (
        lax.all_gather(norm_gains, "shard", axis=1, tiled=True),
        lax.all_gather(decay_params, "shard", axis=1, tiled=True),
        lax.all_gather(conv_weight, "shard", axis=1, tiled=True),
        lax.all_gather(out_gain[None, :], "shard", axis=1, tiled=True),
    )
    out_scale = gain_row[0]
    hidden = hidden_in.astype(jnp.float32)
    normed_one_f, norm_one_pull = jax.vjp(rms_scale, hidden, gains[0])
    normed_one = normed_one_f.astype(jnp.bfloat16)
    projected, decay_logits = pair_fold(
        normed_one,
        (
            lax.all_gather(w_mix_in, "shard", axis=0, tiled=True),
            lax.all_gather(w_decay, "shard", axis=0, tiled=True),
        ),
    )

    def local_prepare(projected_in, logits_in, params_in, conv_in):
        return prepare(projected_in, logits_in, segment_ids, params_in, conv_in)

    prepared, prepare_pull = jax.vjp(local_prepare, projected, decay_logits, rate_params, conv_full)
    queries, keys_unit, values, beta, gamma, gate_raw = prepared

    def local_core(queries_in, keys_in, values_in, beta_in, gamma_in):
        return block_rule(queries_in, keys_in, values_in, beta_in, gamma_in, segment_ids)

    outputs, core_pull = jax.vjp(
        local_core, rounded(queries), rounded(keys_unit), rounded(values), beta, gamma
    )
    finished, finish_pull = jax.vjp(finish, outputs, gate_raw, out_scale)
    mixed_out = finished.astype(jnp.bfloat16)
    branch = row_fold(mixed_out, lax.all_gather(w_mix_out, "shard", axis=0, tiled=True))
    residual = hidden + branch
    normed_two_f, norm_two_pull = jax.vjp(rms_scale, residual, gains[1])
    normed_two = normed_two_f.astype(jnp.bfloat16)
    gate_up = row_fold(normed_two, lax.all_gather(w_gate_up, "shard", axis=0, tiled=True))
    inner_f, inner_pull = jax.vjp(swiglu, gate_up)
    inner = inner_f.astype(jnp.bfloat16)
    down = row_fold(inner, lax.all_gather(w_down, "shard", axis=0, tiled=True))
    result = (residual + down).astype(jnp.bfloat16)
    inner_back = back_rows(cotangent, lax.all_gather(w_down, "shard", axis=0, tiled=True))
    grad_down_local = contract_rows(inner, cotangent)
    (gate_up_grad,) = inner_pull(inner_back)
    gate_up_back = gate_up_grad.astype(jnp.bfloat16)
    grad_gate_up_local = contract_rows(normed_two, gate_up_back)
    ffn_shares = (
        lax.psum_scatter(
            grad_gate_up_local.astype(jnp.bfloat16), "shard", scatter_dimension=0, tiled=True
        ).astype(jnp.float32),
        lax.psum_scatter(
            grad_down_local.astype(jnp.bfloat16), "shard", scatter_dimension=0, tiled=True
        ).astype(jnp.float32),
    )
    normed_two_back = back_rows(
        gate_up_back, lax.all_gather(w_gate_up, "shard", axis=0, tiled=True)
    )
    residual_part, gain_two = norm_two_pull(normed_two_back)
    residual_back = cotangent.astype(jnp.float32) + residual_part
    branch_back = residual_back.astype(jnp.bfloat16)
    grad_mix_out_local = contract_rows(mixed_out, branch_back)
    mixed_back = back_rows(branch_back, lax.all_gather(w_mix_out, "shard", axis=0, tiled=True))
    outputs_back, gate_back, gain_out_grad = finish_pull(mixed_back)
    queries_back, keys_back, values_back, beta_back, gamma_back = core_pull(outputs_back)
    projected_grad, logits_grad, params_grad, conv_grad = prepare_pull(
        (queries_back, keys_back, values_back, beta_back, gamma_back, gate_back)
    )
    projected_back = projected_grad.astype(jnp.bfloat16)
    logits_back = logits_grad.astype(jnp.bfloat16)
    grad_mix_in_local = contract_rows(normed_one, projected_back)
    grad_decay_local = contract_rows(normed_one, logits_back)
    normed_one_back = back_pair(
        projected_back,
        logits_back,
        lax.all_gather((w_mix_in, w_decay), "shard", axis=0, tiled=True),
    )
    hidden_part, gain_one = norm_one_pull(normed_one_back)
    grad_in = residual_back + hidden_part
    mix_shares = (
        lax.psum_scatter(
            grad_mix_in_local.astype(jnp.bfloat16), "shard", scatter_dimension=0, tiled=True
        ).astype(jnp.float32),
        lax.psum_scatter(
            grad_decay_local.astype(jnp.bfloat16), "shard", scatter_dimension=0, tiled=True
        ).astype(jnp.float32),
        lax.psum_scatter(
            grad_mix_out_local.astype(jnp.bfloat16), "shard", scatter_dimension=0, tiled=True
        ).astype(jnp.float32),
        lax.psum_scatter(
            jnp.stack([gain_one, gain_two]).astype(jnp.bfloat16),
            "shard",
            scatter_dimension=1,
            tiled=True,
        ).astype(jnp.float32),
        lax.psum_scatter(
            params_grad.astype(jnp.bfloat16), "shard", scatter_dimension=1, tiled=True
        ).astype(jnp.float32),
        lax.psum_scatter(
            conv_grad.astype(jnp.bfloat16), "shard", scatter_dimension=1, tiled=True
        ).astype(jnp.float32),
        lax.psum_scatter(
            gain_out_grad[None, :].astype(jnp.bfloat16), "shard", scatter_dimension=1, tiled=True
        ).astype(jnp.float32),
    )
    totals = lax.psum(
        (
            ffn_shares[0],
            ffn_shares[1],
            mix_shares[0],
            mix_shares[1],
            mix_shares[2],
            mix_shares[3],
            mix_shares[4],
            mix_shares[5],
            mix_shares[6],
        ),
        "rep",
    )
    return (
        result,
        grad_in,
        totals[5],
        totals[2],
        totals[3],
        totals[6],
        totals[7],
        totals[8][0],
        totals[4],
        totals[0],
        totals[1],
    )


def solution(mesh):
    return jax.shard_map(
        body,
        mesh=mesh,
        in_specs=(
            P(("rep", "shard"), None),
            P(("rep", "shard")),
            P(None, "shard"),
            P("shard", None),
            P("shard", None),
            P(None, "shard"),
            P(None, "shard"),
            P("shard"),
            P("shard", None),
            P("shard", None),
            P("shard", None),
            P(("rep", "shard"), None),
        ),
        out_specs=(
            P(("rep", "shard"), None),
            P(("rep", "shard"), None),
            P(None, "shard"),
            P("shard", None),
            P("shard", None),
            P(None, "shard"),
            P(None, "shard"),
            P("shard"),
            P("shard", None),
            P("shard", None),
            P("shard", None),
        ),
        check_vma=False,
    )
```

profile of v0, /device:TPU:0, one launch (start us, length us, event | category | flops | bytes accessed | tf_op | source)
XLA Modules:
  0.0 2669.2 jit_solution(14119255060265108069)
XLA Ops:
  99.0 133.2 %all-gather.7.cloned.1.call-done = bf16[1024,6144]{1,0:T(8,128)(2,1)} async-done(((bf16[256,6144]{1,0:T(8,128)(2,1)}), bf16[1024,6144]{1,0:T(8,128)(2,1)}) %all-gather.7.cloned.1.call-update) | async-done | bytes 12582928 | tf_op jit(solution)/shard_map/all_gather | solution.py:185
  271.9 575.0 %while.91 = (s32[]{:T(128)}, f32[8,256,128]{2,1,0:T(8,128)S(1)}, f32[8,64,8,256]{3,1,2,0:T(8,128)}, f32[8,8,64]{2,1,0:T(8,128)}, f32[8,1,64]{2,1,0:T(1,128)}, /*...) while((s32[]{:T(128)}, f32[8,256,128]{2,1,0:T(8,128)S(1)}, ...), condition=%wide.region_4.5_spmd.clone.clone, body=%wide.region_2.4_spmd.clone.clone.sunk | while | flops 909509440 | bytes 20685872 | solution.py:119
  287.5 39.9 %custom-call.54 = f32[8,1,64,64]{2,3,1,0:T(8,128)} custom-call(f32[8,1,64,64]{3,2,1,0:T(8,128)S(1)} %get-tuple-element.2802), custom_call_target="InvertDiagBlocksLowerTriangular" | custom-call | tf_op jit(solution)/shard_map/jvp()/while/body/eval_jaxpr/jit(_solve_triangular)/vmap()/triangular_solve | solution.py:89
  359.3 39.9 %custom-call.54 = f32[8,1,64,64]{2,3,1,0:T(8,128)} custom-call(f32[8,1,64,64]{3,2,1,0:T(8,128)S(1)} %get-tuple-element.2802), custom_call_target="InvertDiagBlocksLowerTriangular" | custom-call | tf_op jit(solution)/shard_map/jvp()/while/body/eval_jaxpr/jit(_solve_triangular)/vmap()/triangular_solve | solution.py:89
  431.0 39.9 %custom-call.54 = f32[8,1,64,64]{2,3,1,0:T(8,128)} custom-call(f32[8,1,64,64]{3,2,1,0:T(8,128)S(1)} %get-tuple-element.2802), custom_call_target="InvertDiagBlocksLowerTriangular" | custom-call | tf_op jit(solution)/shard_map/jvp()/while/body/eval_jaxpr/jit(_solve_triangular)/vmap()/triangular_solve | solution.py:89
  503.0 39.9 %custom-call.54 = f32[8,1,64,64]{2,3,1,0:T(8,128)} custom-call(f32[8,1,64,64]{3,2,1,0:T(8,128)S(1)} %get-tuple-element.2802), custom_call_target="InvertDiagBlocksLowerTriangular" | custom-call | tf_op jit(solution)/shard_map/jvp()/while/body/eval_jaxpr/jit(_solve_triangular)/vmap()/triangular_solve | solution.py:89
  574.8 39.9 %custom-call.54 = f32[8,1,64,64]{2,3,1,0:T(8,128)} custom-call(f32[8,1,64,64]{3,2,1,0:T(8,128)S(1)} %get-tuple-element.2802), custom_call_target="InvertDiagBlocksLowerTriangular" | custom-call | tf_op jit(solution)/shard_map/jvp()/while/body/eval_jaxpr/jit(_solve_triangular)/vmap()/triangular_solve | solution.py:89
  646.6 39.9 %custom-call.54 = f32[8,1,64,64]{2,3,1,0:T(8,128)} custom-call(f32[8,1,64,64]{3,2,1,0:T(8,128)S(1)} %get-tuple-element.2802), custom_call_target="InvertDiagBlocksLowerTriangular" | custom-call | tf_op jit(solution)/shard_map/jvp()/while/body/eval_jaxpr/jit(_solve_triangular)/vmap()/triangular_solve | solution.py:89
  718.5 39.9 %custom-call.54 = f32[8,1,64,64]{2,3,1,0:T(8,128)} custom-call(f32[8,1,64,64]{3,2,1,0:T(8,128)S(1)} %get-tuple-element.2802), custom_call_target="InvertDiagBlocksLowerTriangular" | custom-call | tf_op jit(solution)/shard_map/jvp()/while/body/eval_jaxpr/jit(_solve_triangular)/vmap()/triangular_solve | solution.py:89
  790.2 39.9 %custom-call.54 = f32[8,1,64,64]{2,3,1,0:T(8,128)} custom-call(f32[8,1,64,64]{3,2,1,0:T(8,128)S(1)} %get-tuple-element.2802), custom_call_target="InvertDiagBlocksLowerTriangular" | custom-call | tf_op jit(solution)/shard_map/jvp()/while/body/eval_jaxpr/jit(_solve_triangular)/vmap()/triangular_solve | solution.py:89
  934.7 635.7 %while.90 = (s32[]{:T(128)}, f32[8,256,128]{2,1,0:T(8,128)S(1)}, f32[8,64,8,128]{3,2,1,0:T(8,128)}, f32[8,64,8,128]{3,2,1,0:T(8,128)}, f32[8,64,8,256]{3,2,1,0:T...) while((s32[]{:T(128)}, f32[8,256,128]{2,1,0:T(8,128)S(1)}, ...), condition=%wide.region_18.19_spmd.clone, body=%wide.region_9.18_spmd.clone.sunk | while | flops 1843081216 | bytes 33436040 | solution.py:119
  948.8 39.3 %custom-call.53 = f32[8,1,64,64]{2,3,1,0:T(8,128)S(1)} custom-call(f32[8,1,64,64]{3,2,1,0:T(8,128)S(1)} %add_bitcast_fusion.3), custom_call_target="InvertDiagBlocksLowerTriangular" | custom-call | tf_op jit(solution)/shard_map/transpose(jvp())/while/body/eval_jaxpr/jit(_solve_triangular)/vmap()/triangular_solve | solution.py:89
  1028.2 39.3 %custom-call.53 = f32[8,1,64,64]{2,3,1,0:T(8,128)S(1)} custom-call(f32[8,1,64,64]{3,2,1,0:T(8,128)S(1)} %add_bitcast_fusion.3), custom_call_target="InvertDiagBlocksLowerTriangular" | custom-call | tf_op jit(solution)/shard_map/transpose(jvp())/while/body/eval_jaxpr/jit(_solve_triangular)/vmap()/triangular_solve | solution.py:89
  1107.6 39.3 %custom-call.53 = f32[8,1,64,64]{2,3,1,0:T(8,128)S(1)} custom-call(f32[8,1,64,64]{3,2,1,0:T(8,128)S(1)} %add_bitcast_fusion.3), custom_call_target="InvertDiagBlocksLowerTriangular" | custom-call | tf_op jit(solution)/shard_map/transpose(jvp())/while/body/eval_jaxpr/jit(_solve_triangular)/vmap()/triangular_solve | solution.py:89
  1187.0 39.3 %custom-call.53 = f32[8,1,64,64]{2,3,1,0:T(8,128)S(1)} custom-call(f32[8,1,64,64]{3,2,1,0:T(8,128)S(1)} %add_bitcast_fusion.3), custom_call_target="InvertDiagBlocksLowerTriangular" | custom-call | tf_op jit(solution)/shard_map/transpose(jvp())/while/body/eval_jaxpr/jit(_solve_triangular)/vmap()/triangular_solve | solution.py:89
  1266.3 39.3 %custom-call.53 = f32[8,1,64,64]{2,3,1,0:T(8,128)S(1)} custom-call(f32[8,1,64,64]{3,2,1,0:T(8,128)S(1)} %add_bitcast_fusion.3), custom_call_target="InvertDiagBlocksLowerTriangular" | custom-call | tf_op jit(solution)/shard_map/transpose(jvp())/while/body/eval_jaxpr/jit(_solve_triangular)/vmap()/triangular_solve | solution.py:89
  1345.7 39.3 %custom-call.53 = f32[8,1,64,64]{2,3,1,0:T(8,128)S(1)} custom-call(f32[8,1,64,64]{3,2,1,0:T(8,128)S(1)} %add_bitcast_fusion.3), custom_call_target="InvertDiagBlocksLowerTriangular" | custom-call | tf_op jit(solution)/shard_map/transpose(jvp())/while/body/eval_jaxpr/jit(_solve_triangular)/vmap()/triangular_solve | solution.py:89
  1425.0 39.3 %custom-call.53 = f32[8,1,64,64]{2,3,1,0:T(8,128)S(1)} custom-call(f32[8,1,64,64]{3,2,1,0:T(8,128)S(1)} %add_bitcast_fusion.3), custom_call_target="InvertDiagBlocksLowerTriangular" | custom-call | tf_op jit(solution)/shard_map/transpose(jvp())/while/body/eval_jaxpr/jit(_solve_triangular)/vmap()/triangular_solve | solution.py:89
  1504.5 39.3 %custom-call.53 = f32[8,1,64,64]{2,3,1,0:T(8,128)S(1)} custom-call(f32[8,1,64,64]{3,2,1,0:T(8,128)S(1)} %add_bitcast_fusion.3), custom_call_target="InvertDiagBlocksLowerTriangular" | custom-call | tf_op jit(solution)/shard_map/transpose(jvp())/while/body/eval_jaxpr/jit(_solve_triangular)/vmap()/triangular_solve | solution.py:89
  1731.3 77.2 %reduce-scatter.20.cloned.1.call-done = bf16[512,1024]{1,0:T(8,128)(2,1)} async-done(((bf16[2048,1024]{1,0:T(8,128)(2,1)}), bf16[512,1024]{1,0:T(8,128)(2,1)}) %reduce-scatter.20.cloned.1.call-update) | async-done | bytes 1048592 | tf_op jit(solution)/shard_map/reduce_scatter | solution.py:257
  1808.5 105.0 %reduce-scatter.24.cloned.1.call-done = bf16[704,1024]{1,0:T(8,128)(2,1)} async-done(((bf16[2816,1024]{1,0:T(8,128)(2,1)}), bf16[704,1024]{1,0:T(8,128)(2,1)}) %reduce-scatter.24.cloned.1.call-update) | async-done | bytes 1441808 | tf_op jit(solution)/shard_map/reduce_scatter | solution.py:222
  1913.6 198.0 %reduce-scatter.22.cloned.1.call-done = bf16[256,5632]{1,0:T(8,128)(2,1)} async-done(((bf16[1024,5632]{1,0:T(8,128)(2,1)}), bf16[256,5632]{1,0:T(8,128)(2,1)}) %reduce-scatter.22.cloned.1.call-update) | async-done | bytes 2883600 | tf_op jit(solution)/shard_map/reduce_scatter | solution.py:219
  2111.5 215.3 %reduce-scatter.16.cloned.1.call-done = bf16[256,6144]{1,0:T(8,128)(2,1)} async-done(((bf16[1024,6144]{1,0:T(8,128)(2,1)}), bf16[256,6144]{1,0:T(8,128)(2,1)}) %reduce-scatter.16.cloned.1.call-update) | async-done | bytes 3145744 | tf_op jit(solution)/shard_map/reduce_scatter | solution.py:251
  2326.8 335.1 %all-reduce.30 = (f32[2,256]{1,0:T(2,128)}, f32[256,6144]{1,0:T(8,128)}, f32[256,16]{0,1:T(8,128)}, f32[2,2]{1,0:T(2,128)}, f32[4,1024]{1,0:T(4,128)}, /*index=5...) all-reduce(bf16[2,256]{1,0:T(2,128)(2,1)S(1)} %copy.302, ...), channel_id=1, replica_groups=mesh['rep'=8,'shard'=4] {'rep'}, use_global_device_ids=true, to_apply=%region_24.25 | all-reduce | flops 4268612 | bytes 25611808 | tf_op jit(solution)/shard_map/psum | solution.py:276
  (916 shorter events, 951.0 us)
Async XLA Ops:
  7.2 56.6 %copy-start.70 = (f32[2,2]{1,0:T(2,128)S(1)}, f32[2,2]{1,0:T(2,128)}, u32[]{:S(2)}) copy-start(f32[2,2]{1,0:T(2,128)} %param.21) | copy-start | bytes 52
  7.3 225.0 %all-gather.7.cloned.1.call-start = ((), (), s32[]{:S(2)}) async-start(), calls=%async_computation.8 | async-start | bytes 15728640 | tf_op jit(solution)/shard_map/all_gather | solution.py:185
  8.0 856.2 %all-gather.9.cloned.1.call-start = ((), (), s32[]{:S(2)}) async-start(), calls=%async_computation.9 | async-start | bytes 5242880 | tf_op jit(solution)/shard_map/all_gather | solution.py:204
  8.7 70.8 %copy-start.58 = (f32[4,1024]{1,0:T(4,128)S(1)}, f32[4,1024]{1,0:T(4,128)}, u32[]{:S(2)}) copy-start(f32[4,1024]{1,0:T(4,128)} %param.22) | copy-start | bytes 49156
  8.7 860.8 %all-gather.11.cloned.1.call-start = ((), (), s32[]{:S(2)}) async-start(), calls=%async_computation.10 | async-start | bytes 14417920 | tf_op jit(solution)/shard_map/all_gather | solution.py:208
  9.5 874.4 %all-gather.13.cloned.1.call-start = ((), (), s32[]{:S(2)}) async-start(), calls=%async_computation.11 | async-start | bytes 7208960 | tf_op jit(solution)/shard_map/all_gather | solution.py:211
  10.1 1702.9 %reduce-scatter.30.cloned.1.call-start = ((), (), s32[]{:S(2)}) async-start(), calls=%async_computation.19 | async-start | bytes 81920
  10.5 239.9 %copy-start.47 = (f32[512]{0:T(512)}, f32[512]{0:T(512)S(1)}, u32[]{:S(2)}) copy-start(f32[512]{0:T(512)S(1)} %get-tuple-element.2343) | copy-start | bytes 6148
  10.5 240.0 %copy-start.49 = (f32[512]{0:T(512)}, f32[512]{0:T(512)S(1)}, u32[]{:S(2)}) copy-start(f32[512]{0:T(512)S(1)} %get-tuple-element.2344) | copy-start | bytes 6148
  10.5 240.0 %copy-start.51 = (f32[512]{0:T(512)}, f32[512]{0:T(512)S(1)}, u32[]{:S(2)}) copy-start(f32[512]{0:T(512)S(1)} %get-tuple-element.2345) | copy-start | bytes 6148
  40.9 205.6 %copy-start.23 = (f32[1,1024]{1,0:T(1,128)}, f32[1,1024]{1,0:T(1,128)S(1)}, u32[]{:S(2)}) copy-start(f32[1,1024]{1,0:T(1,128)S(1)} %get-tuple-element.2342) | copy-start | bytes 12292
  41.1 205.3 %copy-start.53 = (f32[512]{0:T(512)}, f32[512]{0:T(512)S(1)}, u32[]{:S(2)}) copy-start(f32[512]{0:T(512)S(1)} %fusion.180) | copy-start | bytes 6148
  41.2 205.3 %copy-start.26 = (f32[512]{0:T(512)}, f32[512]{0:T(512)S(1)}, u32[]{:S(2)}) copy-start(f32[512]{0:T(512)S(1)} %fusion.203) | copy-start | bytes 6148
  98.3 152.2 %copy-start.28 = (f32[1,4096]{1,0:T(1,128)}, f32[1,4096]{1,0:T(1,128)S(1)}, u32[]{:S(2)}) copy-start(f32[1,4096]{1,0:T(1,128)S(1)} %get-tuple-element.2334) | copy-start | bytes 49156
  98.3 152.2 %copy-start.30 = (f32[1,4096]{1,0:T(1,128)}, f32[1,4096]{1,0:T(1,128)S(1)}, u32[]{:S(2)}) copy-start(f32[1,4096]{1,0:T(1,128)S(1)} %get-tuple-element.2335) | copy-start | bytes 49156
  98.3 152.2 %copy-start.32 = (f32[1,4096]{1,0:T(1,128)}, f32[1,4096]{1,0:T(1,128)S(1)}, u32[]{:S(2)}) copy-start(f32[1,4096]{1,0:T(1,128)S(1)} %get-tuple-element.2336) | copy-start | bytes 49156
  98.3 152.2 %copy-start.34 = (f32[1,4096]{1,0:T(1,128)}, f32[1,4096]{1,0:T(1,128)S(1)}, u32[]{:S(2)}) copy-start(f32[1,4096]{1,0:T(1,128)S(1)} %get-tuple-element.2333) | copy-start | bytes 49156
  1645.3 68.5 %reduce-scatter.26.cloned.1.call-start = ((), (), s32[]{:S(2)}) async-start(), calls=%async_computation.17 | async-start | bytes 327680
  1646.3 68.5 %reduce-scatter.28.cloned.1.call-start = ((), (), s32[]{:S(2)}) async-start(), calls=%async_computation.18 | async-start | bytes 1310720
  1647.8 83.5 %reduce-scatter.18.cloned.1.call-start = ((), (), s32[]{:S(2)}) async-start(), calls=%async_computation.13 | async-start | bytes 40960 | tf_op jit(solution)/shard_map/reduce_scatter | solution.py:254
  1649.0 159.6 %reduce-scatter.20.cloned.1.call-start = ((), (), s32[]{:S(2)}) async-start(), calls=%async_computation.14 | async-start | bytes 5242880 | tf_op jit(solution)/shard_map/reduce_scatter | solution.py:257
  1655.7 257.8 %reduce-scatter.24.cloned.1.call-start = ((), (), s32[]{:S(2)}) async-start(), calls=%async_computation.16 | async-start | bytes 7208960 | tf_op jit(solution)/shard_map/reduce_scatter | solution.py:222
  1663.6 448.0 %reduce-scatter.22.cloned.1.call-start = ((), (), s32[]{:S(2)}) async-start(), calls=%async_computation.15 | async-start | bytes 14417920 | tf_op jit(solution)/shard_map/reduce_scatter | solution.py:219
  1677.5 649.2 %reduce-scatter.16.cloned.1.call-start = ((), (), s32[]{:S(2)}) async-start(), calls=%async_computation.12 | async-start | bytes 15728640 | tf_op jit(solution)/shard_map/reduce_scatter | solution.py:251
  (70 other events, 567.8 us)
Sparse Core Ops, SparseCore 0:
  9.7 222.5 all-gather.6
  233.8 79.0 all-gather.8
  314.5 200.1 all-gather.10
  516.2 105.1 all-gather.12
  1645.4 17.3 reduce-scatter.29
  1665.0 17.7 reduce-scatter.25
  1685.7 25.6 reduce-scatter.27
  1713.7 17.5 reduce-scatter.17
  1733.6 74.8 reduce-scatter.19
  1810.8 102.7 reduce-scatter.23
  1916.0 195.4 reduce-scatter.21
  2113.8 212.8 reduce-scatter.15
where the time goes:
time: 2690 us; the launch traced here: 2670 us
  other arithmetic  802 us (30%)
  waiting for transfers between devices  747 us (28%)
  matrix products  511 us (19%)
  blocking collectives  426 us (16%)
  local copies, waits for them, and re-layouts  162 us (6%)
    another operation x72, other arithmetic, span_step(): jax.scipy.linalg.solve_triangular(system, right, lower=True, unit_diagona...  643 us
    psum x1, blocking collectives, body(): lax.psum((ffn_shares[0], ffn_shares[1], mix_shares[0], mix_shares[1], mix...  335 us
    reduce_scatter x1, waiting for transfers between devices, body(): lax.psum_scatter(grad_mix_in_local.astype(jnp.bfloat16), 'shard', scatter...  215 us
    reduce_scatter x1, waiting for transfers between devices, body(): lax.psum_scatter(grad_gate_up_local.astype(jnp.bfloat16), 'shard', scatte...  198 us
    all_gather x1, waiting for transfers between devices, body(): lax.all_gather(w_mix_in, 'shard', axis=0, tiled=True)  133 us
    reduce_scatter x1, waiting for transfers between devices, body(): lax.psum_scatter(grad_down_local.astype(jnp.bfloat16), 'shard', scatter_d...  105 us
    reduce_scatter x1, waiting for transfers between devices, body(): lax.psum_scatter(grad_mix_out_local.astype(jnp.bfloat16), 'shard', scatte...  77.2 us
    dot_general x24, matrix products, span_step(): jnp.einsum('hvd,ihd->hiv', state, keys_unit, precision=HIGHEST)  67.1 us
  transfers between devices with their start and end apart: 12, of which 6 were waited for; matrix products, arithmetic and copies ran while one was open for 27% of the time, Pallas kernels for 0%

commit v1 on v0

v1 whole, which is shorter than its diff:
```python
import functools

import jax
import jax.numpy as jnp
from jax import lax
from jax.experimental import pallas as pl
from jax.experimental.pallas import tpu as pltpu
from jax.sharding import PartitionSpec as P

HEADS = 8
DK = 128
DV = 256
FF = 2816
CONV = 4
KEYS = 1024
VALS = 2048
CHUNK = 128
epsilon = 1e-06
out_floor = 0.01
BF = jnp.bfloat16
F32 = jnp.float32


def dot_nn(a, b):
    return jnp.dot(a, b, preferred_element_type=F32)


def dot_nt(a, b):
    return lax.dot_general(a, b, (((1,), (1,)), ((), ())), preferred_element_type=F32)


def dot_tn(a, b):
    return lax.dot_general(a, b, (((0,), (0,)), ((), ())), preferred_element_type=F32)


def twice(x):
    return jnp.concatenate([x, x], axis=1)


def sigmoid(x):
    return 1.0 / (1.0 + jnp.exp(-x))


def column(row):
    return jnp.broadcast_to(row, (CHUNK, CHUNK)).T


def fill_masks(seg_ref, mask_ref):
    rows = seg_ref.shape[0]
    seg = seg_ref[...]
    at = lax.broadcasted_iota(jnp.int32, seg.shape, 0)
    for shift in range(1, CONV):
        match = (pltpu.roll(seg, shift, 0) == seg) & (at >= shift)
        mask_ref[shift - 1] = match.astype(F32)


def fill_sums(gamma_ref, sums_ref):
    lane = lax.broadcasted_iota(jnp.int32, (HEADS, CHUNK), 1)
    for c in range(gamma_ref.shape[1] // CHUNK):
        span = pl.ds(c * CHUNK, CHUNK)
        total = gamma_ref[:, span]
        step = 1
        while step < CHUNK:
            total = total + jnp.where(lane >= step, pltpu.roll(total, step, 1), 0.0)
            step *= 2
        for i in range(HEADS):
            sums_ref[i, :, span] = total[i : i + 1]


def wide(mask, columns):
    return mask if columns == CHUNK else twice(mask)


def convolve(x, taps, mask_ref):
    total = x * taps[0:1]
    for shift in range(1, CONV):
        total = total + pltpu.roll(x, shift, 0) * (wide(mask_ref[shift - 1], x.shape[1]) * taps[shift : shift + 1])
    return total


def inverses(systems):
    row = lax.broadcasted_iota(jnp.int32, (CHUNK, CHUNK), 0)
    col = lax.broadcasted_iota(jnp.int32, (CHUNK, CHUNK), 1)
    eye = (row == col).astype(F32)
    near = (row // 2) == (col // 2)
    found = [eye - jnp.where(near, a, 0.0) for a in systems]
    size = 2
    while size < CHUNK:
        part = ((row // (2 * size)) == (col // (2 * size))) & ((row // size) != (col // size))
        packed = [x.astype(BF) for x in found]
        inner = [dot_nn(jnp.where(part, a, 0.0).astype(BF), x).astype(BF) for a, x in zip(systems, packed)]
        found = [x - dot_nn(p, i) for x, p, i in zip(found, packed, inner)]
        size *= 2
    return [x.astype(BF) for x in found]


def chunk_scales(c, h, sums_ref, beta_ref, seg_ref, segrow_ref):
    span = pl.ds(c * CHUNK, CHUNK)
    seg = seg_ref[span, :]
    segrow = segrow_ref[0:1, span]
    sums = sums_ref[h, :, span]
    beta = column(beta_ref[0, :, span])
    down = column(sums)
    row = lax.broadcasted_iota(jnp.int32, (CHUNK, CHUNK), 0)
    col = lax.broadcasted_iota(jnp.int32, (CHUNK, CHUNK), 1)
    same = seg == segrow
    decays = jnp.exp(jnp.where(same & (row >= col), down - sums, -1e30))
    strict = jnp.where(row > col, decays, 0.0)
    ends = jnp.exp(jnp.where(seg == seg[CHUNK - 1 : CHUNK], down[CHUNK - 1 : CHUNK] - down, -1e30))
    if c:
        before = seg_ref[c * CHUNK - 1 : c * CHUNK, :]
        reach = jnp.where(seg == before, jnp.exp(down), 0.0)
    else:
        reach = None
    return beta, decays, strict, ends, reach


def mix_kernel(
    q_ref, k_ref, v_ref, gate_ref, seg_ref, segrow_ref, gamma_ref, beta_ref,
    tapq_ref, tapk_ref, tapv_ref, gain_ref,
    mixed_ref, out_ref, fresh_ref, inv_ref, state_ref,
    mask_ref, sums_ref,
):
    h = pl.program_id(0)

    @pl.when(h == 0)
    def _():
        fill_masks(seg_ref, mask_ref)
        fill_sums(gamma_ref, sums_ref)

    rows = q_ref.shape[0]
    chunks = rows // CHUNK

    def active(ref, tap_ref):
        total = convolve(ref[...].astype(F32), tap_ref[...], mask_ref)
        return total * sigmoid(total)

    q = active(q_ref, tapq_ref).astype(BF)
    kraw = active(k_ref, tapk_ref)
    k = (kraw * lax.rsqrt(jnp.sum(kraw * kraw, axis=-1, keepdims=True) + epsilon)).astype(BF)
    v = active(v_ref, tapv_ref).astype(BF)
    cut = lambda x, c: x[c * CHUNK : (c + 1) * CHUNK]
    scales = [chunk_scales(c, h, sums_ref, beta_ref, seg_ref, segrow_ref) for c in range(chunks)]
    systems = []
    attend = []
    for c in range(chunks):
        beta, decays, strict, ends, reach = scales[c]
        systems.append(beta * strict * dot_nt(cut(k, c), cut(k, c)))
        attend.append((decays * dot_nt(cut(q, c), cut(k, c))).astype(BF))
    found = inverses(systems)
    state = None
    for c in range(chunks):
        beta, decays, strict, ends, reach = scales[c]
        kc, qc, vc = cut(k, c), cut(q, c), cut(v, c).astype(F32)
        inv_ref[0, c] = found[c]
        if c:
            packed = state.astype(BF)
            state_ref[0, c] = packed
            right = twice(beta) * (vc - twice(reach) * dot_nn(kc, packed))
        else:
            state_ref[0, c] = jnp.zeros((DK, DV), BF)
            right = twice(beta) * vc
        fresh = dot_nn(found[c], right.astype(BF)).astype(BF)
        fresh_ref[c * CHUNK : (c + 1) * CHUNK, :] = fresh
        out = dot_nn(attend[c], fresh)
        if c:
            out = out + twice(reach) * dot_nn(qc, packed)
        if c < chunks - 1:
            grown = dot_tn((ends * kc.astype(F32)).astype(BF), fresh)
            state = grown + twice(reach[CHUNK - 1 : CHUNK]) * state if c else grown
        out_ref[c * CHUNK : (c + 1) * CHUNK, :] = out
        unit = out * lax.rsqrt(jnp.mean(out * out, axis=-1, keepdims=True) + out_floor)
        gate = gate_ref[c * CHUNK : (c + 1) * CHUNK, :].astype(F32)
        mixed_ref[c * CHUNK : (c + 1) * CHUNK, :] = (unit * gain_ref[...] * (gate * sigmoid(gate))).astype(BF)


def whole(shape):
    return pl.BlockSpec(shape, lambda h: (0,) * len(shape))


def per_head(rows):
    return pl.BlockSpec((1, 1, rows), lambda h: (h, 0, 0))


def mixer(projected, seg, segrow, gamma, beta, taps, gain):
    rows = projected.shape[0]
    chunks = rows // CHUNK
    return pl.pallas_call(
        mix_kernel,
        grid=(HEADS,),
        in_specs=[
            pl.BlockSpec((rows, DK), lambda h: (0, h)),
            pl.BlockSpec((rows, DK), lambda h: (0, HEADS + h)),
            pl.BlockSpec((rows, DV), lambda h: (0, HEADS + h)),
            pl.BlockSpec((rows, DV), lambda h: (0, 2 * HEADS + h)),
            whole((rows, CHUNK)), whole((8, rows)), whole((HEADS, rows)), per_head(rows),
            pl.BlockSpec((CONV, DK), lambda h: (0, h)),
            pl.BlockSpec((CONV, DK), lambda h: (0, HEADS + h)),
            pl.BlockSpec((CONV, DV), lambda h: (0, HEADS + h)),
            whole((1, DV)),
        ],
        out_specs=[
            pl.BlockSpec((rows, DV), lambda h: (0, h)),
            pl.BlockSpec((rows, DV), lambda h: (0, h)),
            pl.BlockSpec((rows, DV), lambda h: (0, h)),
            pl.BlockSpec((1, chunks, CHUNK, CHUNK), lambda h: (h, 0, 0, 0)),
            pl.BlockSpec((1, chunks, DK, DV), lambda h: (h, 0, 0, 0)),
        ],
        out_shape=[
            jax.ShapeDtypeStruct((rows, VALS), BF),
            jax.ShapeDtypeStruct((rows, VALS), F32),
            jax.ShapeDtypeStruct((rows, VALS), BF),
            jax.ShapeDtypeStruct((HEADS, chunks, CHUNK, CHUNK), BF),
            jax.ShapeDtypeStruct((HEADS, chunks, DK, DV), BF),
        ],
        scratch_shapes=[pltpu.VMEM((CONV - 1, rows, CHUNK), F32), pltpu.VMEM((HEADS, 1, rows), F32)],
        compiler_params=pltpu.CompilerParams(vmem_limit_bytes=48 * 2**20),
        cost_estimate=pl.CostEstimate(flops=int(3e10), bytes_accessed=int(3e7), transcendentals=0),
    )(projected, projected, projected, projected, seg, segrow, gamma, beta[:, None], taps, taps, taps, gain)


def back_kernel(
    q_ref, k_ref, v_ref, gate_ref, seg_ref, segrow_ref, gamma_ref, beta_ref,
    tapq_ref, tapk_ref, tapv_ref, gain_ref, out_ref, fresh_ref, inv_ref, state_ref, back_ref,
    dq_ref, dk_ref, dv_ref, dgate_ref, dtapq_ref, dtapk_ref, dtapv_ref, dgain_ref, dgamma_ref, dbeta_ref,
    mask_ref, sums_ref, lift_ref,
):
    h = pl.program_id(0)

    @pl.when(h == 0)
    def _():
        fill_masks(seg_ref, mask_ref)
        fill_sums(gamma_ref, sums_ref)
        dgain_ref[...] = jnp.zeros_like(dgain_ref)

    rows = q_ref.shape[0]
    chunks = rows // CHUNK

    def active(ref, tap_ref):
        total = convolve(ref[...].astype(F32), tap_ref[...], mask_ref)
        s = sigmoid(total)
        return total * s, s * (1.0 + total * (1.0 - s))

    qf, qslope = active(q_ref, tapq_ref)
    kraw, kslope = active(k_ref, tapk_ref)
    vf, vslope = active(v_ref, tapv_ref)
    kscale = lax.rsqrt(jnp.sum(kraw * kraw, axis=-1, keepdims=True) + epsilon)
    kunit = kraw * kscale
    q, k, v = qf.astype(BF), kunit.astype(BF), vf.astype(BF)
    cut = lambda x, c: x[c * CHUNK : (c + 1) * CHUNK]
    gain = gain_ref[...]
    carried = None
    dqs, dks, dvs = [None] * chunks, [None] * chunks, [None] * chunks
    dgain = jnp.zeros((1, DV), F32)
    for c in reversed(range(chunks)):
        span = pl.ds(c * CHUNK, CHUNK)
        beta, decays, strict, ends, reach = chunk_scales(c, h, sums_ref, beta_ref, seg_ref, segrow_ref)
        kc, qc, vc = cut(k, c), cut(q, c), cut(v, c).astype(F32)
        kcf, qcf = kc.astype(F32), qc.astype(F32)
        out, gate, back = out_ref[span, :], gate_ref[span, :].astype(F32), back_ref[span, :].astype(F32)
        p = lax.rsqrt(jnp.mean(out * out, axis=-1, keepdims=True) + out_floor)
        z = out * p
        s = sigmoid(gate)
        a = back * (gate * s)
        az = a * z
        dgain = dgain + jnp.sum(az, axis=0, keepdims=True)
        dgate_ref[span, :] = (back * (z * gain) * (s * (1.0 + gate * (1.0 - s)))).astype(BF)
        dout = p * (a * gain - z * jnp.mean(az * gain, axis=-1, keepdims=True))
        doutb = dout.astype(BF)
        key_key = dot_nt(kc, kc)
        query_key = dot_nt(qc, kc)
        attend = (decays * query_key).astype(BF)
        fresh = fresh_ref[span, :]
        found = inv_ref[0, c]
        dfresh = dot_tn(attend, doutb)
        if carried is not None:
            carriedb = carried.astype(BF)
            dfresh = dfresh + twice(ends) * dot_nn(kc, carriedb)
        dscore = decays * dot_nt(doutb, fresh)
        dright = dot_tn(found, dfresh.astype(BF))
        drightb = dright.astype(BF)
        dsystem = dot_nt(drightb, fresh)
        dvs[c] = twice(beta) * dright
        m = key_key * (strict * dsystem)
        dkk = (beta * strict) * dsystem
        tally = query_key * dscore - beta * m
        dscoreb = dscore.astype(BF)
        dq = dot_nn(dscoreb, kc)
        dk = dot_tn(dscoreb, qc) - dot_nn((dkk + dkk.T).astype(BF), kc)
        side = tally
        edge = None
        if carried is not None:
            dkf = dot_nt((twice(ends) * fresh.astype(F32)).astype(BF), carriedb)
            dk = dk + dkf
            moved = kcf * dkf
            side = side - moved
            edge = jnp.sum(moved, axis=0, keepdims=True)
        if c:
            state = state_ref[0, c]
            rout = (twice(reach) * dout).astype(BF)
            given = dot_nn(kc, state)
            drest = dright * (vc - twice(reach) * given)
            w = (-twice(beta * reach) * dright).astype(BF)
            dqs1 = dot_nt(rout, state)
            dks1 = dot_nt(w, state)
            dq = dq + dqs1
            dk = dk + dks1
            side = side + qcf * dqs1 + kcf * dks1
            grown = dot_tn(jnp.concatenate([qc, kc], axis=0), jnp.concatenate([rout, w], axis=0))
            if carried is not None:
                last = reach[CHUNK - 1 : CHUNK]
                kept = carried * state.astype(F32)
                edge = edge + last * jnp.sum(kept[:, :CHUNK] + kept[:, CHUNK:], axis=0, keepdims=True)
                carried = twice(last) * carried + grown
            else:
                carried = grown
        else:
            drest = dright * vc
        dqs[c] = dq
        dks[c] = dk
        dbeta = drest[:, :CHUNK] + drest[:, CHUNK:] - m
        dbeta_ref[0, :, span] = jnp.sum(dbeta.T, axis=0, keepdims=True)
        lift = jnp.sum(side.T - tally, axis=0, keepdims=True)
        if edge is not None:
            lane = lax.broadcasted_iota(jnp.int32, (1, CHUNK), 1)
            lift = lift + jnp.where(lane == CHUNK - 1, jnp.sum(edge, axis=1, keepdims=True), 0.0)
        lift_ref[h, :, span] = lift
    dgain_ref[...] += dgain

    def spread(grad, ref, tap_ref, to_ref, dtap_ref):
        x, taps = ref[...].astype(F32), tap_ref[...]
        total = grad * taps[0:1]
        sums = [jnp.sum(grad * x, axis=0, keepdims=True)]
        for shift in range(1, CONV):
            masked = grad * wide(mask_ref[shift - 1], x.shape[1])
            sums.append(jnp.sum(masked * pltpu.roll(x, shift, 0), axis=0, keepdims=True))
            total = total + pltpu.roll(masked, rows - shift, 0) * taps[shift : shift + 1]
        to_ref[...] = total.astype(BF)
        dtap_ref[...] = jnp.concatenate(sums, axis=0)

    spread(jnp.concatenate(dqs, axis=0) * qslope, q_ref, tapq_ref, dq_ref, dtapq_ref)
    dk = jnp.concatenate(dks, axis=0)
    dk = kscale * (dk - kunit * jnp.sum(kunit * dk, axis=-1, keepdims=True))
    spread(dk * kslope, k_ref, tapk_ref, dk_ref, dtapk_ref)
    spread(jnp.concatenate(dvs, axis=0) * vslope, v_ref, tapv_ref, dv_ref, dtapv_ref)

    @pl.when(h == HEADS - 1)
    def _():
        lane = lax.broadcasted_iota(jnp.int32, (HEADS, CHUNK), 1)
        for c in range(chunks):
            span = pl.ds(c * CHUNK, CHUNK)
            total = jnp.concatenate([lift_ref[i, :, span] for i in range(HEADS)], axis=0)
            step = 1
            while step < CHUNK:
                total = total + jnp.where(lane < CHUNK - step, pltpu.roll(total, CHUNK - step, 1), 0.0)
                step *= 2
            dgamma_ref[:, span] = total


def mixer_back(projected, seg, segrow, gamma, beta, taps, gain, out, fresh, inv, state, back):
    rows = projected.shape[0]
    chunks = rows // CHUNK
    cols = lambda width, at: pl.BlockSpec((rows, width), lambda h: (0, at + h))
    tap = lambda width, at: pl.BlockSpec((CONV, width), lambda h: (0, at + h))
    return pl.pallas_call(
        back_kernel,
        grid=(HEADS,),
        in_specs=[
            cols(DK, 0), cols(DK, HEADS), cols(DV, HEADS), cols(DV, 2 * HEADS),
            whole((rows, CHUNK)), whole((8, rows)), whole((HEADS, rows)), per_head(rows),
            tap(DK, 0), tap(DK, HEADS), tap(DV, HEADS), whole((1, DV)),
            cols(DV, 0), cols(DV, 0),
            pl.BlockSpec((1, chunks, CHUNK, CHUNK), lambda h: (h, 0, 0, 0)),
            pl.BlockSpec((1, chunks, DK, DV), lambda h: (h, 0, 0, 0)),
            cols(DV, 0),
        ],
        out_specs=[
            cols(DK, 0), cols(DK, 0), cols(DV, 0), cols(DV, 0),
            tap(DK, 0), tap(DK, 0), tap(DV, 0),
            whole((1, DV)), whole((HEADS, rows)), per_head(rows),
        ],
        out_shape=[
            jax.ShapeDtypeStruct((rows, KEYS), BF),
            jax.ShapeDtypeStruct((rows, KEYS), BF),
            jax.ShapeDtypeStruct((rows, VALS), BF),
            jax.ShapeDtypeStruct((rows, VALS), BF),
            jax.ShapeDtypeStruct((CONV, KEYS), F32),
            jax.ShapeDtypeStruct((CONV, KEYS), F32),
            jax.ShapeDtypeStruct((CONV, VALS), F32),
            jax.ShapeDtypeStruct((1, DV), F32),
            jax.ShapeDtypeStruct((HEADS, rows), F32),
            jax.ShapeDtypeStruct((HEADS, 1, rows), F32),
        ],
        scratch_shapes=[
            pltpu.VMEM((CONV - 1, rows, CHUNK), F32),
            pltpu.VMEM((HEADS, 1, rows), F32),
            pltpu.VMEM((HEADS, 1, rows), F32),
        ],
        compiler_params=pltpu.CompilerParams(vmem_limit_bytes=56 * 2**20),
        cost_estimate=pl.CostEstimate(flops=int(6e10), bytes_accessed=int(4e7), transcendentals=0),
    )(projected, projected, projected, projected, seg, segrow, gamma, beta[:, None], taps, taps, taps, gain, out, fresh, inv, state, back)


SHIFTS = (1, 2, 3)


def place():
    rep = lax.axis_index("rep")
    core, x, y = rep % 2, (rep // 2) % 2, (rep // 4) % 2
    a = jnp.where(core == 0, x, y)
    b = jnp.where(core == 0, y, x)
    return core, a, b


def hop(value, kind):
    count = lax.axis_size("rep")
    if kind == "core":
        pairs = [(i, i ^ 1) for i in range(count)]
    elif kind == "first":
        pairs = [(i, i ^ (4 if i & 1 else 2)) for i in range(count)]
    elif kind == "second":
        pairs = [(i, i ^ (2 if i & 1 else 4)) for i in range(count)]
    else:
        pairs = [(i, i ^ kind) for i in range(count)]
    return lax.ppermute(value, "rep", pairs)


def shift(value, by):
    count = lax.axis_size("shard")
    return lax.ppermute(value, "shard", [(i, (i + by) % count) for i in range(count)])


def assemble_kernel(along, size, rows, at_ref, *refs):
    own, pieces, whole_ref = refs[0], refs[1:-1], refs[-1]
    whole_ref[pl.ds(pl.multiple_of(at_ref[0] * rows, 16), rows), :] = own[...]
    for n, piece in enumerate(pieces):
        block, part = at_ref[1 + 2 * n], at_ref[2 + 2 * n]
        if along == 0:
            whole_ref[pl.ds(pl.multiple_of(block * rows + part * size, 16), size), :] = piece[...]
        else:
            whole_ref[pl.ds(pl.multiple_of(block * rows, 16), rows), pl.ds(pl.multiple_of(part * size, 128), size)] = piece[...]


def gather(weight, along):
    core, a, b = place()
    z = lax.axis_index("shard")
    count = lax.axis_size("shard")
    size = weight.shape[along] // 8
    rows = weight.shape[0]
    part = core * 4 + a * 2 + b
    other = (1 - core) * 4 + b * 2 + a
    mine = lax.dynamic_slice_in_dim(weight, part * size, size, along)
    at, pieces = [z], []
    for by in range(1, count):
        block = (z - by) % count
        here = shift(mine, by)
        token = here
        first = hop(here, "first")
        found = [(here, 0), (first, 2), (hop(here, "second"), 1), (hop(first, "second"), 3)]
        for piece, flip in found:
            pieces += [piece, hop(piece, "core")]
            at += [block, part ^ flip, block, other ^ flip]
    full = pl.pallas_call(
        functools.partial(assemble_kernel, along, size, rows),
        in_specs=[pl.BlockSpec(memory_space=pltpu.SMEM)] + [pl.BlockSpec(memory_space=pltpu.VMEM)] * (len(pieces) + 1),
        out_specs=pl.BlockSpec(memory_space=pltpu.VMEM),
        compiler_params=pltpu.CompilerParams(vmem_limit_bytes=48 * 2**20),
        out_shape=jax.ShapeDtypeStruct((rows * count, weight.shape[1]), BF),
    )(jnp.stack(at).astype(jnp.int32), weight, *pieces)
    return full, token


def pick(value, at, size, axis):
    return lax.dynamic_slice_in_dim(value, at * size, size, axis)


def join(bit, mine, theirs, axis):
    return jnp.where(bit == 0, jnp.concatenate([mine, theirs], axis), jnp.concatenate([theirs, mine], axis))


def reduce_grad(left, right):
    core, a, b = place()
    z = lax.axis_index("shard")
    count = lax.axis_size("shard")
    columns = right.shape[1]
    half, quarter = columns // 2, columns // 4
    rows = left.shape[1] // count
    got = hop(dot_tn(left, pick(right, 1 - core, half, 1)).astype(BF), "core")
    own = pick(right, core, half, 1)
    sent = dot_tn(left, pick(own, 1 - a, quarter, 1)) + pick(got, 1 - a, quarter, 1).astype(F32)
    got_first = hop(sent.astype(BF), "first")
    kept = dot_tn(left, pick(own, a, quarter, 1)) + pick(got, a, quarter, 1).astype(F32) + got_first.astype(F32)
    kept = kept.astype(BF).reshape(count, rows, quarter)
    axis = 2 if quarter % 256 == 0 else 1
    size = kept.shape[axis] // 2
    kept = (pick(kept, b, size, axis).astype(F32) + hop(pick(kept, 1 - b, size, axis), "second").astype(F32)).astype(BF)
    extra = 8
    while extra < lax.axis_size("rep"):
        kept = (kept.astype(F32) + hop(kept, extra).astype(F32)).astype(BF)
        extra *= 2
    total = pick(kept, z, 1, 0)[0].astype(F32)
    for by in range(1, count):
        total = total + shift(pick(kept, (z + by) % count, 1, 0)[0], by).astype(F32)
    done = total.astype(BF)
    done = join(b, done, hop(done, "second"), axis - 1)
    done = join(a, done, hop(done, "first"), 1)
    return join(core, done, hop(done, "core"), 1).astype(F32)


def rms_scale(values, gain):
    return values * lax.rsqrt(jnp.mean(values * values, axis=-1, keepdims=True) + epsilon) * gain


def swiglu(gate_up):
    return jax.nn.silu(gate_up[..., :FF]) * gate_up[..., FF:]


def after(value, *others):
    return lax.optimization_barrier((value,) + others)[0]


def share_small(arrays):
    count = lax.axis_size("shard")
    z = lax.axis_index("shard")
    flat = jnp.concatenate([x.astype(F32).reshape(-1) for x in arrays])
    flat = jnp.pad(flat, (0, -flat.shape[0] % 1024)).reshape(1, -1, 128)
    every = jnp.zeros((count,) + flat.shape[1:], F32)
    every = lax.dynamic_update_slice_in_dim(every, flat, z, 0)
    for by in range(1, count):
        every = lax.dynamic_update_slice_in_dim(every, shift(flat, by), (z - by) % count, 0)
    every = every.reshape(count, -1)
    found, start = [], 0
    for x in arrays:
        found.append(every[:, start : start + x.size].reshape((count,) + x.shape))
        start += x.size
    return found


def beside(blocks):
    return jnp.concatenate(list(blocks), axis=-1)


def body(
    hidden_in,
    segment_ids,
    norm_gains,
    w_mix_in,
    w_decay,
    decay_params,
    conv_weight,
    out_gain,
    w_mix_out,
    w_gate_up,
    w_down,
    cotangent,
):
    rows = hidden_in.shape[0]
    z = lax.axis_index("shard")
    small = share_small([norm_gains, decay_params, conv_weight, out_gain[None], w_decay])
    gains, rates, taps, gain_row = (beside(x) for x in small[:4])
    decay_full = small[4].reshape(-1, 2 * HEADS).astype(BF)
    mix_in, token = gather(w_mix_in, 1)
    mix_out, token = gather(after(w_mix_out, token), 1)
    gate_up_full, token = gather(after(w_gate_up, token), 0)
    down_full, token = gather(after(w_down, token), 1)

    hidden = hidden_in.astype(F32)
    normed_one_f, norm_one_pull = jax.vjp(rms_scale, hidden, gains[0])
    normed_one = normed_one_f.astype(BF)
    projected = dot_nn(normed_one, mix_in)
    logits = dot_nt(decay_full.T, normed_one)
    rate, bias = jnp.exp(rates[0])[:, None], rates[1][:, None]
    gamma = -rate * jax.nn.softplus(logits[:HEADS] + bias)
    beta = jax.nn.sigmoid(logits[HEADS:])
    seg = jnp.broadcast_to(segment_ids[:, None], (rows, CHUNK))
    segrow = jnp.broadcast_to(segment_ids[None], (8, rows))
    mixed_out, out, fresh, inv, state = mixer(projected, seg, segrow, gamma, beta, taps, gain_row)
    residual = hidden + dot_nn(mixed_out, mix_out)
    normed_two_f, norm_two_pull = jax.vjp(rms_scale, residual, gains[1])
    normed_two = normed_two_f.astype(BF)
    gate_up = dot_nn(normed_two, gate_up_full)
    inner_f, inner_pull = jax.vjp(swiglu, gate_up)
    inner = inner_f.astype(BF)
    result = (residual + dot_nn(inner, down_full)).astype(BF)
    inner_back = dot_nt(cotangent, down_full)
    (gate_up_grad,) = inner_pull(inner_back)
    gate_up_back = gate_up_grad.astype(BF)
    grad_down = reduce_grad(inner, cotangent)
    grad_gate_up = reduce_grad(normed_two, gate_up_back)
    normed_two_back = dot_nt(gate_up_back, gate_up_full)
    residual_part, gain_two = norm_two_pull(normed_two_back)
    residual_back = cotangent.astype(F32) + residual_part
    branch_back = residual_back.astype(BF)
    mixed_back = dot_nt(branch_back, mix_out)
    grad_mix_out = reduce_grad(mixed_out, branch_back)
    dq, dk, dv, dgate, dtq, dtk, dtv, dgain, dgamma, dbeta = mixer_back(
        projected, seg, segrow, gamma, beta, taps, gain_row, out, fresh, inv, state, mixed_back
    )
    dbeta = dbeta[:, 0]
    projected_back = jnp.concatenate([dq, dk, dv, dgate], axis=1)
    slope = -dgamma * rate * jax.nn.sigmoid(logits[:HEADS] + bias)
    logits_back = jnp.concatenate([slope, dbeta * beta * (1.0 - beta)], axis=0).astype(BF)
    grad_rates = jnp.stack([jnp.sum(dgamma * gamma, axis=1), jnp.sum(slope, axis=1)])
    grad_decay = lax.dot_general(normed_one, logits_back, (((0,), (1,)), ((), ())), preferred_element_type=F32)
    normed_one_back = dot_nt(projected_back, mix_in) + lax.dot_general(
        logits_back, decay_full, (((0,), (1,)), ((), ())), preferred_element_type=F32
    )
    grad_mix_in = reduce_grad(normed_one, projected_back)
    hidden_part, gain_one = norm_one_pull(normed_one_back)
    grad_in = residual_back + hidden_part

    parts = [jnp.stack([gain_one, gain_two]), grad_decay, grad_rates, jnp.concatenate([dtq, dtk, dtv], axis=1), dgain]
    flat = jnp.concatenate([x.reshape(-1) for x in parts])
    flat = jnp.pad(flat, (0, -flat.shape[0] % 1024)).reshape(-1, 128)
    flat = lax.psum(flat, ("rep", "shard")).reshape(-1)
    found, start = [], 0
    for x in parts:
        found.append(flat[start : start + x.size].reshape(x.shape))
        start += x.size
    count = lax.axis_size("shard")
    mine = lambda x, axis: lax.dynamic_slice_in_dim(x, z * (x.shape[axis] // count), x.shape[axis] // count, axis)
    return (
        result,
        grad_in,
        mine(found[0], 1),
        grad_mix_in,
        mine(found[1], 0),
        mine(found[2], 1),
        mine(found[3], 1),
        mine(found[4][0], 0),
        grad_mix_out,
        grad_gate_up,
        grad_down,
    )


def solution(mesh):
    rows, columns, both = P("shard", None), P(None, "shard"), P(("rep", "shard"), None)
    return jax.shard_map(
        body,
        mesh=mesh,
        in_specs=(both, P(("rep", "shard")), columns, rows, rows, columns, columns, P("shard"), rows, rows, rows, both),
        out_specs=(both, both, columns, rows, rows, columns, columns, P("shard"), rows, rows, rows),
        check_vma=False,
    )
```

time: 2690 us -> 849 us (0.32)
  other arithmetic: 802 us -> 65 us
  waiting for transfers between devices: 747 us -> 302 us
  blocking collectives: 426 us -> 0 us
  matrix products: 511 us -> 127 us
  starting transfers between devices: 0.48 us -> 139 us
  Pallas kernels: 0 us -> 107 us
  local copies, waits for them, and re-layouts: 162 us -> 81.1 us
    another operation x117 -> x1, other arithmetic: 661 us -> 0.01 us  [body(): jnp.stack([jnp.sum(dgamma * gamma, axis=1), jnp.sum(slope, axis=1)])]
    reduce_scatter x5 -> x0, waiting for transfers between devices: 611 us -> none  [the longest x1 215 us: body(): lax.psum_scatter(grad_mix_in_local.astype(jnp.bfloat16), 'shard', scatter...]
    dot_general x167 -> x23, matrix products: 470 us -> 127 us  [the longest x12 43.6 us: dot_tn(): lax.dot_general(a, b, (((0,), (0,)), ((), ())), preferred_element_type=F32)]
    psum x1 -> x0, blocking collectives: 335 us -> none  [body(): lax.psum((ffn_shares[0], ffn_shares[1], mix_shares[0], mix_shares[1], mix...]
    ppermute x0 -> x135, waiting for transfers between devices: none -> 201 us  [the longest x108 130 us: hop(): return lax.ppermute(value, 'rep', pairs)]
    ppermute x0 -> x135, starting transfers between devices: none -> 139 us  [the longest x27 74.4 us: shift(): lax.ppermute(value, 'shard', [(i, (i + by) % count) for i in range(count)])]
    all_gather x4 -> x0, waiting for transfers between devices: 133 us -> none  [the longest x1 133 us: body(): lax.all_gather(w_mix_in, 'shard', axis=0, tiled=True)]
    pallas_call x0 -> x6, Pallas kernels: none -> 107 us  [the longest x1 42.7 us: mixer_back(): pl.pallas_call(back_kernel, grid=(HEADS,), in_specs=[cols(DK, 0), cols(DK...]
  transfers between devices with their start and end apart: 12 -> 136, of which waited for: 6 -> 37; matrix products, arithmetic and copies ran while one was open for 27% -> 21% of each run, Pallas kernels for 0% -> 7%
where the time goes in v1:
time: 849 us; the launch traced here: 838 us
  waiting for transfers between devices  302 us (36%)
  starting transfers between devices  139 us (16%)
  matrix products  127 us (15%)
  Pallas kernels  107 us (13%)
  local copies, waits for them, and re-layouts  81.1 us (10%)
  other arithmetic  65 us (8%)
  between operations  16 us (2%)
    ppermute x108, waiting for transfers between devices, hop(): return lax.ppermute(value, 'rep', pairs)  130 us
    psum x1, waiting for transfers between devices, body(): flat = lax.psum(flat, ('rep', 'shard')).reshape(-1)  101 us
    ppermute x27, starting transfers between devices, shift(): lax.ppermute(value, 'shard', [(i, (i + by) % count) for i in range(count)])  74.4 us
    ppermute x27, waiting for transfers between devices, shift(): lax.ppermute(value, 'shard', [(i, (i + by) % count) for i in range(count)])  71.1 us
    ppermute x108, starting transfers between devices, hop(): return lax.ppermute(value, 'rep', pairs)  64.7 us
    unnamed x301, local copies, waits for them, and re-layouts  45.3 us
    dot_general x12, matrix products, dot_tn(): lax.dot_general(a, b, (((0,), (0,)), ((), ())), preferred_element_type=F32)  43.6 us
    pallas_call x1, Pallas kernels, mixer_back(): pl.pallas_call(back_kernel, grid=(HEADS,), in_specs=[cols(DK, 0), cols(DK...  42.7 us
  transfers between devices with their start and end apart: 136, of which 37 were waited for; matrix products, arithmetic and copies ran while one was open for 21% of the time, Pallas kernels for 7%

profile of v1, /device:TPU:0, one launch (start us, length us, event | category | flops | bytes accessed | tf_op | source)
XLA Modules:
  0.0 837.7 jit_solution(1249494972776474681)
XLA Ops:
  24.1 22.0 %collective-permute-start.27 = (bf16[512,128]{1,0:T(8,128)(2,1)S(1)}, bf16[512,128]{1,0:T(8,128)(2,1)S(1)}, u32[]{:S(2)}, u32[]{:S(2)}) collective-permute-start(bf16[512,128]{1,0:T(8,128)(2,1)S(1)} %constant_dynamic-slice_fusion.10), channel_id=1, source_target_pairs={{0,1},{1,2},{2,3},{3,0},{4,5},{5,6},{6,7},{7,4},{8,9},{9,10},{10,1... | collective-permute-start | bytes 393224 | tf_op jit(solution)/shard_map/ppermute | solution.py:430
  52.0 6.5 collective-permute-start.1
  127.5 12.2 %collective-permute-done.59.refs_9_ = bf16[32,5632]{1,0:T(8,128)(2,1)} collective-permute-done((bf16[32,5632]{1,0:T(8,128)(2,1)}, bf16[32,5632]{1,0:T(8,128)(2,1)}, u32[]{:S(2)}, u32[]{:S(2)}) %collective-permute-start.59) | collective-permute-done | bytes 360480 | tf_op jit(solution)/shard_map/ppermute | solution.py:430
  149.9 7.4 collective-permute-done.83.refs_9_
  235.0 8.8 %shard_map.203 = bf16[1024,6144]{1,0:T(8,128)(2,1)} custom-call(s32[49]{0:T(128)S(1)} %stack.46.at_ref, bf16[256,6144]{1,0:T(8,128)(2,1)} %refs_0_.1, bf16[256,768]{1,0:T(8,128)(2,1)S(1)} %collective-permute-done.3.refs_1_, bf16[256,768]{1,0:T(8,128)(2,1)S(1)} %copy-done.5, bf16[256,768]{1,0:T(8,128)(2,1)S(1)} %copy-done.7, ...), custom_call_target="tpu_custom_call" | custom-call | tf_op jit(solution)/shard_map/pallas_call | solution.py:463
  246.6 14.5 %fusion.87.q_ref.k_ref.v_ref.gate_ref = f32[512,6144]{1,0:T(8,128)} fusion(bf16[1024,6144]{1,0:T(8,128)(2,1)} %shard_map.203, bf16[512,1024]{1,0:T(8,128)(2,1)S(1)} %copy-done.86, f32[1024]{0:T(1024)S(1)} %bitcast.158, f32[512]{0:T(512)S(1)} %fusion.75), kind=kOutput, calls=%fused_computation.201 | convolution fusion | flops 6444548096 | bytes 26220544 | tf_op jit(solution)/shard_map/dot_general | solution.py:25
  263.8 37.4 %shard_map.204 = (bf16[512,2048]{1,0:T(8,128)(2,1)S(1)}, f32[512,2048]{1,0:T(8,128)}, bf16[512,2048]{1,0:T(8,128)(2,1)S(1)}, bf16[8,4,128,128]{3,2,1,0:T(8,128)(2,1)S(1)}, bf16[8,4,128,256]{3,2,1,0:T(8,128)(2,1)}) custom-call(f32[512,6144]{1,0:T(8,128)} %fusion.87.q_ref.k_ref.v_ref.gate_ref, f32[512,6144]{1,0:T(8,128)} %fusion.87.q_ref.k_ref.v_ref.gate_ref, ...), custom_call_target="tpu_custom_call" | custom-call | flops 30000001024 | bytes 30000000 | tf_op jit(solution)/shard_map/pallas_call | solution.py:188
  324.0 8.4 %shard_map.206 = bf16[1024,5632]{1,0:T(8,128)(2,1)} custom-call(s32[49]{0:T(128)S(1)} %stack.46.at_ref, bf16[256,5632]{1,0:T(8,128)(2,1)} %refs_0_.3, bf16[32,5632]{1,0:T(8,128)(2,1)} %collective-permute-done.51.refs_1_, bf16[32,5632]{1,0:T(8,128)(2,1)} %collective-permute-done.52.refs_2_, bf16[32,5632]{1,0:T(8,128)(2,1)} %collective-permute-done.53.refs_3_, ...), custom_call_target="tpu_custom_call" | custom-call | tf_op jit(solution)/shard_map/pallas_call | solution.py:463
  332.4 13.6 %fusion.92 = f32[512,5632]{1,0:T(8,128)} fusion(bf16[512,1024]{1,0:T(8,128)(2,1)S(1)} %multiply_convert_fusion.1, bf16[1024,5632]{1,0:T(8,128)(2,1)} %shard_map.206), kind=kOutput, calls=%fused_computation.205 | convolution fusion | flops 5905580032 | bytes 24117248 | tf_op jit(solution)/shard_map/dot_general | solution.py:25
  346.1 11.0 %bitcast_multiply_fusion.1 = (f32[512,2816]{1,0:T(8,128)}, f32[512,2816]{1,0:T(8,128)}, bf16[512,2816]{1,0:T(8,128)(2,1)}) fusion(f32[512,5632]{1,0:T(8,128)} %fusion.92, bf16[2816,1024]{1,0:T(8,128)(2,1)S(1)} %bitcast.134, bf16[512,1024]{1,0:T(8,128)(2,1)S(1)} %copy-done.82), kind=kOutput, calls=%fused_computation.7 | convolution fusion | flops 2972975104 | bytes 32768000 | tf_op jit(solution)/shard_map/dot_general | solution.py:29
  357.1 7.5 add_convert_fusion
  364.5 11.0 %multiply_reduce_fusion = (f32[1024]{0:T(1024)S(1)}, f32[512]{0:T(512)S(1)}, f32[512,1024]{1,0:T(8,128)S(1)}) fusion(f32[512,1024]{1,0:T(8,128)S(1)} %copy-done.77, f32[512]{0:T(512)S(1)} %fusion.76, f32[1024]{0:T(1024)S(1)} %bitcast.152, bf16[512,5632]{1,0:T(8,128)(2,1)} %add_convert_fusion, bf16[1024,5632]{1,0:T(8,128)(2,1)} %shard_map.206), kind=kOutput, calls=%fused_computation.44 | convolution fusion | flops 5908724224 | bytes 21508096 | tf_op jit(solution)/shard_map/dot_general | solution.py:29
  382.9 42.7 %shard_map.208 = (bf16[512,1024]{1,0:T(8,128)(2,1)}, bf16[512,1024]{1,0:T(8,128)(2,1)}, bf16[512,2048]{1,0:T(8,128)(2,1)}, bf16[512,2048]{1,0:T(8,128)(2,1)}, f3...) custom-call(f32[512,6144]{1,0:T(8,128)} %fusion.87.q_ref.k_ref.v_ref, ...), custom_call_target="tpu_custom_call" | custom-call | flops 60000002048 | bytes 40000000 | tf_op jit(solution)/shard_map/pallas_call | solution.py:365
  441.7 13.3 %fusion.10 = (f32[1024]{0:T(1024)S(1)}, f32[512]{0:T(512)S(1)}, f32[512,1024]{1,0:T(8,128)}) fusion(bf16[512,1024]{1,0:T(8,128)(2,1)S(1)} %copy-done.87, f32[512]{0:T(512)S(1)} %copy-done.131, f32[1024]{0:T(1024)S(1)} %bitcast.160, f32[512,1024]{1,0:T(8,128)S(1)} %fusion.74, bf16[512,6144]{1,0:T(8,128)(2,1)} %copy-done.111, bf16[1024,6144]{1,0:T(8,128)(2,1)} %shard_map.203), kind=kOutput, calls=%fused_computation.37 | convolution fusion | flops 6446643712 | bytes 24129536 | tf_op jit(solution)/shard_map/dot_general | solution.py:29
  467.5 7.8 add_convert_fusion.11
  494.9 31.8 %collective-permute-done.109 = bf16[2048,256]{1,0:T(8,128)(2,1)S(1)} collective-permute-done((bf16[2048,256]{1,0:T(8,128)(2,1)S(1)}, bf16[2048,256]{1,0:T(8,128)(2,1)S(1)}, u32[]{:S(2)}, u32[]{:S(2)}) %collective-permute-start.109) | collective-permute-done | bytes 1048608 | tf_op jit(solution)/shard_map/ppermute | solution.py:425
  530.6 12.7 %collective-permute-done.110 = bf16[4,512,128]{2,1,0:T(8,128)(2,1)S(1)} collective-permute-done((bf16[4,512,128]{2,1,0:T(8,128)(2,1)S(1)}, bf16[4,512,128]{2,1,0:T(8,128)(2,1)S(1)}, u32[]{:S(2)}, u32[]{:S(2)}) %collective-permute-start.110) | collective-permute-done | bytes 524320 | tf_op jit(solution)/shard_map/ppermute | solution.py:425
  559.5 19.4 %collective-permute-done.100 = bf16[1024,1536]{1,0:T(8,128)(2,1)} collective-permute-done((bf16[1024,1536]{1,0:T(8,128)(2,1)S(1)}, bf16[1024,1536]{1,0:T(8,128)(2,1)}, u32[]{:S(2)}, u32[]{:S(2)}) %collective-permute-start.100) | collective-permute-done | bytes 3145760 | tf_op jit(solution)/shard_map/ppermute | solution.py:425
  592.9 16.9 %collective-permute-done.127 = bf16[2816,256]{1,0:T(8,128)(2,1)} collective-permute-done((bf16[2816,256]{1,0:T(8,128)(2,1)}, bf16[2816,256]{1,0:T(8,128)(2,1)}, u32[]{:S(2)}, u32[]{:S(2)}) %collective-permute-start.127) | collective-permute-done | bytes 1441824 | tf_op jit(solution)/shard_map/ppermute | solution.py:425
  614.1 7.5 collective-permute-done.121
  635.5 14.0 %collective-permute-start.130 = (bf16[704,128]{1,0:T(8,128)(2,1)S(1)}, bf16[704,128]{1,0:T(8,128)(2,1)S(1)}, u32[]{:S(2)}, u32[]{:S(2)}) collective-permute-start(bf16[704,128]{1,0:T(8,128)(2,1)S(1)} %get-tuple-element.87), channel_id=1, source_target_pairs={{0,2},{1,3},{2,0},{3,1},{4,6},{5,7},{6,4},{7,5},{8,10},{9,11},{10,... | collective-permute-start | bytes 540680 | tf_op jit(solution)/shard_map/ppermute | solution.py:430
  649.4 14.7 %collective-permute-done.103 = bf16[256,768]{1,0:T(8,128)(2,1)S(1)} collective-permute-done((bf16[256,768]{1,0:T(8,128)(2,1)S(1)}, bf16[256,768]{1,0:T(8,128)(2,1)S(1)}, u32[]{:S(2)}, u32[]{:S(2)}) %collective-permute-start.103) | collective-permute-done | bytes 393248 | tf_op jit(solution)/shard_map/ppermute | solution.py:430
  667.1 6.9 collective-permute-done.130
  696.4 100.8 %all-reduce.6.cloned.1.call-done = f32[280,128]{1,0:T(8,128)} async-done(((f32[280,128]{1,0:T(8,128)}), f32[280,128]{1,0:T(8,128)}) %all-reduce.6.cloned.1.call-update) | async-done | bytes 143376 | tf_op jit(solution)/shard_map/psum | solution.py:615
  (691 shorter events, 373.1 us)
Async XLA Ops:
  7.2 790.0 %all-reduce.6.cloned.1.call-start = ((), (), s32[]{:S(2)}) async-start(), calls=%async_computation | async-start | bytes 286720 | tf_op jit(solution)/shard_map/psum | solution.py:615
  13.5 53.2 %collective-permute-start.3 = (bf16[256,768]{1,0:T(8,128)(2,1)S(1)}, bf16[256,768]{1,0:T(8,128)(2,1)S(1)}, u32[]{:S(2)}, u32[]{:S(2)}) collective-permute-start(bf16[256,768]{1,0:T(8,128)(2,1)S(1)} %constant_dynamic-slice_fusion.11), channel_id=1, source_target_pairs={{0,1},{1,2},{2,3},{3,0},{4,5},{5,6},{6,7},{7,4},{8,9},{9,10},{10,1... | collective-permute-start | bytes 1179656 | tf_op jit(solution)/shard_map/ppermute | solution.py:430
  13.5 54.7 %collective-permute-start.11 = (bf16[256,768]{1,0:T(8,128)(2,1)S(1)}, bf16[256,768]{1,0:T(8,128)(2,1)S(1)}, u32[]{:S(2)}, u32[]{:S(2)}) collective-permute-start(bf16[256,768]{1,0:T(8,128)(2,1)S(1)} %constant_dynamic-slice_fusion.11), channel_id=1, source_target_pairs={{0,2},{1,3},{2,0},{3,1},{4,6},{5,7},{6,4},{7,5},{8,10},{9,11},{10,... | collective-permute-start | bytes 1179656 | tf_op jit(solution)/shard_map/ppermute | solution.py:430
  24.1 42.6 %collective-permute-start.27 = (bf16[512,128]{1,0:T(8,128)(2,1)S(1)}, bf16[512,128]{1,0:T(8,128)(2,1)S(1)}, u32[]{:S(2)}, u32[]{:S(2)}) collective-permute-start(bf16[512,128]{1,0:T(8,128)(2,1)S(1)} %constant_dynamic-slice_fusion.10), channel_id=1, source_target_pairs={{0,1},{1,2},{2,3},{3,0},{4,5},{5,6},{6,7},{7,4},{8,9},{9,10},{10,1... | collective-permute-start | bytes 393224 | tf_op jit(solution)/shard_map/ppermute | solution.py:430
  261.0 43.1 %collective-permute-start.54 = (bf16[32,5632]{1,0:T(8,128)(2,1)}, bf16[32,5632]{1,0:T(8,128)(2,1)S(1)}, u32[]{:S(2)}, u32[]{:S(2)}) collective-permute-start(bf16[32,5632]{1,0:T(8,128)(2,1)} %collective-permute-done.53.refs_3_), channel_id=1, source_target_pairs={{0,4},{4,0},{8,12},{12,8},{16,20},{20,16},{24,28},{28,24},{1,5},{5... | collective-permute-start | bytes 1081352 | tf_op jit(solution)/shard_map/ppermute | solution.py:425
  261.1 45.1 %collective-permute-start.57 = (bf16[32,5632]{1,0:T(8,128)(2,1)}, bf16[32,5632]{1,0:T(8,128)(2,1)S(1)}, u32[]{:S(2)}, u32[]{:S(2)}) collective-permute-start(bf16[32,5632]{1,0:T(8,128)(2,1)} %collective-permute-done.53.refs_3_), channel_id=1, source_target_pairs={{0,16},{4,12},{8,24},{12,4},{16,0},{20,28},{24,8},{28,20},{1,17},{... | collective-permute-start | bytes 1081352 | tf_op jit(solution)/shard_map/ppermute | solution.py:425
  263.0 41.3 %collective-permute-start.56 = (bf16[32,5632]{1,0:T(8,128)(2,1)}, bf16[32,5632]{1,0:T(8,128)(2,1)S(1)}, u32[]{:S(2)}, u32[]{:S(2)}) collective-permute-start(bf16[32,5632]{1,0:T(8,128)(2,1)} %collective-permute-done.55.refs_5_), channel_id=1, source_target_pairs={{0,4},{4,0},{8,12},{12,8},{16,20},{20,16},{24,28},{28,24},{1,5},{5... | collective-permute-start | bytes 1081352 | tf_op jit(solution)/shard_map/ppermute | solution.py:425
  263.1 43.1 %collective-permute-start.62 = (bf16[32,5632]{1,0:T(8,128)(2,1)}, bf16[32,5632]{1,0:T(8,128)(2,1)S(1)}, u32[]{:S(2)}, u32[]{:S(2)}) collective-permute-start(bf16[32,5632]{1,0:T(8,128)(2,1)} %collective-permute-done.61.refs_11_), channel_id=1, source_target_pairs={{0,4},{4,0},{8,12},{12,8},{16,20},{20,16},{24,28},{28,24},{1,5},{5... | collective-permute-start | bytes 1081352 | tf_op jit(solution)/shard_map/ppermute | solution.py:425
  263.5 43.2 %collective-permute-start.64 = (bf16[32,5632]{1,0:T(8,128)(2,1)}, bf16[32,5632]{1,0:T(8,128)(2,1)S(1)}, u32[]{:S(2)}, u32[]{:S(2)}) collective-permute-start(bf16[32,5632]{1,0:T(8,128)(2,1)} %collective-permute-done.63.refs_13_), channel_id=1, source_target_pairs={{0,4},{4,0},{8,12},{12,8},{16,20},{20,16},{24,28},{28,24},{1,5},{5... | collective-permute-start | bytes 1081352 | tf_op jit(solution)/shard_map/ppermute | solution.py:425
  432.1 43.2 %collective-permute-start.117 = (bf16[1024,2816]{1,0:T(8,128)(2,1)}, bf16[1024,2816]{1,0:T(8,128)(2,1)}, u32[]{:S(2)}, u32[]{:S(2)}) collective-permute-start(bf16[1024,2816]{1,0:T(8,128)(2,1)} %convolution_convert_fusion), channel_id=1, source_target_pairs={{0,4},{4,0},{8,12},{12,8},{16,20},{20,16},{24,28},{28,24},{1,5},{5... | collective-permute-start | bytes 17301512 | tf_op jit(solution)/shard_map/ppermute | solution.py:425
  440.9 49.5 %collective-permute-start.99 = (bf16[1024,3072]{1,0:T(8,128)(2,1)}, bf16[1024,3072]{1,0:T(8,128)(2,1)}, u32[]{:S(2)}, u32[]{:S(2)}) collective-permute-start(bf16[1024,3072]{1,0:T(8,128)(2,1)} %convolution_convert_fusion.1), channel_id=1, source_target_pairs={{0,4},{4,0},{8,12},{12,8},{16,20},{20,16},{24,28},{28,24},{1,5},{5... | collective-permute-start | bytes 18874376 | tf_op jit(solution)/shard_map/ppermute | solution.py:425
  464.2 87.8 %collective-permute-start.126 = (bf16[2816,512]{1,0:T(8,128)(2,1)}, bf16[2816,512]{1,0:T(8,128)(2,1)}, u32[]{:S(2)}, u32[]{:S(2)}) collective-permute-start(bf16[2816,512]{1,0:T(8,128)(2,1)} %convolution_convert_fusion.2), channel_id=1, source_target_pairs={{0,4},{4,0},{8,12},{12,8},{16,20},{20,16},{24,28},{28,24},{1,5},{5... | collective-permute-start | bytes 8650760 | tf_op jit(solution)/shard_map/ppermute | solution.py:425
  480.7 66.4 %collective-permute-start.118 = (bf16[1024,1408]{1,0:T(8,128)(2,1)}, bf16[1024,1408]{1,0:T(8,128)(2,1)S(1)}, u32[]{:S(2)}, u32[]{:S(2)}) collective-permute-start(bf16[1024,1408]{1,0:T(8,128)(2,1)} %add_convert_fusion.4), channel_id=1, source_target_pairs={{0,8},{4,20},{8,0},{12,28},{16,24},{20,4},{24,16},{28,12},{1,9},{5... | collective-permute-start | bytes 8650760 | tf_op jit(solution)/shard_map/ppermute | solution.py:425
  483.1 43.5 %collective-permute-start.109 = (bf16[2048,256]{1,0:T(8,128)(2,1)S(1)}, bf16[2048,256]{1,0:T(8,128)(2,1)S(1)}, u32[]{:S(2)}, u32[]{:S(2)}) collective-permute-start(bf16[2048,256]{1,0:T(8,128)(2,1)S(1)} %add_convert_fusion.10), channel_id=1, source_target_pairs={{0,8},{4,20},{8,0},{12,28},{16,24},{20,4},{24,16},{28,12},{1,9},{5... | collective-permute-start | bytes 3145736 | tf_op jit(solution)/shard_map/ppermute | solution.py:425
  494.5 84.4 %collective-permute-start.100 = (bf16[1024,1536]{1,0:T(8,128)(2,1)S(1)}, bf16[1024,1536]{1,0:T(8,128)(2,1)}, u32[]{:S(2)}, u32[]{:S(2)}) collective-permute-start(bf16[1024,1536]{1,0:T(8,128)(2,1)S(1)} %add_convert_fusion.2), channel_id=1, source_target_pairs={{0,8},{4,20},{8,0},{12,28},{16,24},{20,4},{24,16},{28,12},{1,9},{5... | collective-permute-start | bytes 9437192 | tf_op jit(solution)/shard_map/ppermute | solution.py:425
  557.3 52.5 %collective-permute-start.127 = (bf16[2816,256]{1,0:T(8,128)(2,1)}, bf16[2816,256]{1,0:T(8,128)(2,1)}, u32[]{:S(2)}, u32[]{:S(2)}) collective-permute-start(bf16[2816,256]{1,0:T(8,128)(2,1)} %add_convert_fusion.7), channel_id=1, source_target_pairs={{0,8},{4,20},{8,0},{12,28},{16,24},{20,4},{24,16},{28,12},{1,9},{5... | collective-permute-start | bytes 4325384 | tf_op jit(solution)/shard_map/ppermute | solution.py:425
  558.3 118.3 %collective-permute-start.114 = (bf16[512,128]{1,0:T(8,128)(2,1)S(1)}, bf16[512,128]{1,0:T(8,128)(2,1)}, u32[]{:S(2)}, u32[]{:S(2)}) collective-permute-start(bf16[512,128]{1,0:T(8,128)(2,1)S(1)} %fusion.42), channel_id=1, source_target_pairs={{0,16},{4,12},{8,24},{12,4},{16,0},{20,28},{24,8},{28,20},{1,17},{... | collective-permute-start | bytes 393224 | tf_op jit(solution)/shard_map/ppermute | solution.py:425
  583.2 39.7 %collective-permute-start.101 = (bf16[4,256,768]{2,1,0:T(8,128)(2,1)S(1)}, bf16[4,256,768]{2,1,0:T(8,128)(2,1)S(1)}, u32[]{:S(2)}, u32[]{:S(2)}) collective-permute-start(bf16[4,256,768]{2,1,0:T(8,128)(2,1)S(1)} %constant_dynamic-slice_fusion.6), channel_id=1, source_target_pairs={{0,16},{4,12},{8,24},{12,4},{16,0},{20,28},{24,8},{28,20},{1,17},{... | collective-permute-start | bytes 4718600 | tf_op jit(solution)/shard_map/ppermute | solution.py:425
  625.9 38.3 %collective-permute-start.102 = (bf16[256,768]{1,0:T(8,128)(2,1)S(1)}, bf16[256,768]{1,0:T(8,128)(2,1)S(1)}, u32[]{:S(2)}, u32[]{:S(2)}) collective-permute-start(bf16[256,768]{1,0:T(8,128)(2,1)S(1)} %get-tuple-element.79), channel_id=1, source_target_pairs={{0,1},{1,2},{2,3},{3,0},{4,5},{5,6},{6,7},{7,4},{8,9},{9,10},{10,1... | collective-permute-start | bytes 1179656 | tf_op jit(solution)/shard_map/ppermute | solution.py:430
  635.5 38.5 %collective-permute-start.130 = (bf16[704,128]{1,0:T(8,128)(2,1)S(1)}, bf16[704,128]{1,0:T(8,128)(2,1)S(1)}, u32[]{:S(2)}, u32[]{:S(2)}) collective-permute-start(bf16[704,128]{1,0:T(8,128)(2,1)S(1)} %get-tuple-element.87), channel_id=1, source_target_pairs={{0,2},{1,3},{2,0},{3,1},{4,6},{5,7},{6,4},{7,5},{8,10},{9,11},{10,... | collective-permute-start | bytes 540680 | tf_op jit(solution)/shard_map/ppermute | solution.py:430
  677.8 121.2 %collective-permute-start.115 = (bf16[512,256]{1,0:T(8,128)(2,1)S(1)}, bf16[512,256]{1,0:T(8,128)(2,1)}, u32[]{:S(2)}, u32[]{:S(2)}) collective-permute-start(bf16[512,256]{1,0:T(8,128)(2,1)S(1)} %maximum_select_fusion.11), channel_id=1, source_target_pairs={{0,8},{4,20},{8,0},{12,28},{16,24},{20,4},{24,16},{28,12},{1,9},{5... | collective-permute-start | bytes 786440 | tf_op jit(solution)/shard_map/ppermute | solution.py:425
  684.5 117.0 %collective-permute-start.133 = (bf16[704,256]{1,0:T(8,128)(2,1)}, bf16[704,256]{1,0:T(8,128)(2,1)}, u32[]{:S(2)}, u32[]{:S(2)}) collective-permute-start(bf16[704,256]{1,0:T(8,128)(2,1)} %maximum_select_fusion.10), channel_id=1, source_target_pairs={{0,8},{4,20},{8,0},{12,28},{16,24},{20,4},{24,16},{28,12},{1,9},{5... | collective-permute-start | bytes 1081352 | tf_op jit(solution)/shard_map/ppermute | solution.py:425
  688.1 115.0 %collective-permute-start.106 = (bf16[256,1536]{1,0:T(8,128)(2,1)}, bf16[256,1536]{1,0:T(8,128)(2,1)}, u32[]{:S(2)}, u32[]{:S(2)}) collective-permute-start(bf16[256,1536]{1,0:T(8,128)(2,1)} %maximum_select_fusion.6), channel_id=1, source_target_pairs={{0,8},{4,20},{8,0},{12,28},{16,24},{20,4},{24,16},{28,12},{1,9},{5... | collective-permute-start | bytes 2359304 | tf_op jit(solution)/shard_map/ppermute | solution.py:425
  692.4 127.6 %collective-permute-start.125 = (bf16[256,2816]{1,0:T(8,128)(2,1)}, bf16[256,2816]{1,0:T(8,128)(2,1)}, u32[]{:S(2)}, u32[]{:S(2)}) collective-permute-start(bf16[256,2816]{1,0:T(8,128)(2,1)} %maximum_select_fusion.3), channel_id=1, source_target_pairs={{0,4},{4,0},{8,12},{12,8},{16,20},{20,16},{24,28},{28,24},{1,5},{5... | collective-permute-start | bytes 4325384 | tf_op jit(solution)/shard_map/ppermute | solution.py:425
  (255 other events, 3363.6 us)
Sparse Core Ops, SparseCore 0:
  676.7 120.4 all-reduce.5

commit v2 on v1

--- a/solution.py
+++ b/solution.py
@@ -1,4 +1,5 @@
 import functools
+import math
 
 import jax
 import jax.numpy as jnp
@@ -55,7 +56,7 @@
 
 
 def fill_sums(gamma_ref, sums_ref):
-    lane = lax.broadcasted_iota(jnp.int32, (HEADS, CHUNK), 1)
+    lane = lax.broadcasted_iota(jnp.int32, (gamma_ref.shape[0], CHUNK), 1)
     for c in range(gamma_ref.shape[1] // CHUNK):
         span = pl.ds(c * CHUNK, CHUNK)
         total = gamma_ref[:, span]
@@ -63,7 +64,7 @@
         while step < CHUNK:
             total = total + jnp.where(lane >= step, pltpu.roll(total, step, 1), 0.0)
             step *= 2
-        for i in range(HEADS):
+        for i in range(gamma_ref.shape[0]):
             sums_ref[i, :, span] = total[i : i + 1]
 
 
@@ -182,40 +183,37 @@
     return pl.BlockSpec((1, 1, rows), lambda h: (h, 0, 0))
 
 
-def mixer(projected, seg, segrow, gamma, beta, taps, gain):
-    rows = projected.shape[0]
-    chunks = rows // CHUNK
+def columns(rows, width, at):
+    return pl.BlockSpec((rows, width), lambda h: (0, at + h))
+
+
+def mixer(projected, at, seg, segrow, gamma, beta, taps, gain):
+    rows, held = projected.shape[0], projected.shape[1] // (2 * DK + 2 * DV)
+    chunks, heads = rows // CHUNK, gamma.shape[0]
     return pl.pallas_call(
         mix_kernel,
-        grid=(HEADS,),
+        grid=(heads,),
         in_specs=[
-            pl.BlockSpec((rows, DK), lambda h: (0, h)),
-            pl.BlockSpec((rows, DK), lambda h: (0, HEADS + h)),
-            pl.BlockSpec((rows, DV), lambda h: (0, HEADS + h)),
-            pl.BlockSpec((rows, DV), lambda h: (0, 2 * HEADS + h)),
-            whole((rows, CHUNK)), whole((8, rows)), whole((HEADS, rows)), per_head(rows),
-            pl.BlockSpec((CONV, DK), lambda h: (0, h)),
-            pl.BlockSpec((CONV, DK), lambda h: (0, HEADS + h)),
-            pl.BlockSpec((CONV, DV), lambda h: (0, HEADS + h)),
+            columns(rows, DK, at), columns(rows, DK, held + at), columns(rows, DV, held + at), columns(rows, DV, 2 * held + at),
+            whole((rows, CHUNK)), whole((8, rows)), whole((heads, rows)), per_head(rows),
+            columns(CONV, DK, at), columns(CONV, DK, held + at), columns(CONV, DV, held + at),
             whole((1, DV)),
         ],
         out_specs=[
-            pl.BlockSpec((rows, DV), lambda h: (0, h)),
-            pl.BlockSpec((rows, DV), lambda h: (0, h)),
-            pl.BlockSpec((rows, DV), lambda h: (0, h)),
+            columns(rows, DV, 0), columns(rows, DV, 0), columns(rows, DV, 0),
             pl.BlockSpec((1, chunks, CHUNK, CHUNK), lambda h: (h, 0, 0, 0)),
             pl.BlockSpec((1, chunks, DK, DV), lambda h: (h, 0, 0, 0)),
         ],
         out_shape=[
-            jax.ShapeDtypeStruct((rows, VALS), BF),
-            jax.ShapeDtypeStruct((rows, VALS), F32),
-            jax.ShapeDtypeStruct((rows, VALS), BF),
-            jax.ShapeDtypeStruct((HEADS, chunks, CHUNK, CHUNK), BF),
-            jax.ShapeDtypeStruct((HEADS, chunks, DK, DV), BF),
+            jax.ShapeDtypeStruct((rows, heads * DV), BF),
+            jax.ShapeDtypeStruct((rows, heads * DV), F32),
+            jax.ShapeDtypeStruct((rows, heads * DV), BF),
+            jax.ShapeDtypeStruct((heads, chunks, CHUNK, CHUNK), BF),
+            jax.ShapeDtypeStruct((heads, chunks, DK, DV), BF),
         ],
-        scratch_shapes=[pltpu.VMEM((CONV - 1, rows, CHUNK), F32), pltpu.VMEM((HEADS, 1, rows), F32)],
-        compiler_params=pltpu.CompilerParams(vmem_limit_bytes=48 * 2**20),
-        cost_estimate=pl.CostEstimate(flops=int(3e10), bytes_accessed=int(3e7), transcendentals=0),
+        scratch_shapes=[pltpu.VMEM((CONV - 1, rows, CHUNK), F32), pltpu.VMEM((heads, 1, rows), F32)],
+        compiler_params=pltpu.CompilerParams(vmem_limit_bytes=32 * 2**20),
+        cost_estimate=pl.CostEstimate(flops=heads * int(5e9), bytes_accessed=heads * int(4e6), transcendentals=0),
     )(projected, projected, projected, projected, seg, segrow, gamma, beta[:, None], taps, taps, taps, gain)
 
 
@@ -344,12 +342,13 @@
     spread(dk * kslope, k_ref, tapk_ref, dk_ref, dtapk_ref)
     spread(jnp.concatenate(dvs, axis=0) * vslope, v_ref, tapv_ref, dv_ref, dtapv_ref)
 
-    @pl.when(h == HEADS - 1)
+    @pl.when(h == pl.num_programs(0) - 1)
     def _():
-        lane = lax.broadcasted_iota(jnp.int32, (HEADS, CHUNK), 1)
+        heads = gamma_ref.shape[0]
+        lane = lax.broadcasted_iota(jnp.int32, (heads, CHUNK), 1)
         for c in range(chunks):
             span = pl.ds(c * CHUNK, CHUNK)
-            total = jnp.concatenate([lift_ref[i, :, span] for i in range(HEADS)], axis=0)
+            total = jnp.concatenate([lift_ref[i, :, span] for i in range(heads)], axis=0)
             step = 1
             while step < CHUNK:
                 total = total + jnp.where(lane < CHUNK - step, pltpu.roll(total, CHUNK - step, 1), 0.0)
@@ -357,48 +356,113 @@
             dgamma_ref[:, span] = total
 
 
-def mixer_back(projected, seg, segrow, gamma, beta, taps, gain, out, fresh, inv, state, back):
-    rows = projected.shape[0]
-    chunks = rows // CHUNK
-    cols = lambda width, at: pl.BlockSpec((rows, width), lambda h: (0, at + h))
-    tap = lambda width, at: pl.BlockSpec((CONV, width), lambda h: (0, at + h))
+def mixer_back(projected, at, seg, segrow, gamma, beta, taps, gain, out, fresh, inv, state, back, back_at):
+    rows, held = projected.shape[0], projected.shape[1] // (2 * DK + 2 * DV)
+    chunks, heads = rows // CHUNK, gamma.shape[0]
     return pl.pallas_call(
         back_kernel,
-        grid=(HEADS,),
+        grid=(heads,),
         in_specs=[
-            cols(DK, 0), cols(DK, HEADS), cols(DV, HEADS), cols(DV, 2 * HEADS),
-            whole((rows, CHUNK)), whole((8, rows)), whole((HEADS, rows)), per_head(rows),
-            tap(DK, 0), tap(DK, HEADS), tap(DV, HEADS), whole((1, DV)),
-            cols(DV, 0), cols(DV, 0),
+            columns(rows, DK, at), columns(rows, DK, held + at), columns(rows, DV, held + at), columns(rows, DV, 2 * held + at),
+            whole((rows, CHUNK)), whole((8, rows)), whole((heads, rows)), per_head(rows),
+            columns(CONV, DK, at), columns(CONV, DK, held + at), columns(CONV, DV, held + at),
+            whole((1, DV)),
+            columns(rows, DV, 0), columns(rows, DV, 0),
             pl.BlockSpec((1, chunks, CHUNK, CHUNK), lambda h: (h, 0, 0, 0)),
             pl.BlockSpec((1, chunks, DK, DV), lambda h: (h, 0, 0, 0)),
-            cols(DV, 0),
+            columns(rows, DV, back_at),
         ],
         out_specs=[
-            cols(DK, 0), cols(DK, 0), cols(DV, 0), cols(DV, 0),
-            tap(DK, 0), tap(DK, 0), tap(DV, 0),
-            whole((1, DV)), whole((HEADS, rows)), per_head(rows),
+            columns(rows, DK, 0), columns(rows, DK, 0), columns(rows, DV, 0), columns(rows, DV, 0),
+            columns(CONV, DK, 0), columns(CONV, DK, 0), columns(CONV, DV, 0),
+            whole((1, DV)), whole((heads, rows)), per_head(rows),
         ],
         out_shape=[
-            jax.ShapeDtypeStruct((rows, KEYS), BF),
-            jax.ShapeDtypeStruct((rows, KEYS), BF),
-            jax.ShapeDtypeStruct((rows, VALS), BF),
-            jax.ShapeDtypeStruct((rows, VALS), BF),
-            jax.ShapeDtypeStruct((CONV, KEYS), F32),
-            jax.ShapeDtypeStruct((CONV, KEYS), F32),
-            jax.ShapeDtypeStruct((CONV, VALS), F32),
+            jax.ShapeDtypeStruct((rows, heads * DK), BF),
+            jax.ShapeDtypeStruct((rows, heads * DK), BF),
+            jax.ShapeDtypeStruct((rows, heads * DV), BF),
+            jax.ShapeDtypeStruct((rows, heads * DV), BF),
+            jax.ShapeDtypeStruct((CONV, heads * DK), F32),
+            jax.ShapeDtypeStruct((CONV, heads * DK), F32),
+            jax.ShapeDtypeStruct((CONV, heads * DV), F32),
             jax.ShapeDtypeStruct((1, DV), F32),
-            jax.ShapeDtypeStruct((HEADS, rows), F32),
-            jax.ShapeDtypeStruct((HEADS, 1, rows), F32),
+            jax.ShapeDtypeStruct((heads, rows), F32),
+            jax.ShapeDtypeStruct((heads, 1, rows), F32),
         ],
         scratch_shapes=[
             pltpu.VMEM((CONV - 1, rows, CHUNK), F32),
-            pltpu.VMEM((HEADS, 1, rows), F32),
-            pltpu.VMEM((HEADS, 1, rows), F32),
+            pltpu.VMEM((heads, 1, rows), F32),
+            pltpu.VMEM((heads, 1, rows), F32),
         ],
-        compiler_params=pltpu.CompilerParams(vmem_limit_bytes=56 * 2**20),
-        cost_estimate=pl.CostEstimate(flops=int(6e10), bytes_accessed=int(4e7), transcendentals=0),
+        compiler_params=pltpu.CompilerParams(vmem_limit_bytes=32 * 2**20),
+        cost_estimate=pl.CostEstimate(flops=heads * int(6e9), bytes_accessed=heads * int(5e6), transcendentals=0),
     )(projected, projected, projected, projected, seg, segrow, gamma, beta[:, None], taps, taps, taps, gain, out, fresh, inv, state, back)
+
+
+TILE = 256
+
+
+def ffn_in_kernel(x_ref, gate_w_ref, up_w_ref, gate_ref, up_ref, inner_ref):
+    gate, up = dot_nn(x_ref[...], gate_w_ref[...]), dot_nn(x_ref[...], up_w_ref[...])
+    gate_ref[...] = gate.astype(BF)
+    up_ref[...] = up.astype(BF)
+    inner_ref[...] = (gate * sigmoid(gate) * up).astype(BF)
+
+
+def ffn_in(x, weight):
+    rows, depth = x.shape
+    width = weight.shape[1] // 2
+    tiles = width // TILE
+    return pl.pallas_call(
+        ffn_in_kernel,
+        grid=(tiles,),
+        in_specs=[whole((rows, depth)), columns(depth, TILE, 0), columns(depth, TILE, tiles)],
+        out_specs=[columns(rows, TILE, 0)] * 3,
+        out_shape=[jax.ShapeDtypeStruct((rows, width), BF)] * 3,
+        compiler_params=pltpu.CompilerParams(vmem_limit_bytes=32 * 2**20),
+        cost_estimate=pl.CostEstimate(flops=4 * rows * depth * width, bytes_accessed=4 * depth * width, transcendentals=0),
+    )(x, weight, weight)
+
+
+def ffn_out_kernel(c_ref, gate_ref, up_ref, inner_ref, down_w_ref, gate_w_ref, up_w_ref, back_ref, down_ref, x_back_ref):
+    @pl.when(pl.program_id(0) == 0)
+    def _():
+        down_ref[...] = jnp.zeros_like(down_ref)
+        x_back_ref[...] = jnp.zeros_like(x_back_ref)
+
+    inner_back = dot_nt(c_ref[...], down_w_ref[...])
+    gate, up = gate_ref[...].astype(F32), up_ref[...].astype(F32)
+    s = sigmoid(gate)
+    gate_back = (inner_back * up * (s * (1.0 + gate * (1.0 - s)))).astype(BF)
+    up_back = (inner_back * (gate * s)).astype(BF)
+    back_ref[0] = gate_back
+    back_ref[1] = up_back
+    down_ref[...] += dot_nn(inner_ref[...], down_w_ref[...])
+    x_back_ref[...] += dot_nt(gate_back, gate_w_ref[...]) + dot_nt(up_back, up_w_ref[...])
+
+
+def ffn_out(cotangent, gate, up, inner, down_w, gate_up_w):
+    rows, width = gate.shape
+    depth = cotangent.shape[1]
+    tiles = width // TILE
+    return pl.pallas_call(
+        ffn_out_kernel,
+        grid=(tiles,),
+        in_specs=[
+            whole((rows, depth)),
+            columns(rows, TILE, 0), columns(rows, TILE, 0), columns(rows, TILE, 0),
+            pl.BlockSpec((TILE, depth), lambda h: (h, 0)),
+            columns(depth, TILE, 0), columns(depth, TILE, tiles),
+        ],
+        out_specs=[pl.BlockSpec((2, rows, TILE), lambda h: (0, 0, h)), whole((rows, depth)), whole((rows, depth))],
+        out_shape=[
+            jax.ShapeDtypeStruct((2, rows, width), BF),
+            jax.ShapeDtypeStruct((rows, depth), F32),
+            jax.ShapeDtypeStruct((rows, depth), F32),
+        ],
+        compiler_params=pltpu.CompilerParams(vmem_limit_bytes=32 * 2**20),
+        cost_estimate=pl.CostEstimate(flops=8 * rows * depth * width, bytes_accessed=6 * depth * width, transcendentals=0),
+    )(cotangent, gate, up, inner, down_w, gate_up_w, gate_up_w)
 
 
 SHIFTS = (1, 2, 3)
@@ -430,44 +494,71 @@
     return lax.ppermute(value, "shard", [(i, (i + by) % count) for i in range(count)])
 
 
-def assemble_kernel(along, size, rows, at_ref, *refs):
-    own, pieces, whole_ref = refs[0], refs[1:-1], refs[-1]
-    whole_ref[pl.ds(pl.multiple_of(at_ref[0] * rows, 16), rows), :] = own[...]
-    for n, piece in enumerate(pieces):
-        block, part = at_ref[1 + 2 * n], at_ref[2 + 2 * n]
-        if along == 0:
-            whole_ref[pl.ds(pl.multiple_of(block * rows + part * size, 16), size), :] = piece[...]
-        else:
-            whole_ref[pl.ds(pl.multiple_of(block * rows, 16), rows), pl.ds(pl.multiple_of(part * size, 128), size)] = piece[...]
-
-
-def gather(weight, along):
-    core, a, b = place()
-    z = lax.axis_index("shard")
-    count = lax.axis_size("shard")
-    size = weight.shape[along] // 8
-    rows = weight.shape[0]
-    part = core * 4 + a * 2 + b
-    other = (1 - core) * 4 + b * 2 + a
-    mine = lax.dynamic_slice_in_dim(weight, part * size, size, along)
-    at, pieces = [z], []
-    for by in range(1, count):
-        block = (z - by) % count
-        here = shift(mine, by)
-        token = here
-        first = hop(here, "first")
-        found = [(here, 0), (first, 2), (hop(here, "second"), 1), (hop(first, "second"), 3)]
-        for piece, flip in found:
-            pieces += [piece, hop(piece, "core")]
-            at += [block, part ^ flip, block, other ^ flip]
-    full = pl.pallas_call(
-        functools.partial(assemble_kernel, along, size, rows),
-        in_specs=[pl.BlockSpec(memory_space=pltpu.SMEM)] + [pl.BlockSpec(memory_space=pltpu.VMEM)] * (len(pieces) + 1),
-        out_specs=pl.BlockSpec(memory_space=pltpu.VMEM),
-        compiler_params=pltpu.CompilerParams(vmem_limit_bytes=48 * 2**20),
-        out_shape=jax.ShapeDtypeStruct((rows * count, weight.shape[1]), BF),
-    )(jnp.stack(at).astype(jnp.int32), weight, *pieces)
-    return full, token
+def after(value, *others):
+    if not others:
+        return value
+    return lax.optimization_barrier((value,) + others)[0]
+
+
+def assemble_kernel(along, size, rows, at_ref, own_ref, *refs):
+    pieces, whole_ref = refs[:-1], refs[-1]
+    whole_ref[pl.ds(pl.multiple_of(at_ref[0] * rows, 16), rows), :] = own_ref[...]
+    n = 1
+    for piece in pieces:
+        for slot in range(piece.shape[0]):
+            block, part = at_ref[n], at_ref[n + 1]
+            n += 2
+            if along == 0:
+                whole_ref[pl.ds(pl.multiple_of(block * rows + part * size, 16), size), :] = piece[slot]
+            else:
+                whole_ref[pl.ds(pl.multiple_of(block * rows, 16), rows), pl.ds(pl.multiple_of(part * size, 128), size)] = piece[slot]
+
+
+class Gather:
+    def __init__(self, weight, along):
+        self.weight, self.along = weight, along
+        self.size = weight.shape[along] // 8
+
+    def deep(self, *tokens):
+        core, a, b = place()
+        mine = lax.dynamic_slice_in_dim(self.weight, (core * 4 + a * 2 + b) * self.size, self.size, self.along)
+        mine = after(mine, *tokens)
+        self.raw = [shift(mine, by) for by in range(1, lax.axis_size("shard"))]
+
+    def first(self, *tokens):
+        count = len(self.raw)
+        raw = lax.optimization_barrier(tuple(self.raw) + tokens)[:count]
+        self.here = jnp.stack(raw)
+        self.come = hop(self.here, "first")
+
+    def second(self, *tokens):
+        self.pair = jnp.concatenate([self.here, after(self.come, *tokens)])
+        self.others = hop(self.pair, "second")
+        self.pair_core = hop(self.pair, "core")
+
+    def core(self, *tokens):
+        self.others_in = after(self.others, *tokens)
+        self.others_core = hop(self.others_in, "core")
+
+    def full(self, *tokens):
+        core, a, b = place()
+        z, count = lax.axis_index("shard"), lax.axis_size("shard")
+        part, other = core * 4 + a * 2 + b, (1 - core) * 4 + b * 2 + a
+        blocks = [(z - by) % count for by in range(1, count)]
+        at = [z]
+        for home, flips in ((part, (0, 2)), (part, (1, 3)), (other, (0, 2)), (other, (1, 3))):
+            for flip in flips:
+                for block in blocks:
+                    at += [block, home ^ flip]
+        rows, width = self.weight.shape
+        pieces = [self.pair, self.others_in, self.pair_core, after(self.others_core, *tokens)]
+        return pl.pallas_call(
+            functools.partial(assemble_kernel, self.along, self.size, rows),
+            in_specs=[pl.BlockSpec(memory_space=pltpu.SMEM)] + [pl.BlockSpec(memory_space=pltpu.VMEM)] * 5,
+            out_specs=pl.BlockSpec(memory_space=pltpu.VMEM),
+            compiler_params=pltpu.CompilerParams(vmem_limit_bytes=48 * 2**20),
+            out_shape=jax.ShapeDtypeStruct((rows * count, width), BF),
+        )(jnp.stack(at).astype(jnp.int32), self.weight, *pieces)
 
 
 def pick(value, at, size, axis):
@@ -478,66 +569,202 @@
     return jnp.where(bit == 0, jnp.concatenate([mine, theirs], axis), jnp.concatenate([theirs, mine], axis))
 
 
-def reduce_grad(left, right):
+class Total:
+    def __init__(self, left, right):
+        self.left, self.right = left, right
+        self.count = lax.axis_size("shard")
+        self.rows = left.shape[1] // self.count
+        self.quarter = right.size // right.shape[-2] // 4
+
+    def core(self, *tokens):
+        core, a, b = place()
+        half = 2 * self.quarter
+        right = after(self.right, *tokens) if tokens else self.right
+        if right.ndim == 3:
+            self.own, other = (pick(right, n, 1, 0)[0] for n in (core, 1 - core))
+        else:
+            self.own, other = (pick(right, n, half, 1) for n in (core, 1 - core))
+        self.given = dot_tn(self.left, other).astype(BF)
+        self.got = hop(self.given, "core")
+        return self.got
+
+    def first(self, *tokens):
+        core, a, b = place()
+        self.got = after(self.got, *tokens)
+        sent = dot_tn(self.left, pick(self.own, 1 - a, self.quarter, 1)) + pick(self.got, 1 - a, self.quarter, 1).astype(F32)
+        self.sent = sent.astype(BF)
+        self.got_first = hop(self.sent, "first")
+
+    def second(self, *tokens):
+        core, a, b = place()
+        got_first = after(self.got_first, *tokens)
+        kept = dot_tn(self.left, pick(self.own, a, self.quarter, 1)) + pick(self.got, a, self.quarter, 1).astype(F32)
+        kept = (kept + got_first.astype(F32)).astype(BF).reshape(self.count, self.rows, self.quarter)
+        self.axis = 2 if self.quarter % 256 == 0 else 1
+        size = kept.shape[self.axis] // 2
+        self.passed = pick(kept, 1 - b, size, self.axis)
+        self.mine = pick(kept, b, size, self.axis)
+        self.got_second = hop(self.passed, "second")
+
+    def deep(self, *tokens):
+        z = lax.axis_index("shard")
+        kept = (self.mine.astype(F32) + after(self.got_second, *tokens).astype(F32)).astype(BF)
+        extra = 8
+        while extra < lax.axis_size("rep"):
+            kept = (kept.astype(F32) + hop(kept, extra).astype(F32)).astype(BF)
+            extra *= 2
+        self.kept = kept
+        self.raw = [shift(pick(kept, (z + by) % self.count, 1, 0)[0], by) for by in range(1, self.count)]
+
+    def finish(self, *tokens):
+        total = pick(self.kept, lax.axis_index("shard"), 1, 0)[0].astype(F32)
+        for piece in lax.optimization_barrier(tuple(self.raw) + tokens)[: len(self.raw)]:
+            total = total + piece.astype(F32)
+        self.done = total.astype(BF)
+
+
+def final_kernel(copies, at_ref, *refs):
+    pieces, outs = refs[:8], refs[8:]
+    n = 0
+    for piece in pieces:
+        for start, size, width, out, moving, fixed in copies:
+            block = piece[start : start + size, :width].astype(F32)
+            if moving == "both":
+                rows = pl.ds(pl.multiple_of(at_ref[n] * size, 8), size)
+                outs[out][rows, pl.ds(pl.multiple_of(at_ref[n + 1] * 128, 128), width)] = block
+                n += 2
+            else:
+                outs[out][:, pl.ds(pl.multiple_of(at_ref[n] * 128, 128), width)] = block
+                n += 1
+
+
+class Spread:
+    def __init__(self, done):
+        self.done = done
+        self.theirs = hop(done, "second")
+
+    def first(self, *tokens):
+        self.pair = jnp.stack([self.done, after(self.theirs, *tokens)])
+        self.others = hop(self.pair, "first")
+
+    def core(self, *tokens):
+        self.four = jnp.concatenate([self.pair, after(self.others, *tokens)])
+        self.over = hop(self.four, "core")
+
+    def parts(self, *tokens):
+        over = after(self.over, *tokens)
+        return [self.four[n] for n in range(4)] + [over[n] for n in range(4)]
+
+
+def part_numbers():
     core, a, b = place()
-    z = lax.axis_index("shard")
-    count = lax.axis_size("shard")
-    columns = right.shape[1]
-    half, quarter = columns // 2, columns // 4
-    rows = left.shape[1] // count
-    got = hop(dot_tn(left, pick(right, 1 - core, half, 1)).astype(BF), "core")
-    own = pick(right, core, half, 1)
-    sent = dot_tn(left, pick(own, 1 - a, quarter, 1)) + pick(got, 1 - a, quarter, 1).astype(F32)
-    got_first = hop(sent.astype(BF), "first")
-    kept = dot_tn(left, pick(own, a, quarter, 1)) + pick(got, a, quarter, 1).astype(F32) + got_first.astype(F32)
-    kept = kept.astype(BF).reshape(count, rows, quarter)
-    axis = 2 if quarter % 256 == 0 else 1
-    size = kept.shape[axis] // 2
-    kept = (pick(kept, b, size, axis).astype(F32) + hop(pick(kept, 1 - b, size, axis), "second").astype(F32)).astype(BF)
-    extra = 8
-    while extra < lax.axis_size("rep"):
-        kept = (kept.astype(F32) + hop(kept, extra).astype(F32)).astype(BF)
-        extra *= 2
-    total = pick(kept, z, 1, 0)[0].astype(F32)
-    for by in range(1, count):
-        total = total + shift(pick(kept, (z + by) % count, 1, 0)[0], by).astype(F32)
-    done = total.astype(BF)
-    done = join(b, done, hop(done, "second"), axis - 1)
-    done = join(a, done, hop(done, "first"), 1)
-    return join(core, done, hop(done, "core"), 1).astype(F32)
+    home, away = core * 4 + a * 2 + b, (1 - core) * 4 + b * 2 + a
+    return [home ^ n for n in range(4)] + [away ^ n for n in range(4)]
+
+
+def finish_totals(pieces, copies, at, shapes):
+    return pl.pallas_call(
+        functools.partial(final_kernel, copies),
+        in_specs=[pl.BlockSpec(memory_space=pltpu.SMEM)] + [pl.BlockSpec(memory_space=pltpu.VMEM)] * 8,
+        out_specs=[pl.BlockSpec(memory_space=pltpu.VMEM)] * len(shapes),
+        compiler_params=pltpu.CompilerParams(vmem_limit_bytes=48 * 2**20),
+        out_shape=[jax.ShapeDtypeStruct(s, F32) for s in shapes],
+    )(jnp.stack(at).astype(jnp.int32), *pieces)
 
 
 def rms_scale(values, gain):
     return values * lax.rsqrt(jnp.mean(values * values, axis=-1, keepdims=True) + epsilon) * gain
 
 
-def swiglu(gate_up):
-    return jax.nn.silu(gate_up[..., :FF]) * gate_up[..., FF:]
-
-
-def after(value, *others):
-    return lax.optimization_barrier((value,) + others)[0]
+def as_rows(x, count):
+    flat = x.astype(F32).reshape(count, -1)
+    return jnp.pad(flat, ((0, 0), (0, -flat.shape[1] % 1024))).reshape(count, -1, 128)
+
+
+def from_rows(rows, shapes):
+    found, start = [], 0
+    for shape in shapes:
+        size = math.prod(shape)
+        deep = -(-size // 1024) * 8
+        piece = rows[:, start : start + deep].reshape(rows.shape[0], -1)[:, :size]
+        found.append(piece.reshape((rows.shape[0],) + shape))
+        start += deep
+    return found
 
 
 def share_small(arrays):
     count = lax.axis_size("shard")
     z = lax.axis_index("shard")
-    flat = jnp.concatenate([x.astype(F32).reshape(-1) for x in arrays])
-    flat = jnp.pad(flat, (0, -flat.shape[0] % 1024)).reshape(1, -1, 128)
+    flat = jnp.concatenate([as_rows(x, 1) for x in arrays], axis=1)
     every = jnp.zeros((count,) + flat.shape[1:], F32)
     every = lax.dynamic_update_slice_in_dim(every, flat, z, 0)
     for by in range(1, count):
         every = lax.dynamic_update_slice_in_dim(every, shift(flat, by), (z - by) % count, 0)
-    every = every.reshape(count, -1)
-    found, start = [], 0
-    for x in arrays:
-        found.append(every[:, start : start + x.size].reshape((count,) + x.shape))
-        start += x.size
-    return found
+    return from_rows(every, [x.shape for x in arrays])
+
+
+class Small:
+    def __init__(self, arrays):
+        self.shapes = [x.shape[1:] for x in arrays]
+        count, z = lax.axis_size("shard"), lax.axis_index("shard")
+        flat = jnp.concatenate([as_rows(x, count) for x in arrays], axis=1)
+        self.total = pick(flat, z, 1, 0)
+        self.raw = [shift(pick(flat, (z + by) % count, 1, 0), by) for by in range(1, count)]
+        self.step = 1
+
+    def add(self, *tokens):
+        for piece in lax.optimization_barrier(tuple(self.raw) + tokens)[: len(self.raw)]:
+            self.total = self.total + piece
+        if self.step < lax.axis_size("rep"):
+            self.raw = [hop(self.total, self.step)]
+            self.step *= 2
+        else:
+            self.raw = []
+
+    def finish(self):
+        while self.raw:
+            self.add()
+        return [x[0] for x in from_rows(self.total, self.shapes)]
 
 
 def beside(blocks):
     return jnp.concatenate(list(blocks), axis=-1)
+
+
+def parted(x):
+    count = lax.axis_size("shard")
+    return jnp.moveaxis(x.reshape(x.shape[:-1] + (count, -1)), -2, 0)
+
+
+GROUPS = 2
+STEPS = 4
+
+
+def group_columns(x, g):
+    wide, deep = KEYS // GROUPS, VALS // GROUPS
+    cuts = [x[:, n * KEYS + g * wide : n * KEYS + (g + 1) * wide] for n in (0, 1)]
+    start = 2 * KEYS
+    while start < x.shape[1]:
+        cuts.append(x[:, start + g * deep : start + (g + 1) * deep])
+        start += VALS
+    return jnp.concatenate(cuts, axis=1)
+
+
+def mix_final_kernel(blocks, at_ref, *refs):
+    for n, piece in enumerate(refs[:-1]):
+        for m in range(blocks):
+            to = pl.ds(pl.multiple_of(at_ref[n * blocks + m] * 128, 128), 128)
+            refs[-1][:, to] = piece[:, m * 128 : (m + 1) * 128].astype(F32)
+
+
+def finish_mix(pieces, blocks, at, shape):
+    return pl.pallas_call(
+        functools.partial(mix_final_kernel, blocks),
+        in_specs=[pl.BlockSpec(memory_space=pltpu.SMEM)] + [pl.BlockSpec(memory_space=pltpu.VMEM)] * len(pieces),
+        out_specs=pl.BlockSpec(memory_space=pltpu.VMEM),
+        compiler_params=pltpu.CompilerParams(vmem_limit_bytes=48 * 2**20),
+        out_shape=jax.ShapeDtypeStruct(shape, F32),
+    )(jnp.stack(at).astype(jnp.int32), *pieces)
 
 
 def body(
@@ -555,79 +782,205 @@
     cotangent,
 ):
     rows = hidden_in.shape[0]
-    z = lax.axis_index("shard")
     small = share_small([norm_gains, decay_params, conv_weight, out_gain[None], w_decay])
     gains, rates, taps, gain_row = (beside(x) for x in small[:4])
     decay_full = small[4].reshape(-1, 2 * HEADS).astype(BF)
-    mix_in, token = gather(w_mix_in, 1)
-    mix_out, token = gather(after(w_mix_out, token), 1)
-    gate_up_full, token = gather(after(w_gate_up, token), 0)
-    down_full, token = gather(after(w_down, token), 1)
+
+    ga, gb = (Gather(group_columns(w_mix_in, g), 1) for g in range(GROUPS))
+    go, gu, gd = Gather(w_mix_out, 1), Gather(w_gate_up, 0), Gather(w_down, 1)
+    ga.deep()
+    ga.first()
+    ga.second()
+    ga.core()
+    gb.deep(ga.others)
 
     hidden = hidden_in.astype(F32)
     normed_one_f, norm_one_pull = jax.vjp(rms_scale, hidden, gains[0])
     normed_one = normed_one_f.astype(BF)
-    projected = dot_nn(normed_one, mix_in)
     logits = dot_nt(decay_full.T, normed_one)
     rate, bias = jnp.exp(rates[0])[:, None], rates[1][:, None]
     gamma = -rate * jax.nn.softplus(logits[:HEADS] + bias)
     beta = jax.nn.sigmoid(logits[HEADS:])
     seg = jnp.broadcast_to(segment_ids[:, None], (rows, CHUNK))
     segrow = jnp.broadcast_to(segment_ids[None], (8, rows))
-    mixed_out, out, fresh, inv, state = mixer(projected, seg, segrow, gamma, beta, taps, gain_row)
+    tap_groups = [group_columns(taps, g) for g in range(GROUPS)]
+    heads = HEADS // STEPS
+
+    mix_in = [ga.full(), None]
+    gb.first(mix_in[0])
+    projected = [dot_nn(normed_one, mix_in[0]), None]
+    gb.second(projected[0])
+    go.deep(projected[0], *gb.raw)
+    kept = []
+
+    def mix(n, *tokens):
+        g, at = n * GROUPS // STEPS, n % (STEPS // GROUPS) * heads
+        span = slice(n * heads, (n + 1) * heads)
+        gate = after(gamma[span], *tokens) if tokens else gamma[span]
+        kept.append(mixer(projected[g], at, seg, segrow, gate, beta[span], tap_groups[g], gain_row))
+        return kept[-1][0]
+
+    done = mix(0)
+    gb.core(done)
+    gu.deep(done, *go.raw)
+    done = mix(1)
+    mix_in[1] = gb.full(done)
+    go.first(done)
+    projected[1] = dot_nn(after(normed_one, done), mix_in[1])
+    go.second(projected[1])
+    gu.first(projected[1])
+    gd.deep(projected[1], *gu.raw)
+    done = mix(2, gu.here, go.pair)
+    gu.second(done)
+    go.core(done)
+    done = mix(3, gu.pair, *gd.raw)
+    gd.first(done)
+    mix_out = go.full()
+    mixed_out = jnp.concatenate([x[0] for x in kept], axis=1)
     residual = hidden + dot_nn(mixed_out, mix_out)
     normed_two_f, norm_two_pull = jax.vjp(rms_scale, residual, gains[1])
     normed_two = normed_two_f.astype(BF)
-    gate_up = dot_nn(normed_two, gate_up_full)
-    inner_f, inner_pull = jax.vjp(swiglu, gate_up)
-    inner = inner_f.astype(BF)
-    result = (residual + dot_nn(inner, down_full)).astype(BF)
-    inner_back = dot_nt(cotangent, down_full)
-    (gate_up_grad,) = inner_pull(inner_back)
-    gate_up_back = gate_up_grad.astype(BF)
-    grad_down = reduce_grad(inner, cotangent)
-    grad_gate_up = reduce_grad(normed_two, gate_up_back)
-    normed_two_back = dot_nt(gate_up_back, gate_up_full)
-    residual_part, gain_two = norm_two_pull(normed_two_back)
+    gu.core(normed_two)
+    gate_up_full = gu.full()
+    gd.second(gate_up_full)
+    gate, up, inner = ffn_in(after(normed_two, gd.pair), gate_up_full)
+    gd.core(inner)
+    down_full = gd.full()
+    t_down = Total(inner, cotangent)
+    t_down.core()
+    gate_up_back, down, normed_two_back = ffn_out(
+        after(cotangent, t_down.given), gate, up, inner, down_full, gate_up_full
+    )
+    t_gu = Total(normed_two, gate_up_back)
+    t_gu.core()
+    t_down.first(t_gu.given)
+    result = (residual + down).astype(BF)
+    residual_part, gain_two = norm_two_pull(after(normed_two_back, t_down.sent))
+    t_gu.first(gain_two)
     residual_back = cotangent.astype(F32) + residual_part
-    branch_back = residual_back.astype(BF)
+    branch_back = after(residual_back.astype(BF), t_gu.sent)
+    t_out = Total(mixed_out, branch_back)
+    t_out.core()
     mixed_back = dot_nt(branch_back, mix_out)
-    grad_mix_out = reduce_grad(mixed_out, branch_back)
-    dq, dk, dv, dgate, dtq, dtk, dtv, dgain, dgamma, dbeta = mixer_back(
-        projected, seg, segrow, gamma, beta, taps, gain_row, out, fresh, inv, state, mixed_back
-    )
-    dbeta = dbeta[:, 0]
-    projected_back = jnp.concatenate([dq, dk, dv, dgate], axis=1)
+
+    backs = []
+
+    def mix_back(n, *tokens):
+        g, at = n * GROUPS // STEPS, n % (STEPS // GROUPS) * heads
+        span = slice(n * heads, (n + 1) * heads)
+        gate = after(gamma[span], *tokens)
+        backs.append(
+            mixer_back(projected[g], at, seg, segrow, gate, beta[span], tap_groups[g], gain_row, *kept[n][1:], mixed_back, n * heads)
+        )
+        return backs[-1][0]
+
+    def group_back(g):
+        each = STEPS // GROUPS
+        return jnp.concatenate([x[n] for n in range(4) for x in backs[g * each : (g + 1) * each]], axis=1)
+
+    done = mix_back(0, t_gu.sent, t_out.given)
+    t_out.first(done)
+    t_down.second(done)
+    done = mix_back(1, t_out.sent, t_down.passed)
+    back_a = group_back(0)
+    t_a = Total(normed_one, back_a)
+    t_a.core(done)
+    t_down.deep(done)
+    done = mix_back(2, t_a.given, t_down.kept)
+    t_gu.second(done)
+    t_a.first(t_gu.passed)
+    t_out.second(t_a.sent)
+    done = mix_back(3, t_a.sent, t_out.passed)
+    t_down.finish(done)
+    t_gu.deep(done)
+    back_b = group_back(1)
+    t_b = Total(normed_one, back_b)
+    t_b.core(t_gu.kept)
+    t_out.deep(t_b.given)
+    dgain = sum(x[7] for x in backs)
+    dgamma = jnp.concatenate([x[8] for x in backs], axis=0)
+    dbeta = jnp.concatenate([x[9][:, 0] for x in backs], axis=0)
     slope = -dgamma * rate * jax.nn.sigmoid(logits[:HEADS] + bias)
     logits_back = jnp.concatenate([slope, dbeta * beta * (1.0 - beta)], axis=0).astype(BF)
     grad_rates = jnp.stack([jnp.sum(dgamma * gamma, axis=1), jnp.sum(slope, axis=1)])
+    grad_taps = jnp.concatenate([x[n] for n in (4, 5, 6) for x in backs], axis=1)
     grad_decay = lax.dot_general(normed_one, logits_back, (((0,), (1,)), ((), ())), preferred_element_type=F32)
-    normed_one_back = dot_nt(projected_back, mix_in) + lax.dot_general(
+    near = dot_nt(after(back_a, t_b.given), mix_in[0]) + lax.dot_general(
         logits_back, decay_full, (((0,), (1,)), ((), ())), preferred_element_type=F32
     )
-    grad_mix_in = reduce_grad(normed_one, projected_back)
-    hidden_part, gain_one = norm_one_pull(normed_one_back)
+    t_b.first(near)
+    near = near + dot_nt(after(back_b, t_b.sent), mix_in[1])
+    t_a.second(t_b.sent)
+    hidden_part, gain_one = norm_one_pull(after(near, t_a.passed))
     grad_in = residual_back + hidden_part
-
-    parts = [jnp.stack([gain_one, gain_two]), grad_decay, grad_rates, jnp.concatenate([dtq, dtk, dtv], axis=1), dgain]
-    flat = jnp.concatenate([x.reshape(-1) for x in parts])
-    flat = jnp.pad(flat, (0, -flat.shape[0] % 1024)).reshape(-1, 128)
-    flat = lax.psum(flat, ("rep", "shard")).reshape(-1)
-    found, start = [], 0
-    for x in parts:
-        found.append(flat[start : start + x.size].reshape(x.shape))
-        start += x.size
+    t_b.second(gain_one)
+    t_a.deep(t_b.passed)
+    t_gu.finish(t_b.passed)
+    t_out.finish(t_b.passed)
     count = lax.axis_size("shard")
-    mine = lambda x, axis: lax.dynamic_slice_in_dim(x, z * (x.shape[axis] // count), x.shape[axis] // count, axis)
+    small_total = Small([
+        parted(jnp.stack([gain_one, gain_two])),
+        grad_decay.reshape(count, -1, 2 * HEADS),
+        parted(grad_rates),
+        parted(grad_taps),
+        parted(dgain[0]),
+    ])
+    numbers = part_numbers()
+    wide = t_gu.done.shape[1] // 128
+    merged = jnp.concatenate(
+        [t_down.done, t_out.done] + [t_gu.done[:, n * 128 : (n + 1) * 128] for n in range(wide)]
+    )
+    s_rest = Spread(merged)
+    t_b.deep(s_rest.done)
+    small_total.add(t_b.kept)
+    s_rest.first(t_b.kept)
+    t_a.finish(s_rest.pair)
+    t_b.finish(s_rest.pair)
+    s_mix = Spread(jnp.concatenate([t_a.done, t_b.done], axis=1))
+    small_total.add(s_mix.done)
+    s_rest.core(s_mix.done)
+    s_mix.first(s_rest.four)
+    small_total.add(s_mix.pair)
+    copies, at, start = [], [], 0
+    for out, deep in enumerate((t_down.rows, t_out.rows)):
+        copies.append((start, deep, 128, out, "columns", 0))
+        start += deep
+    for n in range(wide):
+        copies.append((start, t_gu.rows // 2, 128, 2, "both", n))
+        start += t_gu.rows // 2
+    for part in numbers:
+        at += [part, part]
+        for n in range(wide):
+            at += [part % 2, part // 2 * wide + n]
+    grad_down, grad_mix_out, grad_gate_up = finish_totals(
+        s_rest.parts(s_mix.pair), copies, at, [w_down.shape, w_mix_out.shape, w_gate_up.shape]
+    )
+    s_mix.core(grad_down)
+    small_total.add(s_mix.four)
+    parts = small_total.finish()
+    each = t_a.done.shape[1] // 128
+    copies, at = [], []
+    edge, wide, tall = 0, KEYS // GROUPS // 128, VALS // GROUPS // 128
+    for part in numbers:
+        for g in range(GROUPS):
+            for n in range(each):
+                block = part * each + n
+                to = block + g * wide
+                to = jnp.where(block >= wide, block - wide + KEYS // 128 + g * wide, to)
+                to = jnp.where(block >= 2 * wide, block - 2 * wide + 2 * KEYS // 128 + g * tall, to)
+                to = jnp.where(block >= 2 * wide + tall, block - 2 * wide - tall + (2 * KEYS + VALS) // 128 + g * tall, to)
+                at.append(to)
+    pieces = s_mix.parts()
+    grad_mix_in = finish_mix(pieces, GROUPS * each, at, w_mix_in.shape)
     return (
         result,
         grad_in,
-        mine(found[0], 1),
+        parts[0],
         grad_mix_in,
-        mine(found[1], 0),
-        mine(found[2], 1),
-        mine(found[3], 1),
-        mine(found[4][0], 0),
+        parts[1],
+        parts[2],
+        parts[3],
+        parts[4],
         grad_mix_out,
         grad_gate_up,
         grad_down,
@@ -635,11 +988,11 @@
 
 
 def solution(mesh):
-    rows, columns, both = P("shard", None), P(None, "shard"), P(("rep", "shard"), None)
+    rows, columns_, both = P("shard", None), P(None, "shard"), P(("rep", "shard"), None)
     return jax.shard_map(
         body,
         mesh=mesh,
-        in_specs=(both, P(("rep", "shard")), columns, rows, rows, columns, columns, P("shard"), rows, rows, rows, both),
-        out_specs=(both, both, columns, rows, rows, columns, columns, P("shard"), rows, rows, rows),
+        in_specs=(both, P(("rep", "shard")), columns_, rows, rows, columns_, columns_, P("shard"), rows, rows, rows, both),
+        out_specs=(both, both, columns_, rows, rows, columns_, columns_, P("shard"), rows, rows, rows),
         check_vma=False,
     )

time: 849 us -> 599 us (0.71)
  waiting for transfers between devices: 302 us -> 117 us
  Pallas kernels: 107 us -> 151 us
  starting transfers between devices: 139 us -> 97.3 us
  matrix products: 127 us -> 91.7 us
  other arithmetic: 65 us -> 41.4 us
  between operations: 16 us -> 3.11 us
  local copies, waits for them, and re-layouts: 81.1 us -> 90.5 us
    psum x1 -> x0, waiting for transfers between devices: 101 us -> none  [body(): flat = lax.psum(flat, ('rep', 'shard')).reshape(-1)]
    ppermute x108 -> x44, waiting for transfers between devices: 130 us -> 79.2 us  [hop(): return lax.ppermute(value, 'rep', pairs)]
    pallas_call x6 -> x17, Pallas kernels: 107 us -> 151 us  [the longest x4 46.4 us: mixer_back(): pl.pallas_call(back_kernel, grid=(heads,), in_specs=[columns(rows, DK, at...]
    ppermute x27 -> x36, waiting for transfers between devices: 71.1 us -> 37.6 us  [shift(): lax.ppermute(value, 'shard', [(i, (i + by) % count) for i in range(count)])]
    ppermute x108 -> x44, starting transfers between devices: 64.7 us -> 33.4 us  [hop(): return lax.ppermute(value, 'rep', pairs)]
    dot_general x5 -> x4, matrix products: 42 us -> 16.5 us  [dot_nt(): lax.dot_general(a, b, (((1,), (1,)), ((), ())), preferred_element_type=F32)]
    dot_general x4 -> x3, matrix products: 40.5 us -> 18.8 us  [dot_nn(): return jnp.dot(a, b, preferred_element_type=F32)]
    convert_element_type x18 -> x14, other arithmetic: 42.2 us -> 21.2 us  [the longest x4 11.7 us: second(): (kept + got_first.astype(F32)).astype(BF)]
  transfers between devices with their start and end apart: 136 -> 80, of which waited for: 37 -> 25; matrix products, arithmetic and copies ran while one was open for 21% -> 30% of each run, Pallas kernels for 7% -> 21%
where the time goes in v2:
time: 599 us; the launch traced here: 592 us
  Pallas kernels  151 us (25%)
  waiting for transfers between devices  117 us (20%)
  starting transfers between devices  97.3 us (16%)
  matrix products  91.7 us (15%)
  local copies, waits for them, and re-layouts  90.5 us (15%)
  other arithmetic  41.4 us (7%)
    ppermute x44, waiting for transfers between devices, hop(): return lax.ppermute(value, 'rep', pairs)  79.2 us
    ppermute x36, starting transfers between devices, shift(): lax.ppermute(value, 'shard', [(i, (i + by) % count) for i in range(count)])  63.9 us
    dot_general x15, matrix products, dot_tn(): lax.dot_general(a, b, (((0,), (0,)), ((), ())), preferred_element_type=F32)  54.6 us
    pallas_call x4, Pallas kernels, mixer_back(): pl.pallas_call(back_kernel, grid=(heads,), in_specs=[columns(rows, DK, at...  46.4 us
    unnamed x312, local copies, waits for them, and re-layouts  45.9 us
    pallas_call x4, Pallas kernels, mixer(): pl.pallas_call(mix_kernel, grid=(heads,), in_specs=[columns(rows, DK, at)...  38.9 us
    ppermute x36, waiting for transfers between devices, shift(): lax.ppermute(value, 'shard', [(i, (i + by) % count) for i in range(count)])  37.6 us
    ppermute x44, starting transfers between devices, hop(): return lax.ppermute(value, 'rep', pairs)  33.4 us
  transfers between devices with their start and end apart: 80, of which 25 were waited for; matrix products, arithmetic and copies ran while one was open for 30% of the time, Pallas kernels for 21%

profile of v2, /device:TPU:0, one launch (start us, length us, event | category | flops | bytes accessed | tf_op | source)
XLA Modules:
  0.0 592.0 jit_solution(14857008699895700618)
XLA Ops:
  45.4 6.9 %collective-permute-done.6 = bf16[3,256,384]{2,1,0:T(8,128)(2,1)} collective-permute-done((bf16[3,256,384]{2,1,0:T(8,128)(2,1)S(1)}, bf16[3,256,384]{2,1,0:T(8,128)(2,1)}, u32[]{:S(2)}, u32[]{:S(2)}) %collective-permute-start.6) | collective-permute-done | bytes 589856 | tf_op jit(solution)/shard_map/ppermute | solution.py:489
  58.6 11.3 %collective-permute-done.7.refs_1_ = bf16[6,256,384]{2,1,0:T(8,128)(2,1)S(1)} collective-permute-done((bf16[6,256,384]{2,1,0:T(8,128)(2,1)S(1)}, bf16[6,256,384]{2,1,0:T(8,128)(2,1)S(1)}, u32[]{:S(2)}, u32[]{:S(2)}) %collective-permute-start.7) | collective-permute-done | bytes 1179680 | tf_op jit(solution)/shard_map/ppermute | solution.py:489
  80.8 7.8 %collective-permute-done.11 = bf16[256,384]{1,0:T(8,128)(2,1)S(1)} collective-permute-done((bf16[256,384]{1,0:T(8,128)(2,1)}, bf16[256,384]{1,0:T(8,128)(2,1)S(1)}, u32[]{:S(2)}, u32[]{:S(2)}) %collective-permute-start.11) | collective-permute-done | bytes 196640 | tf_op jit(solution)/shard_map/ppermute | solution.py:494
  90.3 8.0 %fusion.104.q_ref.k_ref.v_ref.gate_ref = f32[512,3072]{1,0:T(8,128)} fusion(bf16[512,1024]{1,0:T(8,128)(2,1)S(1)} %copy-done.61, bf16[1024,3072]{1,0:T(8,128)(2,1)} %shard_map.203), kind=kOutput, calls=%fused_computation.302 | convolution fusion | flops 3221225472 | bytes 13631488 | tf_op jit(solution)/shard_map/dot_general | solution.py:26
  111.8 9.6 %shard_map.204 = (bf16[512,512]{1,0:T(8,128)(2,1)S(1)}, f32[512,512]{1,0:T(8,128)S(1)}, bf16[512,512]{1,0:T(8,128)(2,1)S(1)}, bf16[2,4,128,128]{3,2,1,0:T(8,128)(2,1)S(1)}, bf16[2,4,128,256]{3,2,1,0:T(8,128)(2,1)S(1)}) custom-call(f32[512,3072]{1,0:T(8,128)S(1)} %copy-done.22, f32[512,3072]{1,0:T(8,128)S(1)} %copy-done.22, f32[512,3072]{1,0:T(8,128)S(1)} %copy-done.22, ...), custom_call_target="tpu_custom_call" | custom-call | flops 10000000000 | bytes 8000000 | tf_op jit(solution)/shard_map/pallas_call | solution.py:193
  125.2 9.6 %shard_map.205 = (bf16[512,512]{1,0:T(8,128)(2,1)S(1)}, f32[512,512]{1,0:T(8,128)S(1)}, bf16[512,512]{1,0:T(8,128)(2,1)S(1)}, bf16[2,4,128,128]{3,2,1,0:T(8,128)(2,1)S(1)}, bf16[2,4,128,256]{3,2,1,0:T(8,128)(2,1)S(1)}) custom-call(f32[512,3072]{1,0:T(8,128)S(1)} %copy-done.22, f32[512,3072]{1,0:T(8,128)S(1)} %copy-done.22, f32[512,3072]{1,0:T(8,128)S(1)} %copy-done.22, ...), custom_call_target="tpu_custom_call" | custom-call | flops 10000000000 | bytes 8000000 | tf_op jit(solution)/shard_map/pallas_call | solution.py:193
  151.8 11.9 %collective-permute-done.21 = bf16[32,5632]{1,0:T(8,128)(2,1)S(1)} collective-permute-done((bf16[32,5632]{1,0:T(8,128)(2,1)S(1)}, bf16[32,5632]{1,0:T(8,128)(2,1)S(1)}, u32[]{:S(2)}, u32[]{:S(2)}) %collective-permute-start.21) | collective-permute-done | bytes 360480 | tf_op jit(solution)/shard_map/ppermute | solution.py:494
  163.7 7.3 %collective-permute-start.25 = (bf16[704,128]{1,0:T(8,128)(2,1)S(1)}, bf16[704,128]{1,0:T(8,128)(2,1)S(1)}, u32[]{:S(2)}, u32[]{:S(2)}) collective-permute-start(bf16[704,128]{1,0:T(8,128)(2,1)S(1)} %copy-done.103), channel_id=1, source_target_pairs={{0,1},{1,2},{2,3},{3,0},{4,5},{5,6},{6,7},{7,4},{8,9},{9,10},{10,1... | collective-permute-start | bytes 540680 | tf_op jit(solution)/shard_map/ppermute | solution.py:494
  175.8 10.0 %shard_map.207 = (bf16[512,512]{1,0:T(8,128)(2,1)S(1)}, f32[512,512]{1,0:T(8,128)S(1)}, bf16[512,512]{1,0:T(8,128)(2,1)S(1)}, bf16[2,4,128,128]{3,2,1,0:T(8,128)(2,1)S(1)}, bf16[2,4,128,256]{3,2,1,0:T(8,128)(2,1)S(1)}) custom-call(f32[512,3072]{1,0:T(8,128)S(1)} %fusion.106.q_ref.k_ref.v_ref.gate_ref, f32[512,3072]{1,0:T(8,128)S(1)} %fusion.106.q_ref.k_ref.v_ref.gate_ref, ...), custom_call_target="tpu_custom_call" | custom-call | flops 10000000000 | bytes 8000000 | tf_op jit(solution)/shard_map/pallas_call | solution.py:193
  185.9 8.9 %collective-permute-done.28.refs_1_ = bf16[6,512,128]{2,1,0:T(8,128)(2,1)S(1)} collective-permute-done((bf16[6,512,128]{2,1,0:T(8,128)(2,1)S(1)}, bf16[6,512,128]{2,1,0:T(8,128)(2,1)S(1)}, u32[]{:S(2)}, u32[]{:S(2)}) %collective-permute-start.28) | collective-permute-done | bytes 786464 | tf_op jit(solution)/shard_map/ppermute | solution.py:489
  197.3 9.6 %shard_map.208 = (bf16[512,512]{1,0:T(8,128)(2,1)S(1)}, f32[512,512]{1,0:T(8,128)S(1)}, bf16[512,512]{1,0:T(8,128)(2,1)S(1)}, bf16[2,4,128,128]{3,2,1,0:T(8,128)(2,1)S(1)}, bf16[2,4,128,256]{3,2,1,0:T(8,128)(2,1)S(1)}) custom-call(f32[512,3072]{1,0:T(8,128)S(1)} %fusion.106.q_ref.k_ref.v_ref.gate_ref, f32[512,3072]{1,0:T(8,128)S(1)} %fusion.106.q_ref.k_ref.v_ref.gate_ref, ...), custom_call_target="tpu_custom_call" | custom-call | flops 10000000000 | bytes 8000000 | tf_op jit(solution)/shard_map/pallas_call | solution.py:193
  228.0 8.2 %shard_map.210.gate_w_ref.up_w_ref = bf16[1024,5632]{1,0:T(8,128)(2,1)} custom-call(s32[49]{0:T(128)S(1)} %stack.394.at_ref, bf16[256,5632]{1,0:T(8,128)(2,1)} %own_ref.4, bf16[6,32,5632]{2,1,0:T(8,128)(2,1)S(1)} %pad_maximum_fusion.1.refs_0_, bf16[6,32,5632]{2,1,0:T(8,128)(2,1)S(1)} %collective-permute-done.32.refs_1_, bf16[6,32,5632]{2,1,0:T(8,128)(2,1)} %copy-done.90, ...), custom_call_target="tpu_custom_call" | custom-call | tf_op jit(solution)/shard_map/pallas_call | solution.py:555
  242.0 9.7 %shard_map.211 = (bf16[512,2816]{1,0:T(8,128)(2,1)S(1)}, bf16[512,2816]{1,0:T(8,128)(2,1)S(1)}, bf16[512,2816]{1,0:T(8,128)(2,1)S(1)}) custom-call(bf16[512,1024]{1,0:T(8,128)(2,1)S(1)} %multiply_convert_fusion.x_ref, bf16[1024,5632]{1,0:T(8,128)(2,1)S(1)} %copy-done, bf16[1024,5632]{1,0:T(8,128)(2,1)S(1)} %copy-done), custom_call_target="tpu_custom_call" | custom-call | flops 5905580032 | bytes 11534336 | tf_op jit(solution)/shard_map/pallas_call | solution.py:416
  270.0 18.6 %shard_map.213 = (bf16[2,512,2816]{2,1,0:T(8,128)(2,1)S(1)}, f32[512,1024]{1,0:T(8,128)S(1)}, f32[512,1024]{1,0:T(8,128)S(1)}) custom-call(bf16[512,1024]{1,0:T(8,128)(2,1)S(1)} %copy-done.1, bf16[512,2816]{1,0:T(8,128)(2,1)S(1)} %copy-done.18, bf16[512,2816]{1,0:T(8,128)(2,1)S(1)} %copy-done.20, bf16[512,2816]{1,0:T(8,128)(2,1)S(1)} %copy-done.15, ...), custom_call_target="tpu_custom_call" | custom-call | flops 11811160064 | bytes 17301504 | tf_op jit(solution)/shard_map/pallas_call | solution.py:448
  294.2 6.0 %fusion.15 = f32[1024,1408]{1,0:T(8,128)} fusion(bf16[512,1024]{1,0:T(8,128)(2,1)S(1)} %multiply_convert_fusion.x_ref, bf16[2,512,2816]{2,1,0:T(8,128)(2,1)} %copy-done.11, s32[]{:T(128)S(6)} %select_n.1217, s32[]{:T(128)S(6)} %select_n.1230), kind=kOutput, calls=%fused_computation.52 | convolution fusion | flops 1476395008 | bytes 8257544 | tf_op jit(solution)/shard_map/dot_general | solution.py:34
  300.2 7.3 %collective-permute-done.38 = bf16[2816,512]{1,0:T(8,128)(2,1)} collective-permute-done((bf16[2816,512]{1,0:T(8,128)(2,1)}, bf16[2816,512]{1,0:T(8,128)(2,1)}, u32[]{:S(2)}, u32[]{:S(2)}) %collective-permute-start.38) | collective-permute-done | bytes 2883616 | tf_op jit(solution)/shard_map/ppermute | solution.py:489
  325.2 11.6 %shard_map.214 = (bf16[512,256]{1,0:T(8,128)(2,1)S(1)}, bf16[512,256]{1,0:T(8,128)(2,1)S(1)}, bf16[512,512]{1,0:T(8,128)(2,1)S(1)}, bf16[512,512]{1,0:T(8,128)(2...) custom-call(f32[512,3072]{1,0:T(8,128)S(1)} %bitcast.373, ...), custom_call_target="tpu_custom_call" | custom-call | flops 12000000000 | bytes 10000000 | tf_op jit(solution)/shard_map/pallas_call | solution.py:362
  347.8 11.8 %shard_map.215 = (bf16[512,256]{1,0:T(8,128)(2,1)S(1)}, bf16[512,256]{1,0:T(8,128)(2,1)S(1)}, bf16[512,512]{1,0:T(8,128)(2,1)S(1)}, bf16[512,512]{1,0:T(8,128)(2...) custom-call(f32[512,3072]{1,0:T(8,128)S(1)} %bitcast.373, ...), custom_call_target="tpu_custom_call" | custom-call | flops 12000000000 | bytes 10000000 | tf_op jit(solution)/shard_map/pallas_call | solution.py:362
  372.6 11.4 %shard_map.216 = (bf16[512,256]{1,0:T(8,128)(2,1)S(1)}, bf16[512,256]{1,0:T(8,128)(2,1)S(1)}, bf16[512,512]{1,0:T(8,128)(2,1)S(1)}, bf16[512,512]{1,0:T(8,128)(2...) custom-call(f32[512,3072]{1,0:T(8,128)S(1)} %bitcast.371, ...), custom_call_target="tpu_custom_call" | custom-call | flops 12000000000 | bytes 10000000 | tf_op jit(solution)/shard_map/pallas_call | solution.py:362
  411.3 11.6 %shard_map.217 = (bf16[512,256]{1,0:T(8,128)(2,1)S(1)}, bf16[512,256]{1,0:T(8,128)(2,1)S(1)}, bf16[512,512]{1,0:T(8,128)(2,1)S(1)}, bf16[512,512]{1,0:T(8,128)(2...) custom-call(f32[512,3072]{1,0:T(8,128)S(1)} %bitcast.371, ...), custom_call_target="tpu_custom_call" | custom-call | flops 12000000000 | bytes 10000000 | tf_op jit(solution)/shard_map/pallas_call | solution.py:362
  422.9 9.2 %collective-permute-done.46 = bf16[4,128,1408]{2,1,0:T(8,128)(2,1)S(1)} collective-permute-done((bf16[4,128,1408]{2,1,0:T(8,128)(2,1)S(1)}, bf16[4,128,1408]{2,1,0:T(8,128)(2,1)S(1)}, u32[]{:S(2)}, u32[]{:S(2)}) %collective-permute-start.46) | collective-permute-done | bytes 1441824 | tf_op jit(solution)/shard_map/ppermute | solution.py:489
  449.4 7.9 %convolution_add_fusion.3 = f32[512,1024]{1,0:T(8,128)} fusion(f32[512,1024]{1,0:T(8,128)S(1)} %fusion.84, bf16[512,3072]{1,0:T(8,128)(2,1)S(1)} %copy-done.98, bf16[1024,3072]{1,0:T(8,128)(2,1)} %shard_map.203), kind=kOutput, calls=%fused_computation.51 | convolution fusion | flops 3221749760 | bytes 13631488 | tf_op jit(solution)/shard_map/dot_general | solution.py:30
  470.9 10.7 %collective-permute-done.52 = bf16[1024,768]{1,0:T(8,128)(2,1)S(1)} collective-permute-done((bf16[1024,768]{1,0:T(8,128)(2,1)S(1)}, bf16[1024,768]{1,0:T(8,128)(2,1)S(1)}, u32[]{:S(2)}, u32[]{:S(2)}) %collective-permute-start.52) | collective-permute-done | bytes 1572896 | tf_op jit(solution)/shard_map/ppermute | solution.py:489
  512.4 7.3 %collective-permute-done.69.refs_1_ = bf16[2624,128]{1,0:T(8,128)(2,1)S(1)} collective-permute-done((bf16[2624,128]{1,0:T(8,128)(2,1)S(1)}, bf16[2624,128]{1,0:T(8,128)(2,1)S(1)}, u32[]{:S(2)}, u32[]{:S(2)}) %collective-permute-start.69) | collective-permute-done | bytes 671776 | tf_op jit(solution)/shard_map/ppermute | solution.py:489
  (639 shorter events, 356.6 us)
Async XLA Ops:
  100.6 34.3 %collective-permute-start.17 = (bf16[512,128]{1,0:T(8,128)(2,1)}, bf16[512,128]{1,0:T(8,128)(2,1)S(1)}, u32[]{:S(2)}, u32[]{:S(2)}) collective-permute-start(bf16[512,128]{1,0:T(8,128)(2,1)} %constant_dynamic-slice_fusion.9), channel_id=1, source_target_pairs={{0,1},{1,2},{2,3},{3,0},{4,5},{5,6},{6,7},{7,4},{8,9},{9,10},{10,1... | collective-permute-start | bytes 393224 | tf_op jit(solution)/shard_map/ppermute | solution.py:494
  104.8 30.1 %collective-permute-start.18 = (bf16[512,128]{1,0:T(8,128)(2,1)}, bf16[512,128]{1,0:T(8,128)(2,1)S(1)}, u32[]{:S(2)}, u32[]{:S(2)}) collective-permute-start(bf16[512,128]{1,0:T(8,128)(2,1)} %constant_dynamic-slice_fusion.9), channel_id=1, source_target_pairs={{0,2},{1,3},{2,0},{3,1},{4,6},{5,7},{6,4},{7,5},{8,10},{9,11},{10,... | collective-permute-start | bytes 393224 | tf_op jit(solution)/shard_map/ppermute | solution.py:494
  104.8 30.2 %collective-permute-start.19 = (bf16[512,128]{1,0:T(8,128)(2,1)}, bf16[512,128]{1,0:T(8,128)(2,1)S(1)}, u32[]{:S(2)}, u32[]{:S(2)}) collective-permute-start(bf16[512,128]{1,0:T(8,128)(2,1)} %constant_dynamic-slice_fusion.9), channel_id=1, source_target_pairs={{0,3},{1,0},{2,1},{3,2},{4,7},{5,4},{6,5},{7,6},{8,11},{9,8},{10,9... | collective-permute-start | bytes 393224 | tf_op jit(solution)/shard_map/ppermute | solution.py:494
  136.1 27.7 %collective-permute-start.21 = (bf16[32,5632]{1,0:T(8,128)(2,1)S(1)}, bf16[32,5632]{1,0:T(8,128)(2,1)S(1)}, u32[]{:S(2)}, u32[]{:S(2)}) collective-permute-start(bf16[32,5632]{1,0:T(8,128)(2,1)S(1)} %copy-done.93), channel_id=1, source_target_pairs={{0,2},{1,3},{2,0},{3,1},{4,6},{5,7},{6,4},{7,5},{8,10},{9,11},{10,... | collective-permute-start | bytes 1081352 | tf_op jit(solution)/shard_map/ppermute | solution.py:494
  140.0 33.5 %collective-permute-start.23 = (bf16[3,512,128]{2,1,0:T(8,128)(2,1)S(1)}, bf16[3,512,128]{2,1,0:T(8,128)(2,1)S(1)}, u32[]{:S(2)}, u32[]{:S(2)}) collective-permute-start(bf16[3,512,128]{2,1,0:T(8,128)(2,1)S(1)} %pad_maximum_fusion.15), channel_id=1, source_target_pairs={{0,8},{4,20},{8,0},{12,28},{16,24},{20,4},{24,16},{28,12},{1,9},{5... | collective-permute-start | bytes 1179656 | tf_op jit(solution)/shard_map/ppermute | solution.py:489
  163.7 31.9 %collective-permute-start.25 = (bf16[704,128]{1,0:T(8,128)(2,1)S(1)}, bf16[704,128]{1,0:T(8,128)(2,1)S(1)}, u32[]{:S(2)}, u32[]{:S(2)}) collective-permute-start(bf16[704,128]{1,0:T(8,128)(2,1)S(1)} %copy-done.103), channel_id=1, source_target_pairs={{0,1},{1,2},{2,3},{3,0},{4,5},{5,6},{6,7},{7,4},{8,9},{9,10},{10,1... | collective-permute-start | bytes 540680 | tf_op jit(solution)/shard_map/ppermute | solution.py:494
  171.1 26.0 %collective-permute-start.26 = (bf16[704,128]{1,0:T(8,128)(2,1)S(1)}, bf16[704,128]{1,0:T(8,128)(2,1)S(1)}, u32[]{:S(2)}, u32[]{:S(2)}) collective-permute-start(bf16[704,128]{1,0:T(8,128)(2,1)S(1)} %copy-done.103), channel_id=1, source_target_pairs={{0,2},{1,3},{2,0},{3,1},{4,6},{5,7},{6,4},{7,5},{8,10},{9,11},{10,... | collective-permute-start | bytes 540680 | tf_op jit(solution)/shard_map/ppermute | solution.py:494
  195.6 26.8 %collective-permute-start.32 = (bf16[6,32,5632]{2,1,0:T(8,128)(2,1)S(1)}, bf16[6,32,5632]{2,1,0:T(8,128)(2,1)S(1)}, u32[]{:S(2)}, u32[]{:S(2)}) collective-permute-start(bf16[6,32,5632]{2,1,0:T(8,128)(2,1)S(1)} %pad_maximum_fusion.1.refs_0_), channel_id=1, source_target_pairs={{0,16},{4,12},{8,24},{12,4},{16,0},{20,28},{24,8},{28,20},{1,17},{... | collective-permute-start | bytes 6488072 | tf_op jit(solution)/shard_map/ppermute | solution.py:489
  197.1 26.9 %collective-permute-start.33 = (bf16[6,32,5632]{2,1,0:T(8,128)(2,1)S(1)}, bf16[6,32,5632]{2,1,0:T(8,128)(2,1)S(1)}, u32[]{:S(2)}, u32[]{:S(2)}) collective-permute-start(bf16[6,32,5632]{2,1,0:T(8,128)(2,1)S(1)} %pad_maximum_fusion.1.refs_0_), channel_id=1, source_target_pairs={{0,4},{4,0},{8,12},{12,8},{16,20},{20,16},{24,28},{28,24},{1,5},{5... | collective-permute-start | bytes 6488072 | tf_op jit(solution)/shard_map/ppermute | solution.py:489
  310.0 26.8 %collective-permute-start.41 = (bf16[2816,256]{1,0:T(8,128)(2,1)S(1)}, bf16[2816,256]{1,0:T(8,128)(2,1)S(1)}, u32[]{:S(2)}, u32[]{:S(2)}) collective-permute-start(bf16[2816,256]{1,0:T(8,128)(2,1)S(1)} %fusion.2), channel_id=1, source_target_pairs={{0,8},{4,20},{8,0},{12,28},{16,24},{20,4},{24,16},{28,12},{1,9},{5... | collective-permute-start | bytes 4325384 | tf_op jit(solution)/shard_map/ppermute | solution.py:489
  322.0 71.2 %collective-permute-start.44 = (bf16[1024,1408]{1,0:T(8,128)(2,1)}, bf16[1024,1408]{1,0:T(8,128)(2,1)S(1)}, u32[]{:S(2)}, u32[]{:S(2)}) collective-permute-start(bf16[1024,1408]{1,0:T(8,128)(2,1)} %add_convert_fusion.1), channel_id=1, source_target_pairs={{0,8},{4,20},{8,0},{12,28},{16,24},{20,4},{24,16},{28,12},{1,9},{5... | collective-permute-start | bytes 8650760 | tf_op jit(solution)/shard_map/ppermute | solution.py:489
  340.3 30.6 %collective-permute-start.42 = (bf16[4,704,128]{2,1,0:T(8,128)(2,1)}, bf16[4,704,128]{2,1,0:T(8,128)(2,1)}, u32[]{:S(2)}, u32[]{:S(2)}) collective-permute-start(bf16[4,704,128]{2,1,0:T(8,128)(2,1)} %constant_dynamic-slice_fusion.7), channel_id=1, source_target_pairs={{0,16},{4,12},{8,24},{12,4},{16,0},{20,28},{24,8},{28,20},{1,17},{... | collective-permute-start | bytes 2162696 | tf_op jit(solution)/shard_map/ppermute | solution.py:489
  347.0 60.1 %collective-permute-start.45 = (bf16[2048,256]{1,0:T(8,128)(2,1)}, bf16[2048,256]{1,0:T(8,128)(2,1)}, u32[]{:S(2)}, u32[]{:S(2)}) collective-permute-start(bf16[2048,256]{1,0:T(8,128)(2,1)} %add_convert_fusion.8), channel_id=1, source_target_pairs={{0,8},{4,20},{8,0},{12,28},{16,24},{20,4},{24,16},{28,12},{1,9},{5... | collective-permute-start | bytes 3145736 | tf_op jit(solution)/shard_map/ppermute | solution.py:489
  370.9 30.7 %collective-permute-start.43 = (bf16[1024,1536]{1,0:T(8,128)(2,1)}, bf16[1024,1536]{1,0:T(8,128)(2,1)}, u32[]{:S(2)}, u32[]{:S(2)}) collective-permute-start(bf16[1024,1536]{1,0:T(8,128)(2,1)} %convolution_convert_fusion.3), channel_id=1, source_target_pairs={{0,4},{4,0},{8,12},{12,8},{16,20},{20,16},{24,28},{28,24},{1,5},{5... | collective-permute-start | bytes 9437192 | tf_op jit(solution)/shard_map/ppermute | solution.py:489
  384.9 53.2 %collective-permute-start.54 = (bf16[704,128]{1,0:T(8,128)(2,1)}, bf16[704,128]{1,0:T(8,128)(2,1)}, u32[]{:S(2)}, u32[]{:S(2)}) collective-permute-start(bf16[704,128]{1,0:T(8,128)(2,1)} %get-tuple-element.375), channel_id=1, source_target_pairs={{0,1},{1,2},{2,3},{3,0},{4,5},{5,6},{6,7},{7,4},{8,9},{9,10},{10,1... | collective-permute-start | bytes 540680 | tf_op jit(solution)/shard_map/ppermute | solution.py:494
  384.9 55.2 %collective-permute-start.55 = (bf16[704,128]{1,0:T(8,128)(2,1)}, bf16[704,128]{1,0:T(8,128)(2,1)}, u32[]{:S(2)}, u32[]{:S(2)}) collective-permute-start(bf16[704,128]{1,0:T(8,128)(2,1)} %get-tuple-element.374), channel_id=1, source_target_pairs={{0,2},{1,3},{2,0},{3,1},{4,6},{5,7},{6,4},{7,5},{8,10},{9,11},{10,... | collective-permute-start | bytes 540680 | tf_op jit(solution)/shard_map/ppermute | solution.py:494
  394.8 45.4 %collective-permute-start.56 = (bf16[704,128]{1,0:T(8,128)(2,1)}, bf16[704,128]{1,0:T(8,128)(2,1)}, u32[]{:S(2)}, u32[]{:S(2)}) collective-permute-start(bf16[704,128]{1,0:T(8,128)(2,1)} %get-tuple-element.373), channel_id=1, source_target_pairs={{0,3},{1,0},{2,1},{3,2},{4,7},{5,4},{6,5},{7,6},{8,11},{9,8},{10,9... | collective-permute-start | bytes 540680 | tf_op jit(solution)/shard_map/ppermute | solution.py:494
  401.6 30.5 %collective-permute-start.46 = (bf16[4,128,1408]{2,1,0:T(8,128)(2,1)S(1)}, bf16[4,128,1408]{2,1,0:T(8,128)(2,1)S(1)}, u32[]{:S(2)}, u32[]{:S(2)}) collective-permute-start(bf16[4,128,1408]{2,1,0:T(8,128)(2,1)S(1)} %constant_dynamic-slice_fusion.6), channel_id=1, source_target_pairs={{0,16},{4,12},{8,24},{12,4},{16,0},{20,28},{24,8},{28,20},{1,17},{... | collective-permute-start | bytes 4325384 | tf_op jit(solution)/shard_map/ppermute | solution.py:489
  407.1 60.3 %collective-permute-start.48 = (bf16[1024,768]{1,0:T(8,128)(2,1)}, bf16[1024,768]{1,0:T(8,128)(2,1)}, u32[]{:S(2)}, u32[]{:S(2)}) collective-permute-start(bf16[1024,768]{1,0:T(8,128)(2,1)} %add_convert_fusion.5), channel_id=1, source_target_pairs={{0,8},{4,20},{8,0},{12,28},{16,24},{20,4},{24,16},{28,12},{1,9},{5... | collective-permute-start | bytes 4718600 | tf_op jit(solution)/shard_map/ppermute | solution.py:489
  438.1 26.2 %collective-permute-start.57 = (bf16[4,512,128]{2,1,0:T(8,128)(2,1)}, bf16[4,512,128]{2,1,0:T(8,128)(2,1)S(1)}, u32[]{:S(2)}, u32[]{:S(2)}) collective-permute-start(bf16[4,512,128]{2,1,0:T(8,128)(2,1)} %constant_dynamic-slice_fusion.5), channel_id=1, source_target_pairs={{0,16},{4,12},{8,24},{12,4},{16,0},{20,28},{24,8},{28,20},{1,17},{... | collective-permute-start | bytes 1572872 | tf_op jit(solution)/shard_map/ppermute | solution.py:489
  441.5 50.9 %collective-permute-start.61 = (bf16[128,1408]{1,0:T(8,128)(2,1)S(1)}, bf16[128,1408]{1,0:T(8,128)(2,1)S(1)}, u32[]{:S(2)}, u32[]{:S(2)}) collective-permute-start(bf16[128,1408]{1,0:T(8,128)(2,1)S(1)} %get-tuple-element.362), channel_id=1, source_target_pairs={{0,1},{1,2},{2,3},{3,0},{4,5},{5,6},{6,7},{7,4},{8,9},{9,10},{10,1... | collective-permute-start | bytes 1081352 | tf_op jit(solution)/shard_map/ppermute | solution.py:494
  442.3 50.0 %collective-permute-start.62 = (bf16[128,1408]{1,0:T(8,128)(2,1)S(1)}, bf16[128,1408]{1,0:T(8,128)(2,1)S(1)}, u32[]{:S(2)}, u32[]{:S(2)}) collective-permute-start(bf16[128,1408]{1,0:T(8,128)(2,1)S(1)} %get-tuple-element.361), channel_id=1, source_target_pairs={{0,2},{1,3},{2,0},{3,1},{4,6},{5,7},{6,4},{7,5},{8,10},{9,11},{10,... | collective-permute-start | bytes 1081352 | tf_op jit(solution)/shard_map/ppermute | solution.py:494
  464.3 28.1 %collective-permute-start.63 = (bf16[128,1408]{1,0:T(8,128)(2,1)S(1)}, bf16[128,1408]{1,0:T(8,128)(2,1)S(1)}, u32[]{:S(2)}, u32[]{:S(2)}) collective-permute-start(bf16[128,1408]{1,0:T(8,128)(2,1)S(1)} %get-tuple-element.360), channel_id=1, source_target_pairs={{0,3},{1,0},{2,1},{3,2},{4,7},{5,4},{6,5},{7,6},{8,11},{9,8},{10,9... | collective-permute-start | bytes 1081352 | tf_op jit(solution)/shard_map/ppermute | solution.py:494
  493.8 25.8 %collective-permute-start.69 = (bf16[2624,128]{1,0:T(8,128)(2,1)S(1)}, bf16[2624,128]{1,0:T(8,128)(2,1)S(1)}, u32[]{:S(2)}, u32[]{:S(2)}) collective-permute-start(bf16[2624,128]{1,0:T(8,128)(2,1)S(1)} %constant_dynamic-update-slice_fusion.46.refs_0_), channel_id=1, source_target_pairs={{0,16},{4,12},{8,24},{12,4},{16,0},{20,28},{24,8},{28,20},{1,17},{... | collective-permute-start | bytes 2015240 | tf_op jit(solution)/shard_map/ppermute | solution.py:489
  (182 other events, 1807.1 us)

commit v3 on v2

--- a/solution.py
+++ b/solution.py
@@ -116,13 +116,19 @@
     return beta, decays, strict, ends, reach
 
 
+def split_head(ref, parts):
+    cuts = ((0, DK), (DK, DK), (2 * DK, DV), (2 * DK + DV, DV))[:parts]
+    return [ref.at[:, pl.ds(start, size)] for start, size in cuts]
+
+
 def mix_kernel(
-    q_ref, k_ref, v_ref, gate_ref, seg_ref, segrow_ref, gamma_ref, beta_ref,
-    tapq_ref, tapk_ref, tapv_ref, gain_ref,
+    x_ref, seg_ref, segrow_ref, gamma_ref, beta_ref, tap_ref, gain_ref,
     mixed_ref, out_ref, fresh_ref, inv_ref, state_ref,
     mask_ref, sums_ref,
 ):
     h = pl.program_id(0)
+    q_ref, k_ref, v_ref, gate_ref = split_head(x_ref, 4)
+    tapq_ref, tapk_ref, tapv_ref = split_head(tap_ref, 3)
 
     @pl.when(h == 0)
     def _():
@@ -187,17 +193,20 @@
     return pl.BlockSpec((rows, width), lambda h: (0, at + h))
 
 
+HEAD = 2 * DK + 2 * DV
+TAPS = 2 * DK + DV
+
+
 def mixer(projected, at, seg, segrow, gamma, beta, taps, gain):
-    rows, held = projected.shape[0], projected.shape[1] // (2 * DK + 2 * DV)
+    rows = projected.shape[0]
     chunks, heads = rows // CHUNK, gamma.shape[0]
     return pl.pallas_call(
         mix_kernel,
         grid=(heads,),
         in_specs=[
-            columns(rows, DK, at), columns(rows, DK, held + at), columns(rows, DV, held + at), columns(rows, DV, 2 * held + at),
+            columns(rows, HEAD, at),
             whole((rows, CHUNK)), whole((8, rows)), whole((heads, rows)), per_head(rows),
-            columns(CONV, DK, at), columns(CONV, DK, held + at), columns(CONV, DV, held + at),
-            whole((1, DV)),
+            columns(CONV, TAPS, at), whole((1, DV)),
         ],
         out_specs=[
             columns(rows, DV, 0), columns(rows, DV, 0), columns(rows, DV, 0),
@@ -214,16 +223,19 @@
         scratch_shapes=[pltpu.VMEM((CONV - 1, rows, CHUNK), F32), pltpu.VMEM((heads, 1, rows), F32)],
         compiler_params=pltpu.CompilerParams(vmem_limit_bytes=32 * 2**20),
         cost_estimate=pl.CostEstimate(flops=heads * int(5e9), bytes_accessed=heads * int(4e6), transcendentals=0),
-    )(projected, projected, projected, projected, seg, segrow, gamma, beta[:, None], taps, taps, taps, gain)
+    )(projected, seg, segrow, gamma, beta[:, None], taps, gain)
 
 
 def back_kernel(
-    q_ref, k_ref, v_ref, gate_ref, seg_ref, segrow_ref, gamma_ref, beta_ref,
-    tapq_ref, tapk_ref, tapv_ref, gain_ref, out_ref, fresh_ref, inv_ref, state_ref, back_ref,
-    dq_ref, dk_ref, dv_ref, dgate_ref, dtapq_ref, dtapk_ref, dtapv_ref, dgain_ref, dgamma_ref, dbeta_ref,
-    mask_ref, sums_ref, lift_ref,
+    x_ref, seg_ref, segrow_ref, gamma_ref, beta_ref, tap_ref, gain_ref,
+    out_ref, fresh_ref, inv_ref, state_ref, back_ref, *rest,
 ):
+    dx_ref, dtap_ref, dgain_ref, dgamma_ref, dbeta_ref, mask_ref, sums_ref, lift_ref = rest[-8:]
     h = pl.program_id(0)
+    q_ref, k_ref, v_ref, gate_ref = split_head(x_ref, 4)
+    tapq_ref, tapk_ref, tapv_ref = split_head(tap_ref, 3)
+    dq_ref, dk_ref, dv_ref, dgate_ref = split_head(dx_ref, 4)
+    dtapq_ref, dtapk_ref, dtapv_ref = split_head(dtap_ref, 3)
 
     @pl.when(h == 0)
     def _():
@@ -356,35 +368,29 @@
             dgamma_ref[:, span] = total
 
 
-def mixer_back(projected, at, seg, segrow, gamma, beta, taps, gain, out, fresh, inv, state, back, back_at):
-    rows, held = projected.shape[0], projected.shape[1] // (2 * DK + 2 * DV)
+def mixer_back(projected, at, seg, segrow, gamma, beta, taps, gain, out, fresh, inv, state, back, back_at, into):
+    rows, width = projected.shape
     chunks, heads = rows // CHUNK, gamma.shape[0]
+    given = [] if into is None else [into]
     return pl.pallas_call(
         back_kernel,
         grid=(heads,),
         in_specs=[
-            columns(rows, DK, at), columns(rows, DK, held + at), columns(rows, DV, held + at), columns(rows, DV, 2 * held + at),
+            columns(rows, HEAD, at),
             whole((rows, CHUNK)), whole((8, rows)), whole((heads, rows)), per_head(rows),
-            columns(CONV, DK, at), columns(CONV, DK, held + at), columns(CONV, DV, held + at),
-            whole((1, DV)),
+            columns(CONV, TAPS, at), whole((1, DV)),
             columns(rows, DV, 0), columns(rows, DV, 0),
             pl.BlockSpec((1, chunks, CHUNK, CHUNK), lambda h: (h, 0, 0, 0)),
             pl.BlockSpec((1, chunks, DK, DV), lambda h: (h, 0, 0, 0)),
             columns(rows, DV, back_at),
-        ],
+        ] + [pl.BlockSpec(memory_space=pl.ANY)] * len(given),
         out_specs=[
-            columns(rows, DK, 0), columns(rows, DK, 0), columns(rows, DV, 0), columns(rows, DV, 0),
-            columns(CONV, DK, 0), columns(CONV, DK, 0), columns(CONV, DV, 0),
+            columns(rows, HEAD, at), columns(CONV, TAPS, 0),
             whole((1, DV)), whole((heads, rows)), per_head(rows),
         ],
         out_shape=[
-            jax.ShapeDtypeStruct((rows, heads * DK), BF),
-            jax.ShapeDtypeStruct((rows, heads * DK), BF),
-            jax.ShapeDtypeStruct((rows, heads * DV), BF),
-            jax.ShapeDtypeStruct((rows, heads * DV), BF),
-            jax.ShapeDtypeStruct((CONV, heads * DK), F32),
-            jax.ShapeDtypeStruct((CONV, heads * DK), F32),
-            jax.ShapeDtypeStruct((CONV, heads * DV), F32),
+            jax.ShapeDtypeStruct((rows, width), BF),
+            jax.ShapeDtypeStruct((CONV, heads * TAPS), F32),
             jax.ShapeDtypeStruct((1, DV), F32),
             jax.ShapeDtypeStruct((heads, rows), F32),
             jax.ShapeDtypeStruct((heads, 1, rows), F32),
@@ -394,9 +400,10 @@
             pltpu.VMEM((heads, 1, rows), F32),
             pltpu.VMEM((heads, 1, rows), F32),
         ],
+        input_output_aliases={12: 0} if given else {},
         compiler_params=pltpu.CompilerParams(vmem_limit_bytes=32 * 2**20),
         cost_estimate=pl.CostEstimate(flops=heads * int(6e9), bytes_accessed=heads * int(5e6), transcendentals=0),
-    )(projected, projected, projected, projected, seg, segrow, gamma, beta[:, None], taps, taps, taps, gain, out, fresh, inv, state, back)
+    )(projected, seg, segrow, gamma, beta[:, None], taps, gain, out, fresh, inv, state, back, *given)
 
 
 TILE = 256
@@ -500,9 +507,12 @@
     return lax.optimization_barrier((value,) + others)[0]
 
 
-def assemble_kernel(along, size, rows, at_ref, own_ref, *refs):
+def assemble_kernel(along, size, rows, cuts, at_ref, own_ref, *refs):
     pieces, whole_ref = refs[:-1], refs[-1]
-    whole_ref[pl.ds(pl.multiple_of(at_ref[0] * rows, 16), rows), :] = own_ref[...]
+    to = 0
+    for start, width in cuts:
+        whole_ref[pl.ds(pl.multiple_of(at_ref[0] * rows, 16), rows), to : to + width] = own_ref[:, start : start + width]
+        to += width
     n = 1
     for piece in pieces:
         for slot in range(piece.shape[0]):
@@ -515,13 +525,19 @@
 
 
 class Gather:
-    def __init__(self, weight, along):
-        self.weight, self.along = weight, along
-        self.size = weight.shape[along] // 8
+    def __init__(self, weight, along, cuts=None, blocks=None):
+        self.weight, self.along, self.blocks = weight, along, blocks
+        self.cuts = cuts or [(0, weight.shape[1])]
+        self.width = sum(width for _, width in self.cuts)
+        self.size = (weight.shape[0], self.width)[along] // 8
 
     def deep(self, *tokens):
         core, a, b = place()
-        mine = lax.dynamic_slice_in_dim(self.weight, (core * 4 + a * 2 + b) * self.size, self.size, self.along)
+        part = core * 4 + a * 2 + b
+        if self.blocks is None:
+            mine = lax.dynamic_slice_in_dim(self.weight, part * self.size, self.size, self.along)
+        else:
+            mine = jnp.concatenate([pick(self.weight, n, 128, 1) for n in self.blocks(part)], axis=1)
         mine = after(mine, *tokens)
         self.raw = [shift(mine, by) for by in range(1, lax.axis_size("shard"))]
 
@@ -550,10 +566,10 @@
             for flip in flips:
                 for block in blocks:
                     at += [block, home ^ flip]
-        rows, width = self.weight.shape
+        rows, width = self.weight.shape[0], self.width
         pieces = [self.pair, self.others_in, self.pair_core, after(self.others_core, *tokens)]
         return pl.pallas_call(
-            functools.partial(assemble_kernel, self.along, self.size, rows),
+            functools.partial(assemble_kernel, self.along, self.size, rows, self.cuts),
             in_specs=[pl.BlockSpec(memory_space=pltpu.SMEM)] + [pl.BlockSpec(memory_space=pltpu.VMEM)] * 5,
             out_specs=pl.BlockSpec(memory_space=pltpu.VMEM),
             compiler_params=pltpu.CompilerParams(vmem_limit_bytes=48 * 2**20),
@@ -692,10 +708,10 @@
     return found
 
 
-def share_small(arrays):
+def share_small(arrays, *tokens):
     count = lax.axis_size("shard")
     z = lax.axis_index("shard")
-    flat = jnp.concatenate([as_rows(x, 1) for x in arrays], axis=1)
+    flat = after(jnp.concatenate([as_rows(x, 1) for x in arrays], axis=1), *tokens)
     every = jnp.zeros((count,) + flat.shape[1:], F32)
     every = lax.dynamic_update_slice_in_dim(every, flat, z, 0)
     for by in range(1, count):
@@ -740,14 +756,21 @@
 STEPS = 4
 
 
-def group_columns(x, g):
-    wide, deep = KEYS // GROUPS, VALS // GROUPS
-    cuts = [x[:, n * KEYS + g * wide : n * KEYS + (g + 1) * wide] for n in (0, 1)]
-    start = 2 * KEYS
-    while start < x.shape[1]:
-        cuts.append(x[:, start + g * deep : start + (g + 1) * deep])
-        start += VALS
-    return jnp.concatenate(cuts, axis=1)
+def group_cuts(g):
+    cuts = []
+    for h in range(g * HEADS // GROUPS, (g + 1) * HEADS // GROUPS):
+        cuts += [(h * DK, DK), (KEYS + h * DK, DK), (2 * KEYS + h * DV, DV), (2 * KEYS + VALS + h * DV, DV)]
+    return cuts
+
+
+def group_blocks(g, part):
+    each, found = HEAD * HEADS // GROUPS // 8 // 128, []
+    for n in range(each):
+        block = (part + 8 * g) * each + n
+        head, slot = block // (HEAD // 128), block % (HEAD // 128)
+        to = jnp.where(slot < 2, slot * HEADS + head, 2 * HEADS + 2 * head + slot - 2)
+        found.append(jnp.where(slot < 4, to, 4 * HEADS + 2 * head + slot - 4))
+    return found
 
 
 def mix_final_kernel(blocks, at_ref, *refs):
@@ -782,17 +805,20 @@
     cotangent,
 ):
     rows = hidden_in.shape[0]
-    small = share_small([norm_gains, decay_params, conv_weight, out_gain[None], w_decay])
-    gains, rates, taps, gain_row = (beside(x) for x in small[:4])
-    decay_full = small[4].reshape(-1, 2 * HEADS).astype(BF)
-
-    ga, gb = (Gather(group_columns(w_mix_in, g), 1) for g in range(GROUPS))
+    ga, gb = (
+        Gather(w_mix_in, 1, group_cuts(g), functools.partial(group_blocks, g)) for g in range(GROUPS)
+    )
     go, gu, gd = Gather(w_mix_out, 1), Gather(w_gate_up, 0), Gather(w_down, 1)
     ga.deep()
     ga.first()
-    ga.second()
-    ga.core()
-    gb.deep(ga.others)
+    gb.deep(*ga.raw)
+    ga.second(*gb.raw)
+    go.deep(*gb.raw)
+    ga.core(*go.raw)
+
+    small = share_small([norm_gains, decay_params, conv_weight, out_gain[None], w_decay], ga.raw[0])
+    gains, rates, taps, gain_row = (beside(x) for x in small[:4])
+    decay_full = small[4].reshape(-1, 2 * HEADS).astype(BF)
 
     hidden = hidden_in.astype(F32)
     normed_one_f, norm_one_pull = jax.vjp(rms_scale, hidden, gains[0])
@@ -803,14 +829,16 @@
     beta = jax.nn.sigmoid(logits[HEADS:])
     seg = jnp.broadcast_to(segment_ids[:, None], (rows, CHUNK))
     segrow = jnp.broadcast_to(segment_ids[None], (8, rows))
-    tap_groups = [group_columns(taps, g) for g in range(GROUPS)]
+    cuts = (taps[:, :KEYS], taps[:, KEYS : 2 * KEYS], taps[:, 2 * KEYS :])
+    by_head = jnp.concatenate([x.reshape(CONV, HEADS, -1) for x in cuts], axis=2).reshape(CONV, -1)
+    tap_groups = jnp.split(by_head, GROUPS, axis=1)
     heads = HEADS // STEPS
 
     mix_in = [ga.full(), None]
     gb.first(mix_in[0])
     projected = [dot_nn(normed_one, mix_in[0]), None]
     gb.second(projected[0])
-    go.deep(projected[0], *gb.raw)
+    gu.deep(mix_in[0])
     kept = []
 
     def mix(n, *tokens):
@@ -822,18 +850,17 @@
 
     done = mix(0)
     gb.core(done)
-    gu.deep(done, *go.raw)
-    done = mix(1)
+    done = mix(1, gu.raw[0])
     mix_in[1] = gb.full(done)
     go.first(done)
-    projected[1] = dot_nn(after(normed_one, done), mix_in[1])
+    projected[1] = dot_nn(after(normed_one, done, gu.raw[1]), mix_in[1])
     go.second(projected[1])
     gu.first(projected[1])
     gd.deep(projected[1], *gu.raw)
     done = mix(2, gu.here, go.pair)
     gu.second(done)
     go.core(done)
-    done = mix(3, gu.pair, *gd.raw)
+    done = mix(3, gu.pair, gd.raw[0])
     gd.first(done)
     mix_out = go.full()
     mixed_out = jnp.concatenate([x[0] for x in kept], axis=1)
@@ -869,20 +896,19 @@
         g, at = n * GROUPS // STEPS, n % (STEPS // GROUPS) * heads
         span = slice(n * heads, (n + 1) * heads)
         gate = after(gamma[span], *tokens)
+        into = backs[-1][0] if at else None
         backs.append(
-            mixer_back(projected[g], at, seg, segrow, gate, beta[span], tap_groups[g], gain_row, *kept[n][1:], mixed_back, n * heads)
+            mixer_back(
+                projected[g], at, seg, segrow, gate, beta[span], tap_groups[g], gain_row, *kept[n][1:], mixed_back, n * heads, into
+            )
         )
         return backs[-1][0]
-
-    def group_back(g):
-        each = STEPS // GROUPS
-        return jnp.concatenate([x[n] for n in range(4) for x in backs[g * each : (g + 1) * each]], axis=1)
 
     done = mix_back(0, t_gu.sent, t_out.given)
     t_out.first(done)
     t_down.second(done)
     done = mix_back(1, t_out.sent, t_down.passed)
-    back_a = group_back(0)
+    back_a = done
     t_a = Total(normed_one, back_a)
     t_a.core(done)
     t_down.deep(done)
@@ -892,25 +918,25 @@
     t_out.second(t_a.sent)
     done = mix_back(3, t_a.sent, t_out.passed)
     t_down.finish(done)
-    t_gu.deep(done)
-    back_b = group_back(1)
+    back_b = done
     t_b = Total(normed_one, back_b)
-    t_b.core(t_gu.kept)
-    t_out.deep(t_b.given)
-    dgain = sum(x[7] for x in backs)
-    dgamma = jnp.concatenate([x[8] for x in backs], axis=0)
-    dbeta = jnp.concatenate([x[9][:, 0] for x in backs], axis=0)
+    t_b.core(done)
+    t_gu.deep(t_b.given)
+    t_out.deep(t_gu.kept)
+    dgain = sum(x[2] for x in backs)
+    dgamma = jnp.concatenate([x[3] for x in backs], axis=0)
+    dbeta = jnp.concatenate([x[4][:, 0] for x in backs], axis=0)
     slope = -dgamma * rate * jax.nn.sigmoid(logits[:HEADS] + bias)
     logits_back = jnp.concatenate([slope, dbeta * beta * (1.0 - beta)], axis=0).astype(BF)
     grad_rates = jnp.stack([jnp.sum(dgamma * gamma, axis=1), jnp.sum(slope, axis=1)])
-    grad_taps = jnp.concatenate([x[n] for n in (4, 5, 6) for x in backs], axis=1)
+    by_head = jnp.concatenate([x[1] for x in backs], axis=1).reshape(CONV, HEADS, TAPS)
+    cuts = (by_head[:, :, :DK], by_head[:, :, DK : 2 * DK], by_head[:, :, 2 * DK :])
+    grad_taps = jnp.concatenate([x.reshape(CONV, -1) for x in cuts], axis=1)
     grad_decay = lax.dot_general(normed_one, logits_back, (((0,), (1,)), ((), ())), preferred_element_type=F32)
-    near = dot_nt(after(back_a, t_b.given), mix_in[0]) + lax.dot_general(
-        logits_back, decay_full, (((0,), (1,)), ((), ())), preferred_element_type=F32
-    )
-    t_b.first(near)
-    near = near + dot_nt(after(back_b, t_b.sent), mix_in[1])
-    t_a.second(t_b.sent)
+    t_b.first()
+    near = lax.dot_general(logits_back, decay_full, (((0,), (1,)), ((), ())), preferred_element_type=F32)
+    near = near + dot_nt(after(back_a, t_b.sent), mix_in[0]) + dot_nt(back_b, mix_in[1])
+    t_a.second(near)
     hidden_part, gain_one = norm_one_pull(after(near, t_a.passed))
     grad_in = residual_back + hidden_part
     t_b.second(gain_one)
@@ -933,7 +959,7 @@
     s_rest = Spread(merged)
     t_b.deep(s_rest.done)
     small_total.add(t_b.kept)
-    s_rest.first(t_b.kept)
+    s_rest.first(t_b.raw[0])
     t_a.finish(s_rest.pair)
     t_b.finish(s_rest.pair)
     s_mix = Spread(jnp.concatenate([t_a.done, t_b.done], axis=1))
@@ -960,16 +986,9 @@
     parts = small_total.finish()
     each = t_a.done.shape[1] // 128
     copies, at = [], []
-    edge, wide, tall = 0, KEYS // GROUPS // 128, VALS // GROUPS // 128
     for part in numbers:
         for g in range(GROUPS):
-            for n in range(each):
-                block = part * each + n
-                to = block + g * wide
-                to = jnp.where(block >= wide, block - wide + KEYS // 128 + g * wide, to)
-                to = jnp.where(block >= 2 * wide, block - 2 * wide + 2 * KEYS // 128 + g * tall, to)
-                to = jnp.where(block >= 2 * wide + tall, block - 2 * wide - tall + (2 * KEYS + VALS) // 128 + g * tall, to)
-                at.append(to)
+            at += group_blocks(g, part)
     pieces = s_mix.parts()
     grad_mix_in = finish_mix(pieces, GROUPS * each, at, w_mix_in.shape)
     return (

time: 599 us -> 569 us (0.950)
  local copies, waits for them, and re-layouts: 90.5 us -> 65.1 us
  starting transfers between devices: 97.3 us -> 112 us
  waiting for transfers between devices: 117 us -> 105 us
  matrix products: 91.7 us -> 80.8 us
    ppermute x44, waiting for transfers between devices: 79.2 us -> 53.7 us  [hop(): return lax.ppermute(value, 'rep', pairs)]
    ppermute x36, starting transfers between devices: 63.9 us -> 81.6 us  [shift(): lax.ppermute(value, 'shard', [(i, (i + by) % count) for i in range(count)])]
    unnamed x312 -> x304, local copies, waits for them, and re-layouts: 45.9 us -> 28.6 us
    ppermute x36, waiting for transfers between devices: 37.6 us -> 50.9 us  [shift(): lax.ppermute(value, 'shard', [(i, (i + by) % count) for i in range(count)])]
    dot_general x15, matrix products: 54.6 us -> 48 us  [dot_tn(): lax.dot_general(a, b, (((0,), (0,)), ((), ())), preferred_element_type=F32)]
  transfers between devices with their start and end apart: 80 -> 80, of which waited for: 25 -> 25; matrix products, arithmetic and copies ran while one was open for 30% -> 27% of each run, Pallas kernels for 21% -> 21%
where the time goes in v3:
time: 569 us; the launch traced here: 562 us
  Pallas kernels  149 us (26%)
  starting transfers between devices  112 us (20%)
  waiting for transfers between devices  105 us (18%)
  matrix products  80.8 us (14%)
  local copies, waits for them, and re-layouts  65.1 us (11%)
  other arithmetic  46.4 us (8%)
    ppermute x36, starting transfers between devices, shift(): lax.ppermute(value, 'shard', [(i, (i + by) % count) for i in range(count)])  81.6 us
    ppermute x44, waiting for transfers between devices, hop(): return lax.ppermute(value, 'rep', pairs)  53.7 us
    ppermute x36, waiting for transfers between devices, shift(): lax.ppermute(value, 'shard', [(i, (i + by) % count) for i in range(count)])  50.9 us
    dot_general x15, matrix products, dot_tn(): lax.dot_general(a, b, (((0,), (0,)), ((), ())), preferred_element_type=F32)  48 us
    pallas_call x4, Pallas kernels, mixer_back(): pl.pallas_call(back_kernel, grid=(heads,), in_specs=[columns(rows, HEAD,...  45.4 us
    pallas_call x4, Pallas kernels, mixer(): pl.pallas_call(mix_kernel, grid=(heads,), in_specs=[columns(rows, HEAD, a...  37.8 us
    ppermute x44, starting transfers between devices, hop(): return lax.ppermute(value, 'rep', pairs)  30.7 us
    unnamed x304, local copies, waits for them, and re-layouts  28.6 us
  transfers between devices with their start and end apart: 80, of which 25 were waited for; matrix products, arithmetic and copies ran while one was open for 27% of the time, Pallas kernels for 21%

profile of v3, /device:TPU:0, one launch (start us, length us, event | category | flops | bytes accessed | tf_op | source)
XLA Modules:
  0.0 562.3 jit_solution(11889839569684691934)
XLA Ops:
  89.5 9.5 %shard_map.204 = (bf16[512,512]{1,0:T(8,128)(2,1)S(1)}, f32[512,512]{1,0:T(8,128)S(1)}, bf16[512,512]{1,0:T(8,128)(2,1)S(1)}, bf16[2,4,128,128]{3,2,1,0:T(8,128)(2,1)S(1)}, bf16[2,4,128,256]{3,2,1,0:T(8,128)(2,1)S(1)}) custom-call(f32[512,3072]{1,0:T(8,128)S(1)} %fusion.100.x_ref, s32[512,128]{1,0:T(8,128)S(1)} %broadcast_in_dim.22.seg_ref, ...), custom_call_target="tpu_custom_call" | custom-call | flops 10000000000 | bytes 8000000 | tf_op jit(solution)/shard_map/pallas_call | solution.py:203
  102.8 9.4 %shard_map.205 = (bf16[512,512]{1,0:T(8,128)(2,1)S(1)}, f32[512,512]{1,0:T(8,128)S(1)}, bf16[512,512]{1,0:T(8,128)(2,1)S(1)}, bf16[2,4,128,128]{3,2,1,0:T(8,128)(2,1)S(1)}, bf16[2,4,128,256]{3,2,1,0:T(8,128)(2,1)S(1)}) custom-call(f32[512,3072]{1,0:T(8,128)S(1)} %fusion.100.x_ref, s32[512,128]{1,0:T(8,128)S(1)} %broadcast_in_dim.22.seg_ref, ...), custom_call_target="tpu_custom_call" | custom-call | flops 10000000000 | bytes 8000000 | tf_op jit(solution)/shard_map/pallas_call | solution.py:203
  132.0 9.8 %collective-permute-start.25 = (bf16[704,128]{1,0:T(8,128)(2,1)S(1)}, bf16[704,128]{1,0:T(8,128)(2,1)S(1)}, u32[]{:S(2)}, u32[]{:S(2)}) collective-permute-start(bf16[704,128]{1,0:T(8,128)(2,1)S(1)} %copy-done.108), channel_id=1, source_target_pairs={{0,1},{1,2},{2,3},{3,0},{4,5},{5,6},{6,7},{7,4},{8,9},{9,10},{10,1... | collective-permute-start | bytes 540680 | tf_op jit(solution)/shard_map/ppermute | solution.py:501
  141.9 9.4 %shard_map.207 = (bf16[512,512]{1,0:T(8,128)(2,1)S(1)}, f32[512,512]{1,0:T(8,128)S(1)}, bf16[512,512]{1,0:T(8,128)(2,1)S(1)}, bf16[2,4,128,128]{3,2,1,0:T(8,128)(2,1)S(1)}, bf16[2,4,128,256]{3,2,1,0:T(8,128)(2,1)S(1)}) custom-call(f32[512,3072]{1,0:T(8,128)S(1)} %fusion.102.x_ref, s32[512,128]{1,0:T(8,128)S(1)} %broadcast_in_dim.22.seg_ref, ...), custom_call_target="tpu_custom_call" | custom-call | flops 10000000000 | bytes 8000000 | tf_op jit(solution)/shard_map/pallas_call | solution.py:203
  156.3 9.5 %shard_map.208 = (bf16[512,512]{1,0:T(8,128)(2,1)S(1)}, f32[512,512]{1,0:T(8,128)S(1)}, bf16[512,512]{1,0:T(8,128)(2,1)S(1)}, bf16[2,4,128,128]{3,2,1,0:T(8,128)(2,1)S(1)}, bf16[2,4,128,256]{3,2,1,0:T(8,128)(2,1)S(1)}) custom-call(f32[512,3072]{1,0:T(8,128)S(1)} %fusion.102.x_ref, s32[512,128]{1,0:T(8,128)S(1)} %broadcast_in_dim.22.seg_ref, ...), custom_call_target="tpu_custom_call" | custom-call | flops 10000000000 | bytes 8000000 | tf_op jit(solution)/shard_map/pallas_call | solution.py:203
  181.1 11.6 %collective-permute-start.29 = (bf16[704,128]{1,0:T(8,128)(2,1)S(1)}, bf16[704,128]{1,0:T(8,128)(2,1)S(1)}, u32[]{:S(2)}, u32[]{:S(2)}) collective-permute-start(bf16[704,128]{1,0:T(8,128)(2,1)S(1)} %copy-done.109), channel_id=1, source_target_pairs={{0,2},{1,3},{2,0},{3,1},{4,6},{5,7},{6,4},{7,5},{8,10},{9,11},{10,... | collective-permute-start | bytes 540680 | tf_op jit(solution)/shard_map/ppermute | solution.py:501
  193.6 8.4 %collective-permute-done.29 = bf16[704,128]{1,0:T(8,128)(2,1)S(1)} collective-permute-done((bf16[704,128]{1,0:T(8,128)(2,1)S(1)}, bf16[704,128]{1,0:T(8,128)(2,1)S(1)}, u32[]{:S(2)}, u32[]{:S(2)}) %collective-permute-start.29) | collective-permute-done | bytes 180256 | tf_op jit(solution)/shard_map/ppermute | solution.py:501
  205.7 8.1 %shard_map.210.gate_w_ref.up_w_ref = bf16[1024,5632]{1,0:T(8,128)(2,1)} custom-call(s32[49]{0:T(128)S(1)} %stack.394.at_ref, bf16[256,5632]{1,0:T(8,128)(2,1)} %own_ref.8, bf16[6,32,5632]{2,1,0:T(8,128)(2,1)S(1)} %pad_maximum_fusion.1.refs_0_, bf16[6,32,5632]{2,1,0:T(8,128)(2,1)S(1)} %collective-permute-done.32.refs_1_, ...), custom_call_target="tpu_custom_call" | custom-call | tf_op jit(solution)/shard_map/pallas_call | solution.py:571
  218.4 9.5 %shard_map.211 = (bf16[512,2816]{1,0:T(8,128)(2,1)S(1)}, bf16[512,2816]{1,0:T(8,128)(2,1)S(1)}, bf16[512,2816]{1,0:T(8,128)(2,1)S(1)}) custom-call(bf16[512,1024]{1,0:T(8,128)(2,1)S(1)} %multiply_convert_fusion.x_ref, bf16[1024,5632]{1,0:T(8,128)(2,1)S(1)} %copy-done, bf16[1024,5632]{1,0:T(8,128)(2,1)S(1)} %copy-done), custom_call_target="tpu_custom_call" | custom-call | flops 5905580032 | bytes 11534336 | tf_op jit(solution)/shard_map/pallas_call | solution.py:423
  238.4 6.0 %shard_map.212.down_w_ref = bf16[2816,1024]{1,0:T(8,128)(2,1)} custom-call(s32[49]{0:T(128)S(1)} %stack.394.at_ref, bf16[704,1024]{1,0:T(8,128)(2,1)S(1)} %copy-done.8, bf16[6,704,128]{2,1,0:T(8,128)(2,1)S(1)} %pad_maximum_fusion.7.refs_0_, bf16[6,704,128]{2,1,0:T(8,128)(2,1)} %collective-permute-done.35.refs_1_, ...), custom_call_target="tpu_custom_call" | custom-call | tf_op jit(solution)/shard_map/pallas_call | solution.py:571
  248.0 18.2 %shard_map.213 = (bf16[2,512,2816]{2,1,0:T(8,128)(2,1)S(1)}, f32[512,1024]{1,0:T(8,128)S(1)}, f32[512,1024]{1,0:T(8,128)S(1)}) custom-call(bf16[512,1024]{1,0:T(8,128)(2,1)S(1)} %copy-done.1, bf16[512,2816]{1,0:T(8,128)(2,1)S(1)} %copy-done.16, bf16[512,2816]{1,0:T(8,128)(2,1)S(1)} %copy-done.18, bf16[512,2816]{1,0:T(8,128)(2,1)S(1)} %copy-done.13, ...), custom_call_target="tpu_custom_call" | custom-call | flops 11811160064 | bytes 17301504 | tf_op jit(solution)/shard_map/pallas_call | solution.py:455
  272.7 6.0 %fusion.15 = f32[1024,1408]{1,0:T(8,128)} fusion(bf16[512,1024]{1,0:T(8,128)(2,1)S(1)} %multiply_convert_fusion.x_ref, bf16[2,512,2816]{2,1,0:T(8,128)(2,1)} %copy-done.11, s32[]{:T(128)S(6)} %select_n.1482, s32[]{:T(128)S(6)} %select_n.1495), kind=kOutput, calls=%fused_computation.49 | convolution fusion | flops 1476395008 | bytes 8257544 | tf_op jit(solution)/shard_map/dot_general | solution.py:34
  278.7 6.7 %collective-permute-done.38 = bf16[2816,512]{1,0:T(8,128)(2,1)} collective-permute-done((bf16[2816,512]{1,0:T(8,128)(2,1)}, bf16[2816,512]{1,0:T(8,128)(2,1)}, u32[]{:S(2)}, u32[]{:S(2)}) %collective-permute-start.38) | collective-permute-done | bytes 2883616 | tf_op jit(solution)/shard_map/ppermute | solution.py:496
  303.2 11.3 %shard_map.214 = (bf16[512,3072]{1,0:T(8,128)(2,1)S(1)}, f32[4,1024]{1,0:T(4,128)S(1)}, f32[1,256]{1,0:T(1,128)S(1)}, f32[2,512]{1,0:T(2,128)S(1)}, f32[2,1,512]{2,1,0:T(1,128)S(1)}) custom-call(f32[512,3072]{1,0:T(8,128)S(1)} %bitcast.397, s32[512,128]{1,0:T(8,128)S(1)} %broadcast_in_dim.22.seg_ref, s32[8,512]{1,0:T(8,128)S(1)} %broadcast_in_dim.46.segrow_ref, ...), custom_call_target="tpu_custom_call" | custom-call | flops 12000000000 | bytes 10000000 | tf_op jit(solution)/shard_map/pallas_call | solution.py:375
  320.3 11.4 %shard_map.215 = (bf16[512,3072]{1,0:T(8,128)(2,1)S(1)}, f32[4,1024]{1,0:T(4,128)S(1)}, f32[1,256]{1,0:T(1,128)S(1)}, f32[2,512]{1,0:T(2,128)S(1)}, f32[2,1,512]{2,1,0:T(1,128)S(1)}) custom-call(f32[512,3072]{1,0:T(8,128)S(1)} %bitcast.397, s32[512,128]{1,0:T(8,128)S(1)} %broadcast_in_dim.22.seg_ref, ...), custom_call_target="tpu_custom_call", output_to_operand_aliasing={{0}: (12, {})} | custom-call | flops 12000000000 | bytes 10000000 | tf_op jit(solution)/shard_map/pallas_call | solution.py:375
  337.9 11.5 %shard_map.216 = (bf16[512,3072]{1,0:T(8,128)(2,1)S(1)}, f32[4,1024]{1,0:T(4,128)S(1)}, f32[1,256]{1,0:T(1,128)S(1)}, f32[2,512]{1,0:T(2,128)S(1)}, f32[2,1,512]{2,1,0:T(1,128)S(1)}) custom-call(f32[512,3072]{1,0:T(8,128)S(1)} %bitcast.395, s32[512,128]{1,0:T(8,128)S(1)} %broadcast_in_dim.22.seg_ref, s32[8,512]{1,0:T(8,128)S(1)} %broadcast_in_dim.46.segrow_ref, ...), custom_call_target="tpu_custom_call" | custom-call | flops 12000000000 | bytes 10000000 | tf_op jit(solution)/shard_map/pallas_call | solution.py:375
  357.8 6.8 %add_convert_fusion = bf16[1024,1408]{1,0:T(8,128)(2,1)} fusion(bf16[1024,1408]{1,0:T(8,128)(2,1)} %collective-permute-done.44, f32[1024,1408]{1,0:T(8,128)} %fusion.15, bf16[1024,2816]{1,0:T(8,128)(2,1)} %collective-permute-done.39, s32[]{:T(128)S(6)} %select_n.1494), kind=kLoop, calls=%fused_computation | loop fusion | flops 7208960 | bytes 14417924 | tf_op jit(solution)/shard_map/convert_element_type | solution.py:618
  374.0 11.2 %shard_map.217 = (bf16[512,3072]{1,0:T(8,128)(2,1)S(1)}, f32[4,1024]{1,0:T(4,128)S(1)}, f32[1,256]{1,0:T(1,128)S(1)}, f32[2,512]{1,0:T(2,128)S(1)}, f32[2,1,512]{2,1,0:T(1,128)S(1)}) custom-call(f32[512,3072]{1,0:T(8,128)S(1)} %bitcast.395, s32[512,128]{1,0:T(8,128)S(1)} %broadcast_in_dim.22.seg_ref, ...), custom_call_target="tpu_custom_call", output_to_operand_aliasing={{0}: (12, {})} | custom-call | flops 12000000000 | bytes 10000000 | tf_op jit(solution)/shard_map/pallas_call | solution.py:375
  396.5 6.8 %collective-permute-done.56 = bf16[4,512,128]{2,1,0:T(8,128)(2,1)S(1)} collective-permute-done((bf16[4,512,128]{2,1,0:T(8,128)(2,1)}, bf16[4,512,128]{2,1,0:T(8,128)(2,1)S(1)}, u32[]{:S(2)}, u32[]{:S(2)}) %collective-permute-start.56) | collective-permute-done | bytes 524320 | tf_op jit(solution)/shard_map/ppermute | solution.py:496
  414.0 7.9 %add_add_fusion.2 = f32[512,1024]{1,0:T(8,128)} fusion(f32[512,1024]{1,0:T(8,128)S(1)} %fusion.84, f32[512,1024]{1,0:T(8,128)} %fusion.104, bf16[512,3072]{1,0:T(8,128)(2,1)S(1)} %get-tuple-element.236, bf16[1024,3072]{1,0:T(8,128)(2,1)} %shard_map.206), kind=kOutput, calls=%fused_computation.36 | convolution fusion | flops 3222274048 | bytes 15728640 | tf_op jit(solution)/shard_map/dot_general | solution.py:30
  444.7 14.9 %collective-permute-done.52 = bf16[4,256,384]{2,1,0:T(8,128)(2,1)S(1)} collective-permute-done((bf16[4,256,384]{2,1,0:T(8,128)(2,1)S(1)}, bf16[4,256,384]{2,1,0:T(8,128)(2,1)S(1)}, u32[]{:S(2)}, u32[]{:S(2)}) %collective-permute-start.52) | collective-permute-done | bytes 786464 | tf_op jit(solution)/shard_map/ppermute | solution.py:496
  488.4 10.0 %collective-permute-done.71 = bf16[256,384]{1,0:T(8,128)(2,1)} collective-permute-done((bf16[256,384]{1,0:T(8,128)(2,1)}, bf16[256,384]{1,0:T(8,128)(2,1)}, u32[]{:S(2)}, u32[]{:S(2)}) %collective-permute-start.71) | collective-permute-done | bytes 196640 | tf_op jit(solution)/shard_map/ppermute | solution.py:501
  498.8 8.0 %collective-permute-done.72 = bf16[256,384]{1,0:T(8,128)(2,1)} collective-permute-done((bf16[256,384]{1,0:T(8,128)(2,1)}, bf16[256,384]{1,0:T(8,128)(2,1)}, u32[]{:S(2)}, u32[]{:S(2)}) %collective-permute-start.72) | collective-permute-done | bytes 196640 | tf_op jit(solution)/shard_map/ppermute | solution.py:501
  541.2 6.0 %shard_map.218 = (f32[704,1024]{1,0:T(8,128)}, f32[512,1024]{1,0:T(8,128)}, f32[256,5632]{1,0:T(8,128)}) custom-call(s32[192]{0:T(256)S(1)} %stack.523.at_ref, bf16[2624,128]{1,0:T(8,128)(2,1)S(1)} %constant_dynamic-update-slice_fusion.18.refs_0_, bf16[2624,128]{1,0:T(8,128)(2,1)S(1)} %collective-permute-done.69.refs_1_, ...), custom_call_target="tpu_custom_call" | custom-call | tf_op jit(solution)/shard_map/pallas_call | solution.py:682
  (625 shorter events, 330.2 us)
Async XLA Ops:
  86.8 26.4 %collective-permute-start.17 = (bf16[32,5632]{1,0:T(8,128)(2,1)}, bf16[32,5632]{1,0:T(8,128)(2,1)S(1)}, u32[]{:S(2)}, u32[]{:S(2)}) collective-permute-start(bf16[32,5632]{1,0:T(8,128)(2,1)} %constant_dynamic-slice_fusion.9), channel_id=1, source_target_pairs={{0,2},{1,3},{2,0},{3,1},{4,6},{5,7},{6,4},{7,5},{8,10},{9,11},{10,... | collective-permute-start | bytes 1081352 | tf_op jit(solution)/shard_map/ppermute | solution.py:501
  88.4 39.0 %collective-permute-start.22 = (bf16[32,5632]{1,0:T(8,128)(2,1)}, bf16[32,5632]{1,0:T(8,128)(2,1)}, u32[]{:S(2)}, u32[]{:S(2)}) collective-permute-start(bf16[32,5632]{1,0:T(8,128)(2,1)} %constant_dynamic-slice_fusion.9), channel_id=1, source_target_pairs={{0,3},{1,0},{2,1},{3,2},{4,7},{5,4},{6,5},{7,6},{8,11},{9,8},{10,9... | collective-permute-start | bytes 1081352 | tf_op jit(solution)/shard_map/ppermute | solution.py:501
  129.4 23.6 %collective-permute-start.24 = (bf16[3,32,5632]{2,1,0:T(8,128)(2,1)S(1)}, bf16[3,32,5632]{2,1,0:T(8,128)(2,1)S(1)}, u32[]{:S(2)}, u32[]{:S(2)}) collective-permute-start(bf16[3,32,5632]{2,1,0:T(8,128)(2,1)S(1)} %pad_maximum_fusion.6), channel_id=1, source_target_pairs={{0,8},{4,20},{8,0},{12,28},{16,24},{20,4},{24,16},{28,12},{1,9},{5... | collective-permute-start | bytes 3244040 | tf_op jit(solution)/shard_map/ppermute | solution.py:496
  132.0 36.2 %collective-permute-start.27 = (bf16[6,512,128]{2,1,0:T(8,128)(2,1)S(1)}, bf16[6,512,128]{2,1,0:T(8,128)(2,1)S(1)}, u32[]{:S(2)}, u32[]{:S(2)}) collective-permute-start(bf16[6,512,128]{2,1,0:T(8,128)(2,1)S(1)} %pad_maximum_fusion.8.refs_0_), channel_id=1, source_target_pairs={{0,4},{4,0},{8,12},{12,8},{16,20},{20,16},{24,28},{28,24},{1,5},{5... | collective-permute-start | bytes 2359304 | tf_op jit(solution)/shard_map/ppermute | solution.py:496
  132.0 24.2 %collective-permute-start.25 = (bf16[704,128]{1,0:T(8,128)(2,1)S(1)}, bf16[704,128]{1,0:T(8,128)(2,1)S(1)}, u32[]{:S(2)}, u32[]{:S(2)}) collective-permute-start(bf16[704,128]{1,0:T(8,128)(2,1)S(1)} %copy-done.108), channel_id=1, source_target_pairs={{0,1},{1,2},{2,3},{3,0},{4,5},{5,6},{6,7},{7,4},{8,9},{9,10},{10,1... | collective-permute-start | bytes 540680 | tf_op jit(solution)/shard_map/ppermute | solution.py:501
  154.3 26.8 %collective-permute-start.32 = (bf16[6,32,5632]{2,1,0:T(8,128)(2,1)S(1)}, bf16[6,32,5632]{2,1,0:T(8,128)(2,1)S(1)}, u32[]{:S(2)}, u32[]{:S(2)}) collective-permute-start(bf16[6,32,5632]{2,1,0:T(8,128)(2,1)S(1)} %pad_maximum_fusion.1.refs_0_), channel_id=1, source_target_pairs={{0,16},{4,12},{8,24},{12,4},{16,0},{20,28},{24,8},{28,20},{1,17},{... | collective-permute-start | bytes 6488072 | tf_op jit(solution)/shard_map/ppermute | solution.py:496
  156.2 48.1 %collective-permute-start.33 = (bf16[6,32,5632]{2,1,0:T(8,128)(2,1)S(1)}, bf16[6,32,5632]{2,1,0:T(8,128)(2,1)}, u32[]{:S(2)}, u32[]{:S(2)}) collective-permute-start(bf16[6,32,5632]{2,1,0:T(8,128)(2,1)S(1)} %pad_maximum_fusion.1.refs_0_), channel_id=1, source_target_pairs={{0,4},{4,0},{8,12},{12,8},{16,20},{20,16},{24,28},{28,24},{1,5},{5... | collective-permute-start | bytes 6488072 | tf_op jit(solution)/shard_map/ppermute | solution.py:496
  214.0 24.4 %collective-permute-start.36 = (bf16[6,704,128]{2,1,0:T(8,128)(2,1)S(1)}, bf16[6,704,128]{2,1,0:T(8,128)(2,1)}, u32[]{:S(2)}, u32[]{:S(2)}) collective-permute-start(bf16[6,704,128]{2,1,0:T(8,128)(2,1)S(1)} %pad_maximum_fusion.7.refs_0_), channel_id=1, source_target_pairs={{0,4},{4,0},{8,12},{12,8},{16,20},{20,16},{24,28},{28,24},{1,5},{5... | collective-permute-start | bytes 3244040 | tf_op jit(solution)/shard_map/ppermute | solution.py:496
  287.8 26.7 %collective-permute-start.41 = (bf16[2816,256]{1,0:T(8,128)(2,1)S(1)}, bf16[2816,256]{1,0:T(8,128)(2,1)S(1)}, u32[]{:S(2)}, u32[]{:S(2)}) collective-permute-start(bf16[2816,256]{1,0:T(8,128)(2,1)S(1)} %fusion.2), channel_id=1, source_target_pairs={{0,8},{4,20},{8,0},{12,28},{16,24},{20,4},{24,16},{28,12},{1,9},{5... | collective-permute-start | bytes 4325384 | tf_op jit(solution)/shard_map/ppermute | solution.py:496
  299.7 56.2 %collective-permute-start.44 = (bf16[1024,1408]{1,0:T(8,128)(2,1)}, bf16[1024,1408]{1,0:T(8,128)(2,1)}, u32[]{:S(2)}, u32[]{:S(2)}) collective-permute-start(bf16[1024,1408]{1,0:T(8,128)(2,1)} %add_convert_fusion.1), channel_id=1, source_target_pairs={{0,8},{4,20},{8,0},{12,28},{16,24},{20,4},{24,16},{28,12},{1,9},{5... | collective-permute-start | bytes 8650760 | tf_op jit(solution)/shard_map/ppermute | solution.py:496
  335.3 30.8 %collective-permute-start.43 = (bf16[1024,1536]{1,0:T(8,128)(2,1)}, bf16[1024,1536]{1,0:T(8,128)(2,1)}, u32[]{:S(2)}, u32[]{:S(2)}) collective-permute-start(bf16[1024,1536]{1,0:T(8,128)(2,1)} %convolution_convert_fusion.3), channel_id=1, source_target_pairs={{0,4},{4,0},{8,12},{12,8},{16,20},{20,16},{24,28},{28,24},{1,5},{5... | collective-permute-start | bytes 9437192 | tf_op jit(solution)/shard_map/ppermute | solution.py:496
  336.2 34.6 %collective-permute-start.45 = (bf16[2048,256]{1,0:T(8,128)(2,1)}, bf16[2048,256]{1,0:T(8,128)(2,1)}, u32[]{:S(2)}, u32[]{:S(2)}) collective-permute-start(bf16[2048,256]{1,0:T(8,128)(2,1)} %add_convert_fusion.8), channel_id=1, source_target_pairs={{0,8},{4,20},{8,0},{12,28},{16,24},{20,4},{24,16},{28,12},{1,9},{5... | collective-permute-start | bytes 3145736 | tf_op jit(solution)/shard_map/ppermute | solution.py:496
  349.5 37.8 %collective-permute-start.53 = (bf16[704,128]{1,0:T(8,128)(2,1)S(1)}, bf16[704,128]{1,0:T(8,128)(2,1)S(1)}, u32[]{:S(2)}, u32[]{:S(2)}) collective-permute-start(bf16[704,128]{1,0:T(8,128)(2,1)S(1)} %get-tuple-element.337), channel_id=1, source_target_pairs={{0,1},{1,2},{2,3},{3,0},{4,5},{5,6},{6,7},{7,4},{8,9},{9,10},{10,1... | collective-permute-start | bytes 540680 | tf_op jit(solution)/shard_map/ppermute | solution.py:501
  352.6 35.7 %collective-permute-start.54 = (bf16[704,128]{1,0:T(8,128)(2,1)S(1)}, bf16[704,128]{1,0:T(8,128)(2,1)}, u32[]{:S(2)}, u32[]{:S(2)}) collective-permute-start(bf16[704,128]{1,0:T(8,128)(2,1)S(1)} %get-tuple-element.336), channel_id=1, source_target_pairs={{0,2},{1,3},{2,0},{3,1},{4,6},{5,7},{6,4},{7,5},{8,10},{9,11},{10,... | collective-permute-start | bytes 540680 | tf_op jit(solution)/shard_map/ppermute | solution.py:501
  355.8 33.8 %collective-permute-start.55 = (bf16[704,128]{1,0:T(8,128)(2,1)S(1)}, bf16[704,128]{1,0:T(8,128)(2,1)}, u32[]{:S(2)}, u32[]{:S(2)}) collective-permute-start(bf16[704,128]{1,0:T(8,128)(2,1)S(1)} %get-tuple-element.335), channel_id=1, source_target_pairs={{0,3},{1,0},{2,1},{3,2},{4,7},{5,4},{6,5},{7,6},{8,11},{9,8},{10,9... | collective-permute-start | bytes 540680 | tf_op jit(solution)/shard_map/ppermute | solution.py:501
  366.1 23.6 %collective-permute-start.57 = (bf16[4,128,1408]{2,1,0:T(8,128)(2,1)S(1)}, bf16[4,128,1408]{2,1,0:T(8,128)(2,1)S(1)}, u32[]{:S(2)}, u32[]{:S(2)}) collective-permute-start(bf16[4,128,1408]{2,1,0:T(8,128)(2,1)S(1)} %constant_dynamic-slice_fusion.6), channel_id=1, source_target_pairs={{0,16},{4,12},{8,24},{12,4},{16,0},{20,28},{24,8},{28,20},{1,17},{... | collective-permute-start | bytes 4325384 | tf_op jit(solution)/shard_map/ppermute | solution.py:496
  387.4 34.5 %collective-permute-start.47 = (bf16[1024,768]{1,0:T(8,128)(2,1)}, bf16[1024,768]{1,0:T(8,128)(2,1)}, u32[]{:S(2)}, u32[]{:S(2)}) collective-permute-start(bf16[1024,768]{1,0:T(8,128)(2,1)} %add_convert_fusion.5), channel_id=1, source_target_pairs={{0,8},{4,20},{8,0},{12,28},{16,24},{20,4},{24,16},{28,12},{1,9},{5... | collective-permute-start | bytes 4718600 | tf_op jit(solution)/shard_map/ppermute | solution.py:496
  390.9 51.2 %collective-permute-start.61 = (bf16[128,1408]{1,0:T(8,128)(2,1)}, bf16[128,1408]{1,0:T(8,128)(2,1)}, u32[]{:S(2)}, u32[]{:S(2)}) collective-permute-start(bf16[128,1408]{1,0:T(8,128)(2,1)} %get-tuple-element.324), channel_id=1, source_target_pairs={{0,1},{1,2},{2,3},{3,0},{4,5},{5,6},{6,7},{7,4},{8,9},{9,10},{10,1... | collective-permute-start | bytes 1081352 | tf_op jit(solution)/shard_map/ppermute | solution.py:501
  391.0 51.2 %collective-permute-start.62 = (bf16[128,1408]{1,0:T(8,128)(2,1)S(1)}, bf16[128,1408]{1,0:T(8,128)(2,1)}, u32[]{:S(2)}, u32[]{:S(2)}) collective-permute-start(bf16[128,1408]{1,0:T(8,128)(2,1)S(1)} %get-tuple-element.323), channel_id=1, source_target_pairs={{0,2},{1,3},{2,0},{3,1},{4,6},{5,7},{6,4},{7,5},{8,10},{9,11},{10,... | collective-permute-start | bytes 1081352 | tf_op jit(solution)/shard_map/ppermute | solution.py:501
  403.4 38.8 %collective-permute-start.63 = (bf16[128,1408]{1,0:T(8,128)(2,1)S(1)}, bf16[128,1408]{1,0:T(8,128)(2,1)}, u32[]{:S(2)}, u32[]{:S(2)}) collective-permute-start(bf16[128,1408]{1,0:T(8,128)(2,1)S(1)} %get-tuple-element.322), channel_id=1, source_target_pairs={{0,3},{1,0},{2,1},{3,2},{4,7},{5,4},{6,5},{7,6},{8,11},{9,8},{10,9... | collective-permute-start | bytes 1081352 | tf_op jit(solution)/shard_map/ppermute | solution.py:501
  439.0 40.2 %collective-permute-start.65 = (bf16[4,256,384]{2,1,0:T(8,128)(2,1)}, bf16[4,256,384]{2,1,0:T(8,128)(2,1)}, u32[]{:S(2)}, u32[]{:S(2)}) collective-permute-start(bf16[4,256,384]{2,1,0:T(8,128)(2,1)} %constant_dynamic-slice_fusion.4), channel_id=1, source_target_pairs={{0,16},{4,12},{8,24},{12,4},{16,0},{20,28},{24,8},{28,20},{1,17},{... | collective-permute-start | bytes 2359304 | tf_op jit(solution)/shard_map/ppermute | solution.py:496
  471.4 38.9 %collective-permute-start.75 = (bf16[2,2624,128]{2,1,0:T(8,128)(2,1)}, bf16[2,2624,128]{2,1,0:T(8,128)(2,1)}, u32[]{:S(2)}, u32[]{:S(2)}) collective-permute-start(bf16[2,2624,128]{2,1,0:T(8,128)(2,1)} %pad_maximum_fusion.3), channel_id=1, source_target_pairs={{0,8},{4,20},{8,0},{12,28},{16,24},{20,4},{24,16},{28,12},{1,9},{5... | collective-permute-start | bytes 4030472 | tf_op jit(solution)/shard_map/ppermute | solution.py:496
  482.6 24.2 %collective-permute-start.66 = (bf16[256,384]{1,0:T(8,128)(2,1)}, bf16[256,384]{1,0:T(8,128)(2,1)}, u32[]{:S(2)}, u32[]{:S(2)}) collective-permute-start(bf16[256,384]{1,0:T(8,128)(2,1)} %get-tuple-element.331), channel_id=1, source_target_pairs={{0,1},{1,2},{2,3},{3,0},{4,5},{5,6},{6,7},{7,4},{8,9},{9,10},{10,1... | collective-permute-start | bytes 589832 | tf_op jit(solution)/shard_map/ppermute | solution.py:501
  513.6 25.6 %collective-permute-start.78 = (bf16[4,2624,128]{2,1,0:T(8,128)(2,1)}, bf16[4,2624,128]{2,1,0:T(8,128)(2,1)}, u32[]{:S(2)}, u32[]{:S(2)}) collective-permute-start(bf16[4,2624,128]{2,1,0:T(8,128)(2,1)} %pad_maximum_fusion), channel_id=1, source_target_pairs={{0,4},{4,0},{8,12},{12,8},{16,20},{20,16},{24,28},{28,24},{1,5},{5... | collective-permute-start | bytes 8060936 | tf_op jit(solution)/shard_map/ppermute | solution.py:496
  (187 other events, 1744.0 us)

commit v4 on v3

--- a/solution.py
+++ b/solution.py
@@ -836,7 +836,7 @@
 
     mix_in = [ga.full(), None]
     gb.first(mix_in[0])
-    projected = [dot_nn(normed_one, mix_in[0]), None]
+    projected = [dot_nn(normed_one, mix_in[0]).astype(BF), None]
     gb.second(projected[0])
     gu.deep(mix_in[0])
     kept = []
@@ -853,7 +853,7 @@
     done = mix(1, gu.raw[0])
     mix_in[1] = gb.full(done)
     go.first(done)
-    projected[1] = dot_nn(after(normed_one, done, gu.raw[1]), mix_in[1])
+    projected[1] = dot_nn(after(normed_one, done, gu.raw[1]), mix_in[1]).astype(BF)
     go.second(projected[1])
     gu.first(projected[1])
     gd.deep(projected[1], *gu.raw)
@@ -888,7 +888,7 @@
     branch_back = after(residual_back.astype(BF), t_gu.sent)
     t_out = Total(mixed_out, branch_back)
     t_out.core()
-    mixed_back = dot_nt(branch_back, mix_out)
+    mixed_back = dot_nt(branch_back, mix_out).astype(BF)
 
     backs = []
 

time: 569 us -> 567 us (level)
    unnamed x304 -> x272, local copies, waits for them, and re-layouts: 28.6 us -> 29.4 us
  transfers between devices with their start and end apart: 80 -> 80, of which waited for: 25 -> 28; matrix products, arithmetic and copies ran while one was open for 27% -> 26% of each run, Pallas kernels for 21% -> 21%
where the time goes in v4:
time: 567 us; the launch traced here: 560 us
  Pallas kernels  149 us (26%)
  starting transfers between devices  111 us (20%)
  waiting for transfers between devices  108 us (19%)
  matrix products  84.3 us (15%)
  local copies, waits for them, and re-layouts  60.2 us (11%)
  other arithmetic  43.9 us (8%)
    ppermute x36, starting transfers between devices, shift(): lax.ppermute(value, 'shard', [(i, (i + by) % count) for i in range(count)])  81 us
    ppermute x36, waiting for transfers between devices, shift(): lax.ppermute(value, 'shard', [(i, (i + by) % count) for i in range(count)])  54.1 us
    ppermute x44, waiting for transfers between devices, hop(): return lax.ppermute(value, 'rep', pairs)  53.7 us
    dot_general x15, matrix products, dot_tn(): lax.dot_general(a, b, (((0,), (0,)), ((), ())), preferred_element_type=F32)  48.2 us
    pallas_call x4, Pallas kernels, mixer_back(): pl.pallas_call(back_kernel, grid=(heads,), in_specs=[columns(rows, HEAD,...  45.6 us
    pallas_call x4, Pallas kernels, mixer(): pl.pallas_call(mix_kernel, grid=(heads,), in_specs=[columns(rows, HEAD, a...  37.7 us
    ppermute x44, starting transfers between devices, hop(): return lax.ppermute(value, 'rep', pairs)  29.9 us
    unnamed x272, local copies, waits for them, and re-layouts  29.4 us
  transfers between devices with their start and end apart: 80, of which 28 were waited for; matrix products, arithmetic and copies ran while one was open for 26% of the time, Pallas kernels for 21%

profile of v4, /device:TPU:0, one launch (start us, length us, event | category | flops | bytes accessed | tf_op | source)
XLA Modules:
  0.0 560.3 jit_solution(7278559789485807182)
XLA Ops:
  70.5 6.4 %convolution_convert_fusion.3.x_ref = bf16[512,3072]{1,0:T(8,128)(2,1)S(1)} fusion(bf16[512,1024]{1,0:T(8,128)(2,1)S(1)} %fusion.7, bf16[1024,3072]{1,0:T(8,128)(2,1)} %shard_map.203), kind=kOutput, calls=%fused_computation.5 | convolution fusion | flops 3222798336 | bytes 10485760 | tf_op jit(solution)/shard_map/dot_general | solution.py:26
  88.3 9.4 %shard_map.204 = (bf16[512,512]{1,0:T(8,128)(2,1)S(1)}, f32[512,512]{1,0:T(8,128)S(1)}, bf16[512,512]{1,0:T(8,128)(2,1)S(1)}, bf16[2,4,128,128]{3,2,1,0:T(8,128)(2,1)S(1)}, bf16[2,4,128,256]{3,2,1,0:T(8,128)(2,1)S(1)}) custom-call(bf16[512,3072]{1,0:T(8,128)(2,1)S(1)} %convolution_convert_fusion.3.x_ref, s32[512,128]{1,0:T(8,128)S(1)} %broadcast_in_dim.22.seg_ref, ...), custom_call_target="tpu_custom_call" | custom-call | flops 10000000000 | bytes 8000000 | tf_op jit(solution)/shard_map/pallas_call | solution.py:203
  101.7 9.4 %shard_map.205 = (bf16[512,512]{1,0:T(8,128)(2,1)S(1)}, f32[512,512]{1,0:T(8,128)S(1)}, bf16[512,512]{1,0:T(8,128)(2,1)S(1)}, bf16[2,4,128,128]{3,2,1,0:T(8,128)(2,1)S(1)}, bf16[2,4,128,256]{3,2,1,0:T(8,128)(2,1)S(1)}) custom-call(bf16[512,3072]{1,0:T(8,128)(2,1)S(1)} %convolution_convert_fusion.3.x_ref, s32[512,128]{1,0:T(8,128)S(1)} %broadcast_in_dim.22.seg_ref, ...), custom_call_target="tpu_custom_call" | custom-call | flops 10000000000 | bytes 8000000 | tf_op jit(solution)/shard_map/pallas_call | solution.py:203
  119.1 6.5 %convolution_convert_fusion.2.x_ref = bf16[512,3072]{1,0:T(8,128)(2,1)S(1)} fusion(bf16[512,1024]{1,0:T(8,128)(2,1)S(1)} %fusion.7, bf16[1024,3072]{1,0:T(8,128)(2,1)} %shard_map.206), kind=kOutput, calls=%fused_computation.4 | convolution fusion | flops 3222798336 | bytes 10485760 | tf_op jit(solution)/shard_map/dot_general | solution.py:26
  129.5 9.4 %collective-permute-start.25 = (bf16[704,128]{1,0:T(8,128)(2,1)S(1)}, bf16[704,128]{1,0:T(8,128)(2,1)S(1)}, u32[]{:S(2)}, u32[]{:S(2)}) collective-permute-start(bf16[704,128]{1,0:T(8,128)(2,1)S(1)} %copy-done.96), channel_id=1, source_target_pairs={{0,1},{1,2},{2,3},{3,0},{4,5},{5,6},{6,7},{7,4},{8,9},{9,10},{10,1... | collective-permute-start | bytes 540680 | tf_op jit(solution)/shard_map/ppermute | solution.py:501
  138.9 9.4 %shard_map.207 = (bf16[512,512]{1,0:T(8,128)(2,1)S(1)}, f32[512,512]{1,0:T(8,128)S(1)}, bf16[512,512]{1,0:T(8,128)(2,1)S(1)}, bf16[2,4,128,128]{3,2,1,0:T(8,128)(2,1)S(1)}, bf16[2,4,128,256]{3,2,1,0:T(8,128)(2,1)S(1)}) custom-call(bf16[512,3072]{1,0:T(8,128)(2,1)S(1)} %convolution_convert_fusion.2.x_ref, s32[512,128]{1,0:T(8,128)S(1)} %broadcast_in_dim.22.seg_ref, ...), custom_call_target="tpu_custom_call" | custom-call | flops 10000000000 | bytes 8000000 | tf_op jit(solution)/shard_map/pallas_call | solution.py:203
  153.1 9.4 %shard_map.208 = (bf16[512,512]{1,0:T(8,128)(2,1)S(1)}, f32[512,512]{1,0:T(8,128)S(1)}, bf16[512,512]{1,0:T(8,128)(2,1)S(1)}, bf16[2,4,128,128]{3,2,1,0:T(8,128)(2,1)S(1)}, bf16[2,4,128,256]{3,2,1,0:T(8,128)(2,1)S(1)}) custom-call(bf16[512,3072]{1,0:T(8,128)(2,1)S(1)} %convolution_convert_fusion.2.x_ref, s32[512,128]{1,0:T(8,128)S(1)} %broadcast_in_dim.22.seg_ref, ...), custom_call_target="tpu_custom_call" | custom-call | flops 10000000000 | bytes 8000000 | tf_op jit(solution)/shard_map/pallas_call | solution.py:203
  178.9 11.0 %collective-permute-start.29 = (bf16[704,128]{1,0:T(8,128)(2,1)S(1)}, bf16[704,128]{1,0:T(8,128)(2,1)S(1)}, u32[]{:S(2)}, u32[]{:S(2)}) collective-permute-start(bf16[704,128]{1,0:T(8,128)(2,1)S(1)} %copy-done.96), channel_id=1, source_target_pairs={{0,2},{1,3},{2,0},{3,1},{4,6},{5,7},{6,4},{7,5},{8,10},{9,11},{10,... | collective-permute-start | bytes 540680 | tf_op jit(solution)/shard_map/ppermute | solution.py:501
  190.7 8.5 %collective-permute-done.29 = bf16[704,128]{1,0:T(8,128)(2,1)S(1)} collective-permute-done((bf16[704,128]{1,0:T(8,128)(2,1)S(1)}, bf16[704,128]{1,0:T(8,128)(2,1)S(1)}, u32[]{:S(2)}, u32[]{:S(2)}) %collective-permute-start.29) | collective-permute-done | bytes 180256 | tf_op jit(solution)/shard_map/ppermute | solution.py:501
  203.2 8.1 %shard_map.210.gate_w_ref.up_w_ref = bf16[1024,5632]{1,0:T(8,128)(2,1)} custom-call(s32[49]{0:T(128)S(1)} %stack.394.at_ref, bf16[256,5632]{1,0:T(8,128)(2,1)} %own_ref.8, bf16[6,32,5632]{2,1,0:T(8,128)(2,1)S(1)} %pad_maximum_fusion.1.refs_0_, bf16[6,32,5632]{2,1,0:T(8,128)(2,1)S(1)} %collective-permute-done.32.refs_1_, ...), custom_call_target="tpu_custom_call" | custom-call | tf_op jit(solution)/shard_map/pallas_call | solution.py:571
  216.5 9.5 %shard_map.211 = (bf16[512,2816]{1,0:T(8,128)(2,1)S(1)}, bf16[512,2816]{1,0:T(8,128)(2,1)S(1)}, bf16[512,2816]{1,0:T(8,128)(2,1)S(1)}) custom-call(bf16[512,1024]{1,0:T(8,128)(2,1)S(1)} %multiply_convert_fusion.x_ref, bf16[1024,5632]{1,0:T(8,128)(2,1)S(1)} %copy-done, bf16[1024,5632]{1,0:T(8,128)(2,1)S(1)} %copy-done), custom_call_target="tpu_custom_call" | custom-call | flops 5905580032 | bytes 11534336 | tf_op jit(solution)/shard_map/pallas_call | solution.py:423
  246.1 18.2 %shard_map.213 = (bf16[2,512,2816]{2,1,0:T(8,128)(2,1)S(1)}, f32[512,1024]{1,0:T(8,128)S(1)}, f32[512,1024]{1,0:T(8,128)S(1)}) custom-call(bf16[512,1024]{1,0:T(8,128)(2,1)S(1)} %copy-done.1, bf16[512,2816]{1,0:T(8,128)(2,1)S(1)} %copy-done.16, bf16[512,2816]{1,0:T(8,128)(2,1)S(1)} %copy-done.18, bf16[512,2816]{1,0:T(8,128)(2,1)S(1)} %copy-done.13, ...), custom_call_target="tpu_custom_call" | custom-call | flops 11811160064 | bytes 17301504 | tf_op jit(solution)/shard_map/pallas_call | solution.py:455
  270.9 6.0 %fusion.15 = f32[1024,1408]{1,0:T(8,128)} fusion(bf16[512,1024]{1,0:T(8,128)(2,1)S(1)} %multiply_convert_fusion.x_ref, bf16[2,512,2816]{2,1,0:T(8,128)(2,1)} %copy-done.11, s32[]{:T(128)S(6)} %select_n.1482, s32[]{:T(128)S(6)} %select_n.1495), kind=kOutput, calls=%fused_computation.52 | convolution fusion | flops 1476395008 | bytes 8257544 | tf_op jit(solution)/shard_map/dot_general | solution.py:34
  276.9 6.7 %collective-permute-done.38 = bf16[2816,512]{1,0:T(8,128)(2,1)} collective-permute-done((bf16[2816,512]{1,0:T(8,128)(2,1)}, bf16[2816,512]{1,0:T(8,128)(2,1)}, u32[]{:S(2)}, u32[]{:S(2)}) %collective-permute-start.38) | collective-permute-done | bytes 2883616 | tf_op jit(solution)/shard_map/ppermute | solution.py:496
  300.3 11.3 %shard_map.214 = (bf16[512,3072]{1,0:T(8,128)(2,1)S(1)}, f32[4,1024]{1,0:T(4,128)S(1)}, f32[1,256]{1,0:T(1,128)S(1)}, f32[2,512]{1,0:T(2,128)S(1)}, f32[2,1,512]{2,1,0:T(1,128)S(1)}) custom-call(bf16[512,3072]{1,0:T(8,128)(2,1)S(1)} %copy-done.22, s32[512,128]{1,0:T(8,128)S(1)} %broadcast_in_dim.22.seg_ref, s32[8,512]{1,0:T(8,128)S(1)} %broadcast_in_dim.46.segrow_ref, ...), custom_call_target="tpu_custom_call" | custom-call | flops 12000000000 | bytes 10000000 | tf_op jit(solution)/shard_map/pallas_call | solution.py:375
  318.1 11.4 %shard_map.215 = (bf16[512,3072]{1,0:T(8,128)(2,1)S(1)}, f32[4,1024]{1,0:T(4,128)S(1)}, f32[1,256]{1,0:T(1,128)S(1)}, f32[2,512]{1,0:T(2,128)S(1)}, f32[2,1,512]{2,1,0:T(1,128)S(1)}) custom-call(bf16[512,3072]{1,0:T(8,128)(2,1)S(1)} %copy-done.22, s32[512,128]{1,0:T(8,128)S(1)} %broadcast_in_dim.22.seg_ref, ...), custom_call_target="tpu_custom_call", output_to_operand_aliasing={{0}: (12, {})} | custom-call | flops 12000000000 | bytes 10000000 | tf_op jit(solution)/shard_map/pallas_call | solution.py:375
  336.7 11.6 %shard_map.216 = (bf16[512,3072]{1,0:T(8,128)(2,1)S(1)}, f32[4,1024]{1,0:T(4,128)S(1)}, f32[1,256]{1,0:T(1,128)S(1)}, f32[2,512]{1,0:T(2,128)S(1)}, f32[2,1,512]{2,1,0:T(1,128)S(1)}) custom-call(bf16[512,3072]{1,0:T(8,128)(2,1)S(1)} %copy-done.20, s32[512,128]{1,0:T(8,128)S(1)} %broadcast_in_dim.22.seg_ref, s32[8,512]{1,0:T(8,128)S(1)} %broadcast_in_dim.46.segrow_ref, ...), custom_call_target="tpu_custom_call" | custom-call | flops 12000000000 | bytes 10000000 | tf_op jit(solution)/shard_map/pallas_call | solution.py:375
  356.3 7.0 %add_convert_fusion = bf16[1024,1408]{1,0:T(8,128)(2,1)} fusion(bf16[1024,1408]{1,0:T(8,128)(2,1)} %collective-permute-done.44, f32[1024,1408]{1,0:T(8,128)} %fusion.15, bf16[1024,2816]{1,0:T(8,128)(2,1)} %collective-permute-done.39, s32[]{:T(128)S(6)} %select_n.1494), kind=kLoop, calls=%fused_computation | loop fusion | flops 7208960 | bytes 14417924 | tf_op jit(solution)/shard_map/convert_element_type | solution.py:618
  371.0 11.3 %shard_map.217 = (bf16[512,3072]{1,0:T(8,128)(2,1)S(1)}, f32[4,1024]{1,0:T(4,128)S(1)}, f32[1,256]{1,0:T(1,128)S(1)}, f32[2,512]{1,0:T(2,128)S(1)}, f32[2,1,512]{2,1,0:T(1,128)S(1)}) custom-call(bf16[512,3072]{1,0:T(8,128)(2,1)S(1)} %copy-done.20, s32[512,128]{1,0:T(8,128)S(1)} %broadcast_in_dim.22.seg_ref, ...), custom_call_target="tpu_custom_call", output_to_operand_aliasing={{0}: (12, {})} | custom-call | flops 12000000000 | bytes 10000000 | tf_op jit(solution)/shard_map/pallas_call | solution.py:375
  410.9 8.1 %add_add_fusion.2 = f32[512,1024]{1,0:T(8,128)} fusion(f32[512,1024]{1,0:T(8,128)} %fusion.84, f32[512,1024]{1,0:T(8,128)} %fusion.101, bf16[512,3072]{1,0:T(8,128)(2,1)S(1)} %get-tuple-element.236, bf16[1024,3072]{1,0:T(8,128)(2,1)} %shard_map.206), kind=kOutput, calls=%fused_computation.39 | convolution fusion | flops 3222274048 | bytes 15728640 | tf_op jit(solution)/shard_map/dot_general | solution.py:30
  441.6 15.2 %collective-permute-done.52 = bf16[4,256,384]{2,1,0:T(8,128)(2,1)S(1)} collective-permute-done((bf16[4,256,384]{2,1,0:T(8,128)(2,1)S(1)}, bf16[4,256,384]{2,1,0:T(8,128)(2,1)S(1)}, u32[]{:S(2)}, u32[]{:S(2)}) %collective-permute-start.52) | collective-permute-done | bytes 786464 | tf_op jit(solution)/shard_map/ppermute | solution.py:496
  485.8 9.7 %collective-permute-done.71 = bf16[256,384]{1,0:T(8,128)(2,1)} collective-permute-done((bf16[256,384]{1,0:T(8,128)(2,1)}, bf16[256,384]{1,0:T(8,128)(2,1)}, u32[]{:S(2)}, u32[]{:S(2)}) %collective-permute-start.71) | collective-permute-done | bytes 196640 | tf_op jit(solution)/shard_map/ppermute | solution.py:501
  495.8 8.0 %collective-permute-done.72 = bf16[256,384]{1,0:T(8,128)(2,1)} collective-permute-done((bf16[256,384]{1,0:T(8,128)(2,1)}, bf16[256,384]{1,0:T(8,128)(2,1)}, u32[]{:S(2)}, u32[]{:S(2)}) %collective-permute-start.72) | collective-permute-done | bytes 196640 | tf_op jit(solution)/shard_map/ppermute | solution.py:501
  538.7 6.0 %shard_map.218 = (f32[704,1024]{1,0:T(8,128)}, f32[512,1024]{1,0:T(8,128)}, f32[256,5632]{1,0:T(8,128)}) custom-call(s32[192]{0:T(256)S(1)} %stack.523.at_ref, bf16[2624,128]{1,0:T(8,128)(2,1)S(1)} %constant_dynamic-update-slice_fusion.18.refs_0_, bf16[2624,128]{1,0:T(8,128)(2,1)S(1)} %collective-permute-done.69.refs_1_, ...), custom_call_target="tpu_custom_call" | custom-call | tf_op jit(solution)/shard_map/pallas_call | solution.py:682
  (591 shorter events, 328.8 us)
Async XLA Ops:
  85.6 26.4 %collective-permute-start.17 = (bf16[32,5632]{1,0:T(8,128)(2,1)}, bf16[32,5632]{1,0:T(8,128)(2,1)S(1)}, u32[]{:S(2)}, u32[]{:S(2)}) collective-permute-start(bf16[32,5632]{1,0:T(8,128)(2,1)} %constant_dynamic-slice_fusion.9), channel_id=1, source_target_pairs={{0,2},{1,3},{2,0},{3,1},{4,6},{5,7},{6,4},{7,5},{8,10},{9,11},{10,... | collective-permute-start | bytes 1081352 | tf_op jit(solution)/shard_map/ppermute | solution.py:501
  87.5 38.1 %collective-permute-start.22 = (bf16[32,5632]{1,0:T(8,128)(2,1)}, bf16[32,5632]{1,0:T(8,128)(2,1)}, u32[]{:S(2)}, u32[]{:S(2)}) collective-permute-start(bf16[32,5632]{1,0:T(8,128)(2,1)} %constant_dynamic-slice_fusion.9), channel_id=1, source_target_pairs={{0,3},{1,0},{2,1},{3,2},{4,7},{5,4},{6,5},{7,6},{8,11},{9,8},{10,9... | collective-permute-start | bytes 1081352 | tf_op jit(solution)/shard_map/ppermute | solution.py:501
  127.6 23.3 %collective-permute-start.24 = (bf16[3,32,5632]{2,1,0:T(8,128)(2,1)S(1)}, bf16[3,32,5632]{2,1,0:T(8,128)(2,1)S(1)}, u32[]{:S(2)}, u32[]{:S(2)}) collective-permute-start(bf16[3,32,5632]{2,1,0:T(8,128)(2,1)S(1)} %pad_maximum_fusion.6), channel_id=1, source_target_pairs={{0,8},{4,20},{8,0},{12,28},{16,24},{20,4},{24,16},{28,12},{1,9},{5... | collective-permute-start | bytes 3244040 | tf_op jit(solution)/shard_map/ppermute | solution.py:496
  129.2 35.0 %collective-permute-start.27 = (bf16[6,512,128]{2,1,0:T(8,128)(2,1)S(1)}, bf16[6,512,128]{2,1,0:T(8,128)(2,1)S(1)}, u32[]{:S(2)}, u32[]{:S(2)}) collective-permute-start(bf16[6,512,128]{2,1,0:T(8,128)(2,1)S(1)} %pad_maximum_fusion.8.refs_0_), channel_id=1, source_target_pairs={{0,4},{4,0},{8,12},{12,8},{16,20},{20,16},{24,28},{28,24},{1,5},{5... | collective-permute-start | bytes 2359304 | tf_op jit(solution)/shard_map/ppermute | solution.py:496
  129.5 23.6 %collective-permute-start.25 = (bf16[704,128]{1,0:T(8,128)(2,1)S(1)}, bf16[704,128]{1,0:T(8,128)(2,1)S(1)}, u32[]{:S(2)}, u32[]{:S(2)}) collective-permute-start(bf16[704,128]{1,0:T(8,128)(2,1)S(1)} %copy-done.96), channel_id=1, source_target_pairs={{0,1},{1,2},{2,3},{3,0},{4,5},{5,6},{6,7},{7,4},{8,9},{9,10},{10,1... | collective-permute-start | bytes 540680 | tf_op jit(solution)/shard_map/ppermute | solution.py:501
  152.1 26.8 %collective-permute-start.32 = (bf16[6,32,5632]{2,1,0:T(8,128)(2,1)S(1)}, bf16[6,32,5632]{2,1,0:T(8,128)(2,1)S(1)}, u32[]{:S(2)}, u32[]{:S(2)}) collective-permute-start(bf16[6,32,5632]{2,1,0:T(8,128)(2,1)S(1)} %pad_maximum_fusion.1.refs_0_), channel_id=1, source_target_pairs={{0,16},{4,12},{8,24},{12,4},{16,0},{20,28},{24,8},{28,20},{1,17},{... | collective-permute-start | bytes 6488072 | tf_op jit(solution)/shard_map/ppermute | solution.py:496
  153.0 48.8 %collective-permute-start.33 = (bf16[6,32,5632]{2,1,0:T(8,128)(2,1)S(1)}, bf16[6,32,5632]{2,1,0:T(8,128)(2,1)}, u32[]{:S(2)}, u32[]{:S(2)}) collective-permute-start(bf16[6,32,5632]{2,1,0:T(8,128)(2,1)S(1)} %pad_maximum_fusion.1.refs_0_), channel_id=1, source_target_pairs={{0,4},{4,0},{8,12},{12,8},{16,20},{20,16},{24,28},{28,24},{1,5},{5... | collective-permute-start | bytes 6488072 | tf_op jit(solution)/shard_map/ppermute | solution.py:496
  212.2 24.3 %collective-permute-start.36 = (bf16[6,704,128]{2,1,0:T(8,128)(2,1)S(1)}, bf16[6,704,128]{2,1,0:T(8,128)(2,1)}, u32[]{:S(2)}, u32[]{:S(2)}) collective-permute-start(bf16[6,704,128]{2,1,0:T(8,128)(2,1)S(1)} %pad_maximum_fusion.7.refs_0_), channel_id=1, source_target_pairs={{0,4},{4,0},{8,12},{12,8},{16,20},{20,16},{24,28},{28,24},{1,5},{5... | collective-permute-start | bytes 3244040 | tf_op jit(solution)/shard_map/ppermute | solution.py:496
  287.1 24.5 %collective-permute-start.41 = (bf16[2816,256]{1,0:T(8,128)(2,1)}, bf16[2816,256]{1,0:T(8,128)(2,1)}, u32[]{:S(2)}, u32[]{:S(2)}) collective-permute-start(bf16[2816,256]{1,0:T(8,128)(2,1)} %fusion.2), channel_id=1, source_target_pairs={{0,8},{4,20},{8,0},{12,28},{16,24},{20,4},{24,16},{28,12},{1,9},{5... | collective-permute-start | bytes 4325384 | tf_op jit(solution)/shard_map/ppermute | solution.py:496
  296.9 57.4 %collective-permute-start.44 = (bf16[1024,1408]{1,0:T(8,128)(2,1)}, bf16[1024,1408]{1,0:T(8,128)(2,1)}, u32[]{:S(2)}, u32[]{:S(2)}) collective-permute-start(bf16[1024,1408]{1,0:T(8,128)(2,1)} %add_convert_fusion.1), channel_id=1, source_target_pairs={{0,8},{4,20},{8,0},{12,28},{16,24},{20,4},{24,16},{28,12},{1,9},{5... | collective-permute-start | bytes 8650760 | tf_op jit(solution)/shard_map/ppermute | solution.py:496
  333.0 31.7 %collective-permute-start.43 = (bf16[1024,1536]{1,0:T(8,128)(2,1)}, bf16[1024,1536]{1,0:T(8,128)(2,1)}, u32[]{:S(2)}, u32[]{:S(2)}) collective-permute-start(bf16[1024,1536]{1,0:T(8,128)(2,1)} %convolution_convert_fusion.5), channel_id=1, source_target_pairs={{0,4},{4,0},{8,12},{12,8},{16,20},{20,16},{24,28},{28,24},{1,5},{5... | collective-permute-start | bytes 9437192 | tf_op jit(solution)/shard_map/ppermute | solution.py:496
  335.2 34.2 %collective-permute-start.45 = (bf16[2048,256]{1,0:T(8,128)(2,1)}, bf16[2048,256]{1,0:T(8,128)(2,1)S(1)}, u32[]{:S(2)}, u32[]{:S(2)}) collective-permute-start(bf16[2048,256]{1,0:T(8,128)(2,1)} %add_convert_fusion.8), channel_id=1, source_target_pairs={{0,8},{4,20},{8,0},{12,28},{16,24},{20,4},{24,16},{28,12},{1,9},{5... | collective-permute-start | bytes 3145736 | tf_op jit(solution)/shard_map/ppermute | solution.py:496
  349.7 34.7 %collective-permute-start.53 = (bf16[704,128]{1,0:T(8,128)(2,1)}, bf16[704,128]{1,0:T(8,128)(2,1)}, u32[]{:S(2)}, u32[]{:S(2)}) collective-permute-start(bf16[704,128]{1,0:T(8,128)(2,1)} %get-tuple-element.337), channel_id=1, source_target_pairs={{0,1},{1,2},{2,3},{3,0},{4,5},{5,6},{6,7},{7,4},{8,9},{9,10},{10,1... | collective-permute-start | bytes 540680 | tf_op jit(solution)/shard_map/ppermute | solution.py:501
  352.7 32.9 %collective-permute-start.54 = (bf16[704,128]{1,0:T(8,128)(2,1)}, bf16[704,128]{1,0:T(8,128)(2,1)}, u32[]{:S(2)}, u32[]{:S(2)}) collective-permute-start(bf16[704,128]{1,0:T(8,128)(2,1)} %get-tuple-element.336), channel_id=1, source_target_pairs={{0,2},{1,3},{2,0},{3,1},{4,6},{5,7},{6,4},{7,5},{8,10},{9,11},{10,... | collective-permute-start | bytes 540680 | tf_op jit(solution)/shard_map/ppermute | solution.py:501
  354.3 32.2 %collective-permute-start.55 = (bf16[704,128]{1,0:T(8,128)(2,1)}, bf16[704,128]{1,0:T(8,128)(2,1)}, u32[]{:S(2)}, u32[]{:S(2)}) collective-permute-start(bf16[704,128]{1,0:T(8,128)(2,1)} %get-tuple-element.335), channel_id=1, source_target_pairs={{0,3},{1,0},{2,1},{3,2},{4,7},{5,4},{6,5},{7,6},{8,11},{9,8},{10,9... | collective-permute-start | bytes 540680 | tf_op jit(solution)/shard_map/ppermute | solution.py:501
  384.4 34.6 %collective-permute-start.47 = (bf16[1024,768]{1,0:T(8,128)(2,1)}, bf16[1024,768]{1,0:T(8,128)(2,1)}, u32[]{:S(2)}, u32[]{:S(2)}) collective-permute-start(bf16[1024,768]{1,0:T(8,128)(2,1)} %add_convert_fusion.5), channel_id=1, source_target_pairs={{0,8},{4,20},{8,0},{12,28},{16,24},{20,4},{24,16},{28,12},{1,9},{5... | collective-permute-start | bytes 4718600 | tf_op jit(solution)/shard_map/ppermute | solution.py:496
  387.1 52.1 %collective-permute-start.61 = (bf16[128,1408]{1,0:T(8,128)(2,1)S(1)}, bf16[128,1408]{1,0:T(8,128)(2,1)}, u32[]{:S(2)}, u32[]{:S(2)}) collective-permute-start(bf16[128,1408]{1,0:T(8,128)(2,1)S(1)} %get-tuple-element.324), channel_id=1, source_target_pairs={{0,1},{1,2},{2,3},{3,0},{4,5},{5,6},{6,7},{7,4},{8,9},{9,10},{10,1... | collective-permute-start | bytes 1081352 | tf_op jit(solution)/shard_map/ppermute | solution.py:501
  387.3 51.9 %collective-permute-start.62 = (bf16[128,1408]{1,0:T(8,128)(2,1)S(1)}, bf16[128,1408]{1,0:T(8,128)(2,1)}, u32[]{:S(2)}, u32[]{:S(2)}) collective-permute-start(bf16[128,1408]{1,0:T(8,128)(2,1)S(1)} %get-tuple-element.323), channel_id=1, source_target_pairs={{0,2},{1,3},{2,0},{3,1},{4,6},{5,7},{6,4},{7,5},{8,10},{9,11},{10,... | collective-permute-start | bytes 1081352 | tf_op jit(solution)/shard_map/ppermute | solution.py:501
  400.5 38.7 %collective-permute-start.63 = (bf16[128,1408]{1,0:T(8,128)(2,1)S(1)}, bf16[128,1408]{1,0:T(8,128)(2,1)S(1)}, u32[]{:S(2)}, u32[]{:S(2)}) collective-permute-start(bf16[128,1408]{1,0:T(8,128)(2,1)S(1)} %get-tuple-element.322), channel_id=1, source_target_pairs={{0,3},{1,0},{2,1},{3,2},{4,7},{5,4},{6,5},{7,6},{8,11},{9,8},{10,9... | collective-permute-start | bytes 1081352 | tf_op jit(solution)/shard_map/ppermute | solution.py:501
  436.2 40.5 %collective-permute-start.65 = (bf16[4,256,384]{2,1,0:T(8,128)(2,1)}, bf16[4,256,384]{2,1,0:T(8,128)(2,1)}, u32[]{:S(2)}, u32[]{:S(2)}) collective-permute-start(bf16[4,256,384]{2,1,0:T(8,128)(2,1)} %constant_dynamic-slice_fusion.4), channel_id=1, source_target_pairs={{0,16},{4,12},{8,24},{12,4},{16,0},{20,28},{24,8},{28,20},{1,17},{... | collective-permute-start | bytes 2359304 | tf_op jit(solution)/shard_map/ppermute | solution.py:496
  440.7 23.2 %collective-permute-start.69 = (bf16[2624,128]{1,0:T(8,128)(2,1)S(1)}, bf16[2624,128]{1,0:T(8,128)(2,1)S(1)}, u32[]{:S(2)}, u32[]{:S(2)}) collective-permute-start(bf16[2624,128]{1,0:T(8,128)(2,1)S(1)} %constant_dynamic-update-slice_fusion.18.refs_0_), channel_id=1, source_target_pairs={{0,16},{4,12},{8,24},{12,4},{16,0},{20,28},{24,8},{28,20},{1,17},{... | collective-permute-start | bytes 2015240 | tf_op jit(solution)/shard_map/ppermute | solution.py:496
  468.6 38.9 %collective-permute-start.75 = (bf16[2,2624,128]{2,1,0:T(8,128)(2,1)}, bf16[2,2624,128]{2,1,0:T(8,128)(2,1)}, u32[]{:S(2)}, u32[]{:S(2)}) collective-permute-start(bf16[2,2624,128]{2,1,0:T(8,128)(2,1)} %pad_maximum_fusion.3), channel_id=1, source_target_pairs={{0,8},{4,20},{8,0},{12,28},{16,24},{20,4},{24,16},{28,12},{1,9},{5... | collective-permute-start | bytes 4030472 | tf_op jit(solution)/shard_map/ppermute | solution.py:496
  480.0 23.9 %collective-permute-start.66 = (bf16[256,384]{1,0:T(8,128)(2,1)}, bf16[256,384]{1,0:T(8,128)(2,1)}, u32[]{:S(2)}, u32[]{:S(2)}) collective-permute-start(bf16[256,384]{1,0:T(8,128)(2,1)} %get-tuple-element.331), channel_id=1, source_target_pairs={{0,1},{1,2},{2,3},{3,0},{4,5},{5,6},{6,7},{7,4},{8,9},{9,10},{10,1... | collective-permute-start | bytes 589832 | tf_op jit(solution)/shard_map/ppermute | solution.py:501
  510.7 26.0 %collective-permute-start.78 = (bf16[4,2624,128]{2,1,0:T(8,128)(2,1)}, bf16[4,2624,128]{2,1,0:T(8,128)(2,1)}, u32[]{:S(2)}, u32[]{:S(2)}) collective-permute-start(bf16[4,2624,128]{2,1,0:T(8,128)(2,1)} %pad_maximum_fusion), channel_id=1, source_target_pairs={{0,4},{4,0},{8,12},{12,8},{16,20},{20,16},{24,28},{28,24},{1,5},{5... | collective-permute-start | bytes 8060936 | tf_op jit(solution)/shard_map/ppermute | solution.py:496
  (171 other events, 1559.3 us)
